TPU v7x, 256 devices: a whole 4x4x8 slice. The times are simulated.
256 devices in a mesh: slot: 32 (over z, x_hi, core), limb: 4 (over y), ct: 2 (over x_lo).
Axes of the slice: x: 4 (x_hi: 2, x_lo: 2; x = x_hi * 2 + x_lo), y: 4, z: 8, core: 2. Of those that a mesh axis runs over, the one named last changes fastest.
Arguments:
- ciphertexts: float32 [2, 2, 24, 65536], P('ct', None, 'limb', 'slot'), parts along dimension 0, may hold values from -6 to 6
- diagonals: bfloat16 [8, 8, 24, 65536], P(None, None, 'limb', 'slot'), may hold values from -0.75 to 0.75
- baby_keys: bfloat16 [7, 3, 2, 32, 65536], P(None, None, None, 'limb', 'slot'), may hold values from -3.5 to 3.5
- giant_keys: bfloat16 [7, 3, 2, 32, 65536], P(None, None, None, 'limb', 'slot'), may hold values from -3.5 to 3.5
- up_factors: float32 [32, 24], P('limb'), may hold values from -2 to 2
- down_factors: float32 [24, 8], P('limb'), may hold values from -2 to 2
Outputs:
- coefficients: float32 [2, 2, 24, 65536], P('ct', None, 'limb', 'slot'), parts along dimension 0
There are 2 independent parts, one for each index of `ct`. A program takes and returns all parts, laid end to end along the dimension named above; an argument that names none is the same for every part. Nothing has to cross between parts.
All inputs are finite; a program needn't handle non-finite values.
Results may differ from a plain program's by a relative error of at most 0.0003.
Values sent between devices are 32-bit elements; how exact they have to be, the bound alone decides.
No kernel may reach another device: no remote copies, remote signals or barrier semaphores. Data moves between devices by JAX's collectives and lax.ppermute only.
A program may use at most 64 MiB of HBM per device.

v0:
```python
import jax
import jax.numpy as jnp
from jax import lax
from jax.sharding import PartitionSpec as P

SIDE = 256
DNUM = 3
ALPHA = 8
BABY = 8
GIANT = 8


TOPMOST_LEVEL = lax.Precision.HIGHEST


def shifted(block, axis, distance):
    devices = range(lax.axis_size(axis))
    route = [((i - distance) % len(devices), i) for i in devices]
    return lax.ppermute(block, axis, route)


def cosine_matrix_entries(side_count):
    freqs = jnp.arange(side_count, dtype=jnp.float32)[:, None]
    slot_positions = jnp.arange(side_count, dtype=jnp.float32)[None, :]
    scaling = jnp.where(freqs == 0, jnp.sqrt(1.0 / side_count), jnp.sqrt(2.0 / side_count))
    return scaling * jnp.cos(jnp.pi * (slot_positions + 0.5) * freqs / side_count)


def transform_local(values, matrix):
    dims_in = values.shape
    row_count = dims_in[3] // SIDE
    squared = values.reshape(dims_in[:3] + (row_count, SIDE))
    across = jnp.einsum("...rb,kb->...rk", squared, matrix, precision=TOPMOST_LEVEL)
    mixed = jnp.einsum(
        "ka,...ac->...kc",
        matrix,
        lax.all_to_all(across, "slot", split_axis=4, concat_axis=3, tiled=True),
        precision=TOPMOST_LEVEL,
    )
    result = lax.all_to_all(mixed, "slot", split_axis=3, concat_axis=4, tiled=True)
    return result.reshape(dims_in)


def neighbour(first_part, second_part):
    return shifted((first_part, second_part), "slot", 1)


def baby_views(own_values, prior_values, stride_length):
    sample_count = own_values.shape[-1]
    views = []
    for baby_step in range(1, BABY):
        cut_at = sample_count - baby_step * stride_length
        views.append(
            jnp.concatenate((prior_values[..., cut_at:], own_values[..., :cut_at]), axis=-1)
        )
    return jnp.stack(views, axis=0)


def decomposed_weight_factors(factor_cols):
    row_count = factor_cols.shape[1]
    digit_of = jnp.arange(row_count, dtype=jnp.int32) // ALPHA
    digit_mask = (digit_of[None, :] == jnp.arange(DNUM, dtype=jnp.int32)[:, None]).astype(
        jnp.float32
    )
    return factor_cols[None, :, :] * digit_mask[:, None, :]


def raise_basis(limb_rows, up_factors):
    weight_factors = decomposed_weight_factors(up_factors)
    return jnp.einsum(
        "var,gwri->gwvai",
        weight_factors,
        lax.all_gather(limb_rows, "limb", axis=2, tiled=True),
        precision=TOPMOST_LEVEL,
    )


def multiply_keys(raised, keys):
    products = raised[:, :, 0][:, :, None] * keys[:, 0].astype(jnp.float32)[:, None]
    for digit in range(1, DNUM):
        products = (
            products + raised[:, :, digit][:, :, None] * keys[:, digit].astype(jnp.float32)[:, None]
        )
    return products


def lower_basis(product, down_factors):
    q_rows = down_factors.shape[0]
    kept = product[:, :, :, :q_rows, :]
    spare = product[:, :, :, q_rows:, :]
    spare_all = lax.all_gather(spare, "limb", axis=3, tiled=True)
    return kept - jnp.einsum("ls,kcusp->kculp", down_factors, spare_all, precision=TOPMOST_LEVEL)


def weigh_diagonals(diagonals, stacked):
    inners = diagonals[:, 0].astype(jnp.float32)[:, None, None] * stacked[0][None]
    for baby_step in range(1, BABY):
        inners = (
            inners
            + diagonals[:, baby_step].astype(jnp.float32)[:, None, None] * stacked[baby_step][None]
        )
    return inners


def per_device(ciphertexts, diagonals, baby_keys, giant_keys, up_factors, down_factors):
    table = cosine_matrix_entries(SIDE)
    evals = transform_local(ciphertexts, table)
    stride_length = evals.shape[3] // BABY
    first_poly = evals[:, 0]
    second_component = evals[:, 1]
    prior_first, prior_second = neighbour(first_poly, second_component)
    rolled_first = baby_views(first_poly, prior_first, stride_length)
    raised_views = raise_basis(
        baby_views(second_component, prior_second, stride_length), up_factors
    )
    switched = lower_basis(multiply_keys(raised_views, baby_keys), down_factors)
    babies = jnp.stack((rolled_first + switched[:, :, 0], switched[:, :, 1]), axis=2)
    stacked = jnp.concatenate((evals[None], babies), axis=0)
    inners = weigh_diagonals(diagonals, stacked)
    moved = jnp.stack(
        [shifted(inners[giant_step], "slot", giant_step) for giant_step in range(1, GIANT)]
    )
    giant_products = multiply_keys(raise_basis(moved[:, :, 1], up_factors), giant_keys)
    giant_switched = lower_basis(giant_products, down_factors)
    rotated = jnp.stack((moved[:, :, 0] + giant_switched[:, :, 0], giant_switched[:, :, 1]), axis=2)
    total = inners[0] + jnp.sum(rotated, axis=0)
    return transform_local(total, table.T)


def solution(mesh):
    placed = (
        P("ct", None, "limb", "slot"),
        P(None, None, "limb", "slot"),
        P(None, None, None, "limb", "slot"),
        P(None, None, None, "limb", "slot"),
        P("limb", None),
        P("limb", None),
    )
    return jax.shard_map(
        per_device,
        mesh=mesh,
        in_specs=placed,
        out_specs=P("ct", None, "limb", "slot"),
        check_vma=False,
    )
```

profile of v0, /device:TPU:1, one launch (start us, length us, event | category | flops | bytes accessed | tf_op | source)
XLA Modules:
  0.0 277.9 jit_solution(7766913154574435565)
XLA Ops:
  7.5 1.3 convolution_bitcast_fusion.7
  9.9 3.1 %reshape.348 = f32[32,1,768]{2,1,0:T(1,128)} reshape(f32[256,1,6,2,8]{4,3,2,1,0:T(2,128)S(1)} %bitcast.303) | data formatting | bytes 196608
  13.0 13.2 %all-to-all-start = ((f32[32,1,768]{2,1,0:T(1,128)}), f32[32,1,768]{2,1,0:T(1,128)S(1)}, u32[]{:S(2)}, u32[]{:S(2)}) async-start(f32[32,1,768]{2,1,0:T(1,128)} %reshape.348), calls=%async_computation | async-start | bytes 196608 | tf_op jit(solution)/shard_map/all_to_all | solution.py:37
  26.2 4.1 %fusion.71 = (bf16[8,1,6,2048]{3,1,2,0:T(2,128)(2,1)S(1)}, bf16[8,1,6,2048]{3,1,2,0:T(2,128)(2,1)}, bf16[8,1,6,2048]{3,1,2,0:T(2,128)(2,1)}, bf16[8,1,6,2048]{3,...) fusion(bf16[8,8,6,2048]{3,1,2,0:T(8,128)(2,1)S(1)} %copy-done.1), kind=kLoop, calls=%fused_computation.154 | loop fusion | bytes 3145728 | tf_op jit(solution)/shard_map/slice | solution.py:96
  30.3 1.2 fusion.20
  31.5 4.8 %all-to-all-done = f32[32,1,768]{2,1,0:T(1,128)S(1)} async-done(((f32[32,1,768]{2,1,0:T(1,128)}), f32[32,1,768]{2,1,0:T(1,128)S(1)}, u32[]{:S(2)}, u32[]{:S(2)}) %all-to-all-start) | async-done | bytes 98336 | tf_op jit(solution)/shard_map/all_to_all | solution.py:37
  37.6 2.4 reshape.349
  41.8 1.3 convolution_bitcast_fusion.6
  44.1 3.1 %reshape.350 = f32[32,1,768]{2,1,0:T(1,128)} reshape(f32[256,1,6,2,8]{4,3,2,1,0:T(2,128)S(1)} %bitcast.306) | data formatting | bytes 196608
  47.2 4.9 %all-to-all-start.1 = ((f32[32,1,768]{2,1,0:T(1,128)}), f32[32,1,768]{2,1,0:T(1,128)S(1)}, u32[]{:S(2)}, u32[]{:S(2)}) async-start(f32[32,1,768]{2,1,0:T(1,128)} %reshape.350), calls=%async_computation.1 | async-start | bytes 196608 | tf_op jit(solution)/shard_map/all_to_all | solution.py:40
  52.4 1.3 fusion.14
  53.7 8.7 %all-to-all-done.1 = f32[32,1,768]{2,1,0:T(1,128)S(1)} async-done(((f32[32,1,768]{2,1,0:T(1,128)}), f32[32,1,768]{2,1,0:T(1,128)S(1)}, u32[]{:S(2)}, u32[]{:S(2)}) %all-to-all-start.1) | async-done | bytes 98336 | tf_op jit(solution)/shard_map/all_to_all | solution.py:40
  63.2 2.4 reshape.351
  65.6 2.5 copy.212
  68.1 2.8 %copy.152 = f32[1,2,6,8,32,8]{5,4,3,1,2,0:T(8,128)S(1)} copy(f32[1,2,6,8,32,8]{3,4,5,2,1,0:T(8,128)} %bitcast.313) | data formatting | bytes 196608 | tf_op jit(solution)/shard_map/all_to_all | solution.py:40
  70.8 1.4 reshape.323
  72.3 1.7 fusion.73
  74.0 1.4 collective-permute-start.1
  75.4 2.5 fusion.16
  81.6 2.6 collective-permute-start
  105.2 3.0 %convolution_bitcast_fusion.1 = f32[7,1,3,8,2048]{4,3,2,0,1:T(8,128)S(1)} fusion(f32[7,1,24,2048]{3,1,0,2:T(1,128)} %all-gather.4.cloned.1.call-done, f32[3,24]{1,0:T(4,128)S(1)} %fusion.66, f32[8,24]{1,0:T(8,128)S(1)} %copy-done.22), kind=kOutput, calls=%fused_computation.1 | convolution fusion | flops 99091008 | bytes 2753568 | tf_op jit(solution)/shard_map/var,gwri->gwvai/dot_general | solution.py:70
  108.3 1.2 copy-done.19
  110.1 13.2 %all_gather.13 = f32[7,1,2,8,2048]{4,2,1,0,3:T(2,128)S(1)} all-gather(f32[7,1,2,2,2048]{4,2,1,0,3:T(2,128)S(1)} %copy.169), channel_id=1, replica_groups=mesh['slot'=32,'limb'=4,'ct'=2] {'limb'}, dimensions={3}, use_global_device_ids=true | all-gather | bytes 1146880 | tf_op jit(solution)/shard_map/all_gather | solution.py:91
  123.4 1.4 fusion
  127.8 5.0 %collective-permute-start.2 = (f32[1,2,6,2048]{3,2,1,0:T(8,128)S(1)}, f32[1,2,6,2048]{3,2,1,0:T(8,128)S(1)}, u32[]{:S(2)}, u32[]{:S(2)}) collective-permute-start(f32[1,2,6,2048]{3,2,1,0:T(8,128)S(1)} %get-tuple-element.26), channel_id=1, source_target_pairs={{248,0},{0,8},{8,16},{16,24},{24,32},{32,40},{40,48},{48,56},{56,6... | collective-permute-start | bytes 294920 | tf_op jit(solution)/shard_map/ppermute | solution.py:19
  132.7 3.1 %collective-permute-start.7 = (f32[1,2,6,2048]{3,2,1,0:T(8,128)S(1)}, f32[1,2,6,2048]{3,2,1,0:T(8,128)S(1)}, u32[]{:S(2)}, u32[]{:S(2)}) collective-permute-start(f32[1,2,6,2048]{3,2,1,0:T(8,128)S(1)} %get-tuple-element.21), channel_id=1, source_target_pairs={{208,0},{216,8},{224,16},{232,24},{240,32},{248,40},{0,48},{8,56},... | collective-permute-start | bytes 294920 | tf_op jit(solution)/shard_map/ppermute | solution.py:19
  135.8 6.2 %collective-permute-start.6 = (f32[1,2,6,2048]{3,2,1,0:T(8,128)S(1)}, f32[1,2,6,2048]{3,2,1,0:T(8,128)S(1)}, u32[]{:S(2)}, u32[]{:S(2)}) collective-permute-start(f32[1,2,6,2048]{3,2,1,0:T(8,128)S(1)} %get-tuple-element.22), channel_id=1, source_target_pairs={{216,0},{224,8},{232,16},{240,24},{248,32},{0,40},{8,48},{16,56},{... | collective-permute-start | bytes 294920 | tf_op jit(solution)/shard_map/ppermute | solution.py:19
  142.4 2.7 collective-permute-start.3
  145.1 12.4 %collective-permute-done.3 = f32[1,2,6,2048]{3,2,1,0:T(8,128)S(1)} collective-permute-done((f32[1,2,6,2048]{3,2,1,0:T(8,128)S(1)}, f32[1,2,6,2048]{3,2,1,0:T(8,128)S(1)}, u32[]{:S(2)}, u32[]{:S(2)}) %collective-permute-start.3) | collective-permute-done | bytes 98336 | tf_op jit(solution)/shard_map/ppermute | solution.py:19
  157.5 1.6 collective-permute-start.4
  159.1 6.4 %collective-permute-done.4 = f32[1,2,6,2048]{3,2,1,0:T(8,128)S(1)} collective-permute-done((f32[1,2,6,2048]{3,2,1,0:T(8,128)S(1)}, f32[1,2,6,2048]{3,2,1,0:T(8,128)S(1)}, u32[]{:S(2)}, u32[]{:S(2)}) %collective-permute-start.4) | collective-permute-done | bytes 98336 | tf_op jit(solution)/shard_map/ppermute | solution.py:19
  165.7 1.1 copy.190
  166.8 26.5 %all-gather.6.cloned.1.call-done = f32[7,1,1,24,2048]{4,2,1,0,3:T(1,128)} async-done(((f32[7,1,1,6,2048]{4,2,1,0,3:T(1,128)}), f32[7,1,1,24,2048]{4,2,1,0,3:T(1,128)}) %all-gather.6.cloned.1.call-update) | async-done | bytes 1376272 | tf_op jit(solution)/shard_map/all_gather | solution.py:73
  193.3 3.0 %convolution_bitcast_fusion = f32[7,1,3,8,2048]{4,3,2,0,1:T(8,128)S(1)} fusion(f32[7,1,1,24,2048]{4,2,1,0,3:T(1,128)} %all-gather.6.cloned.1.call-done, f32[3,24]{1,0:T(4,128)S(1)} %fusion.66, f32[8,24]{1,0:T(8,128)S(1)} %copy-done.22), kind=kOutput, calls=%fused_computation | convolution fusion | flops 99091008 | bytes 2753568 | tf_op jit(solution)/shard_map/var,gwri->gwvai/dot_general | solution.py:70
  196.5 1.2 copy-done.20
  198.3 12.4 %all_gather.15 = f32[7,1,2,8,2048]{4,2,1,0,3:T(2,128)S(1)} all-gather(f32[7,1,2,2,2048]{4,2,1,0,3:T(2,128)S(1)} %copy.195), channel_id=1, replica_groups=mesh['slot'=32,'limb'=4,'ct'=2] {'limb'}, dimensions={3}, use_global_device_ids=true | all-gather | bytes 1146880 | tf_op jit(solution)/shard_map/all_gather | solution.py:91
  210.7 1.4 fusion.1
  212.4 1.2 convolution_bitcast_fusion.5
  214.7 2.4 reshape.352
  217.1 23.1 %all_to_all.60 = f32[32,1,768]{2,1,0:T(1,128)S(1)} all-to-all(f32[32,1,768]{2,1,0:T(1,128)S(1)} %reshape.352), channel_id=1, replica_groups=mesh['slot'=32,'limb'=4,'ct'=2] {'slot'}, dimensions={0} | all-to-all | bytes 196608 | tf_op jit(solution)/shard_map/all_to_all | solution.py:37
  241.0 2.4 reshape.353
  245.1 1.2 convolution_bitcast_fusion.4
  247.3 2.4 reshape.354
  249.8 13.4 %all_to_all.61 = f32[32,1,768]{2,1,0:T(1,128)S(1)} all-to-all(f32[32,1,768]{2,1,0:T(1,128)S(1)} %reshape.354), channel_id=1, replica_groups=mesh['slot'=32,'limb'=4,'ct'=2] {'slot'}, dimensions={0} | all-to-all | bytes 196608 | tf_op jit(solution)/shard_map/all_to_all | solution.py:40
  264.0 2.4 reshape.355
  266.3 1.5 copy.218
  267.9 1.6 copy.205
  269.4 1.4 reshape.329
  (155 shorter events, 41.7 us)
Async XLA Ops:
  6.5 116.8 %copy-start = (f32[6,8]{1,0:T(8,128)S(1)}, f32[6,8]{1,0:T(8,128)}, u32[]{:S(2)}) copy-start(f32[6,8]{1,0:T(8,128)} %param.11) | copy-start | bytes 580
  8.8 17.4 %copy-start.1 = (bf16[8,8,6,2048]{3,1,2,0:T(8,128)(2,1)S(1)}, bf16[8,8,6,2048]{3,1,2,0:T(8,128)(2,1)}, u32[]{:S(2)}) copy-start(bf16[8,8,6,2048]{3,1,2,0:T(8,128)(2,1)} %param.7) | copy-start | bytes 4718596
  13.0 23.4 %all-to-all-start = ((f32[32,1,768]{2,1,0:T(1,128)}), f32[32,1,768]{2,1,0:T(1,128)S(1)}, u32[]{:S(2)}, u32[]{:S(2)}) async-start(f32[32,1,768]{2,1,0:T(1,128)} %reshape.348), calls=%async_computation | async-start | bytes 196608 | tf_op jit(solution)/shard_map/all_to_all | solution.py:37
  43.0 9.3 %copy-start.17 = (bf16[8,1,6,2048]{3,1,2,0:T(2,128)(2,1)S(1)}, bf16[8,1,6,2048]{3,1,2,0:T(2,128)(2,1)}, u32[]{:S(2)}) copy-start(bf16[8,1,6,2048]{3,1,2,0:T(2,128)(2,1)} %get-tuple-element.6) | copy-start | bytes 589828
  43.0 9.3 %copy-start.18 = (bf16[8,1,6,2048]{3,1,2,0:T(2,128)(2,1)S(1)}, bf16[8,1,6,2048]{3,1,2,0:T(2,128)(2,1)}, u32[]{:S(2)}) copy-start(bf16[8,1,6,2048]{3,1,2,0:T(2,128)(2,1)} %get-tuple-element.12) | copy-start | bytes 589828
  47.2 15.2 %all-to-all-start.1 = ((f32[32,1,768]{2,1,0:T(1,128)}), f32[32,1,768]{2,1,0:T(1,128)S(1)}, u32[]{:S(2)}, u32[]{:S(2)}) async-start(f32[32,1,768]{2,1,0:T(1,128)} %reshape.350), calls=%async_computation.1 | async-start | bytes 196608 | tf_op jit(solution)/shard_map/all_to_all | solution.py:40
  52.1 53.1 %all-gather.4.cloned.1.call-start = ((), (), s32[]{:S(2)}) async-start(), calls=%async_computation.4 | async-start | bytes 1720320 | tf_op jit(solution)/shard_map/all_gather | solution.py:73
  74.0 4.0 %collective-permute-start.1 = (f32[1,6,2048]{2,0,1:T(1,128)S(1)}, f32[1,6,2048]{2,0,1:T(1,128)S(1)}, u32[]{:S(2)}, u32[]{:S(2)}) collective-permute-start(f32[1,6,2048]{2,0,1:T(1,128)S(1)} %get-tuple-element.39), channel_id=1, source_target_pairs={{248,0},{0,8},{8,16},{16,24},{24,32},{32,40},{40,48},{48,56},{56,6... | collective-permute-start | bytes 147464 | tf_op jit(solution)/shard_map/ppermute | solution.py:19
  78.0 2.2 copy-start.11
  78.0 2.2 copy-start.12
  79.0 5.2 %copy-start.10 = (f32[8,6,2048]{2,0,1:T(8,128)S(1)}, f32[8,6,2048]{2,0,1:T(8,128)}, u32[]{:S(2)}) copy-start(f32[8,6,2048]{2,0,1:T(8,128)} %get-tuple-element.48) | copy-start | bytes 1179652
  80.1 0.8 copy-start.21
  80.2 113.2 %all-gather.6.cloned.1.call-start = ((), (), s32[]{:S(2)}) async-start(), calls=%async_computation.5 | async-start | bytes 1720320 | tf_op jit(solution)/shard_map/all_gather | solution.py:73
  80.2 6.1 %copy-start.14 = (f32[8,6,2048]{2,0,1:T(8,128)S(1)}, f32[8,6,2048]{2,0,1:T(8,128)}, u32[]{:S(2)}) copy-start(f32[8,6,2048]{2,0,1:T(8,128)} %get-tuple-element.42) | copy-start | bytes 1179652
  81.6 18.1 %collective-permute-start = (f32[1,6,2048]{2,1,0:T(8,128)}, f32[1,6,2048]{2,1,0:T(8,128)}, u32[]{:S(2)}, u32[]{:S(2)}) collective-permute-start(f32[1,6,2048]{2,1,0:T(8,128)} %bitcast.299), channel_id=1, source_target_pairs={{248,0},{0,8},{8,16},{16,24},{24,32},{32,40},{40,48},{48,56},{56,6... | collective-permute-start | bytes 147464 | tf_op jit(solution)/shard_map/ppermute | solution.py:19
  84.2 3.1 %copy-start.13 = (f32[8,6,2048]{2,0,1:T(8,128)S(1)}, f32[8,6,2048]{2,0,1:T(8,128)}, u32[]{:S(2)}) copy-start(f32[8,6,2048]{2,0,1:T(8,128)} %get-tuple-element.43) | copy-start | bytes 1179652
  85.3 3.2 %copy-start.16 = (f32[8,6,2048]{2,0,1:T(8,128)S(1)}, f32[8,6,2048]{2,0,1:T(8,128)}, u32[]{:S(2)}) copy-start(f32[8,6,2048]{2,0,1:T(8,128)} %get-tuple-element.44) | copy-start | bytes 1179652
  86.3 3.1 %copy-start.15 = (f32[8,6,2048]{2,0,1:T(8,128)S(1)}, f32[8,6,2048]{2,0,1:T(8,128)}, u32[]{:S(2)}) copy-start(f32[8,6,2048]{2,0,1:T(8,128)} %get-tuple-element.45) | copy-start | bytes 1179652
  98.8 6.3 %copy-start.22 = (f32[8,24]{1,0:T(8,128)S(1)}, f32[8,24]{1,0:T(8,128)}, u32[]{:S(2)}) copy-start(f32[8,24]{1,0:T(8,128)} %param.10) | copy-start | bytes 2308
  108.2 1.3 copy-start.19
  123.4 1.7 copy-start.9
  124.8 1.0 copy-start.5
  124.8 1.2 copy-start.6
  124.8 1.3 copy-start.7
  124.8 1.5 copy-start.8
  124.9 1.6 copy-start.2
  124.9 1.7 copy-start.3
  125.0 1.9 copy-start.4
  127.8 14.6 %collective-permute-start.2 = (f32[1,2,6,2048]{3,2,1,0:T(8,128)S(1)}, f32[1,2,6,2048]{3,2,1,0:T(8,128)S(1)}, u32[]{:S(2)}, u32[]{:S(2)}) collective-permute-start(f32[1,2,6,2048]{3,2,1,0:T(8,128)S(1)} %get-tuple-element.26), channel_id=1, source_target_pairs={{248,0},{0,8},{8,16},{16,24},{24,32},{32,40},{40,48},{48,56},{56,6... | collective-permute-start | bytes 294920 | tf_op jit(solution)/shard_map/ppermute | solution.py:19
  132.7 32.9 %collective-permute-start.8 = (f32[1,2,6,2048]{3,2,1,0:T(8,128)S(1)}, f32[1,2,6,2048]{3,2,1,0:T(8,128)S(1)}, u32[]{:S(2)}, u32[]{:S(2)}) collective-permute-start(f32[1,2,6,2048]{3,2,1,0:T(8,128)S(1)} %get-tuple-element.20), channel_id=1, source_target_pairs={{200,0},{208,8},{216,16},{224,24},{232,32},{240,40},{248,48},{0,56... | collective-permute-start | bytes 294920 | tf_op jit(solution)/shard_map/ppermute | solution.py:19
  132.7 32.8 %collective-permute-start.7 = (f32[1,2,6,2048]{3,2,1,0:T(8,128)S(1)}, f32[1,2,6,2048]{3,2,1,0:T(8,128)S(1)}, u32[]{:S(2)}, u32[]{:S(2)}) collective-permute-start(f32[1,2,6,2048]{3,2,1,0:T(8,128)S(1)} %get-tuple-element.21), channel_id=1, source_target_pairs={{208,0},{216,8},{224,16},{232,24},{240,32},{248,40},{0,48},{8,56},... | collective-permute-start | bytes 294920 | tf_op jit(solution)/shard_map/ppermute | solution.py:19
  135.8 29.7 %collective-permute-start.6 = (f32[1,2,6,2048]{3,2,1,0:T(8,128)S(1)}, f32[1,2,6,2048]{3,2,1,0:T(8,128)S(1)}, u32[]{:S(2)}, u32[]{:S(2)}) collective-permute-start(f32[1,2,6,2048]{3,2,1,0:T(8,128)S(1)} %get-tuple-element.22), channel_id=1, source_target_pairs={{216,0},{224,8},{232,16},{240,24},{248,32},{0,40},{8,48},{16,56},{... | collective-permute-start | bytes 294920 | tf_op jit(solution)/shard_map/ppermute | solution.py:19
  142.0 23.5 %collective-permute-start.5 = (f32[1,2,6,2048]{3,2,1,0:T(8,128)S(1)}, f32[1,2,6,2048]{3,2,1,0:T(8,128)S(1)}, u32[]{:S(2)}, u32[]{:S(2)}) collective-permute-start(f32[1,2,6,2048]{3,2,1,0:T(8,128)S(1)} %get-tuple-element.23), channel_id=1, source_target_pairs={{224,0},{232,8},{240,16},{248,24},{0,32},{8,40},{16,48},{24,56},{3... | collective-permute-start | bytes 294920 | tf_op jit(solution)/shard_map/ppermute | solution.py:19
  142.4 15.1 %collective-permute-start.3 = (f32[1,2,6,2048]{3,2,1,0:T(8,128)S(1)}, f32[1,2,6,2048]{3,2,1,0:T(8,128)S(1)}, u32[]{:S(2)}, u32[]{:S(2)}) collective-permute-start(f32[1,2,6,2048]{3,2,1,0:T(8,128)S(1)} %get-tuple-element.25), channel_id=1, source_target_pairs={{240,0},{248,8},{0,16},{8,24},{16,32},{24,40},{32,48},{40,56},{48,... | collective-permute-start | bytes 294920 | tf_op jit(solution)/shard_map/ppermute | solution.py:19
  157.5 8.0 %collective-permute-start.4 = (f32[1,2,6,2048]{3,2,1,0:T(8,128)S(1)}, f32[1,2,6,2048]{3,2,1,0:T(8,128)S(1)}, u32[]{:S(2)}, u32[]{:S(2)}) collective-permute-start(f32[1,2,6,2048]{3,2,1,0:T(8,128)S(1)} %get-tuple-element.24), channel_id=1, source_target_pairs={{232,0},{240,8},{248,16},{0,24},{8,32},{16,40},{24,48},{32,56},{40... | collective-permute-start | bytes 294920 | tf_op jit(solution)/shard_map/ppermute | solution.py:19
  196.4 1.3 copy-start.20
Sparse Core Ops, SparseCore 0:
  80.3 24.4 all-gather.3
  166.9 26.3 all-gather.5
where the time goes:
time: 283 us; the launch traced here: 278 us
  local copies, waits for them, and re-layouts  76.4 us (27%)
  blocking collectives  62.1 us (22%)
  waiting for transfers between devices  58.9 us (21%)
  starting transfers between devices  41.4 us (15%)
  between operations  14.5 us (5%)
  matrix products  13.9 us (5%)
  other arithmetic  10.8 us (4%)
    all_gather x2, waiting for transfers between devices, raise_basis(): lax.all_gather(limb_rows, 'limb', axis=2, tiled=True)  26.5 us
    unnamed x61, local copies, waits for them, and re-layouts  25.7 us
    all_gather x2, blocking collectives, lower_basis(): spare_all = lax.all_gather(spare, 'limb', axis=3, tiled=True)  25.7 us
    all_to_all x1, blocking collectives, transform_local(): lax.all_to_all(across, 'slot', split_axis=4, concat_axis=3, tiled=True)  23.1 us
    ppermute x9, starting transfers between devices, shifted(): return lax.ppermute(block, axis, route)  23 us
    ppermute x9, waiting for transfers between devices, shifted(): return lax.ppermute(block, axis, route)  18.8 us
    all_to_all x1, blocking collectives, transform_local(): lax.all_to_all(mixed, 'slot', split_axis=3, concat_axis=4, tiled=True)  13.4 us
    all_to_all x1, starting transfers between devices, transform_local(): lax.all_to_all(across, 'slot', split_axis=4, concat_axis=3, tiled=True)  13.2 us
  transfers between devices with their start and end apart: 13, of which 5 were waited for; matrix products, arithmetic and copies ran while one was open for 11% of the time, Pallas kernels for 0%

commit v1 on v0

v1 whole, which is shorter than its diff:
```python
import numpy as np
import jax
import jax.numpy as jnp
import ml_dtypes
from jax import lax
from jax.experimental import pallas as pl
from jax.experimental.pallas import tpu as pltpu
from jax.sharding import PartitionSpec as P

SIDE = 256
DNUM = 3
BABY = 8
GIANT = 8
Q_DEV = 6
LANES = 128
POINTS_DEV = 2048
HALO = 2 * POINTS_DEV
SLOTS = 32
GROUPS = 4
CHUNK = 512
VMEM_BYTES = 48 * 1024 * 1024
F32 = jnp.float32
BF16 = jnp.bfloat16


def split_constant(values):
    high = values.astype(ml_dtypes.bfloat16)
    low = (values - high.astype(np.float64)).astype(ml_dtypes.bfloat16)
    return np.stack([high, low])


def cosine_matrix():
    k = np.arange(SIDE, dtype=np.float64)[:, None]
    n = np.arange(SIDE, dtype=np.float64)[None, :]
    scale = np.where(k == 0, np.sqrt(1.0 / SIDE), np.sqrt(2.0 / SIDE))
    return scale * np.cos(np.pi * (n + 0.5) * k / SIDE)


def lane_orders():
    lane = np.arange(SIDE)
    half, low = lane // LANES, lane % LANES
    block, rest = low // 64, low % 64
    rows = half * 128 + block * 64 + (rest % 8) * 8 + rest // 8
    cols_fwd = half * 128 + (low % 16) * 8 + low // 16
    c = (low // 64) * 8 + low % 8
    k = (low // 8) % 8
    cols_inv = half * 128 + c * 8 + k
    return rows, cols_fwd, cols_inv


def dct_constants():
    c = cosine_matrix()
    rows, cols_fwd, cols_inv = lane_orders()
    return (
        split_constant(c.T[rows]),
        split_constant(c.T[cols_fwd]),
        split_constant(c[rows]),
        split_constant(c[cols_inv]),
    )


def baby_selectors():
    limb_of = np.array([6 * (q // 8) + q % 8 if q % 8 < 6 else -1 for q in range(32)])
    pick = np.zeros((24, 32), np.float32)
    for q in range(32):
        if limb_of[q] >= 0:
            pick[limb_of[q], q] = 1.0
    rows = np.zeros((120, 16), np.float32)
    mask = np.zeros((120, 32), np.float32)
    for d in range(DNUM):
        for e in range(8):
            rows[d * 8 + e, e] = 1.0
            mask[d * 8 + e] = (limb_of >= 0) & (limb_of // 8 == d)
        for g in range(GROUPS):
            for t in range(8):
                row = 24 + (g * 3 + d) * 8 + t
                rows[row, 8 + 2 * g + t % 2] = 1.0
                mask[row] = (limb_of >= 0) & (limb_of // 8 == d)
    return rows, pick, mask


def giant_selectors():
    rows = np.zeros((96, 8), np.float32)
    pick = np.zeros((24, 96), np.float32)
    mask = np.zeros((96, 96), np.float32)
    for j in range(4):
        for d in range(DNUM):
            for e in range(8):
                rows[(j * 3 + d) * 8 + e, e] = 1.0
    for g in range(GROUPS):
        for j in range(4):
            for i in range(Q_DEV):
                limb = 6 * g + i
                pick[limb, g * 24 + j * 6 + i] = 1.0
                d = limb // 8
                mask[(j * 3 + d) * 8 : (j * 3 + d) * 8 + 8, g * 24 + j * 6 + i] = 1.0
    return rows, pick, mask


def exchange(values, lane_bits):
    values = list(values)
    lane = lax.broadcasted_iota(jnp.int32, values[0].shape, values[0].ndim - 1)
    for place, bit in enumerate(reversed(lane_bits)):
        step, span = 1 << place, 1 << bit
        keep = (lane & span) == 0
        for i in range(len(values)):
            if i & step:
                continue
            a, b = values[i], values[i + step]
            values[i] = jnp.where(keep, a, pltpu.roll(b, span, a.ndim - 1))
            values[i + step] = jnp.where(keep, pltpu.roll(a, LANES - span, a.ndim - 1), b)
    return values


def halves(values):
    high = values.astype(BF16)
    return high, (values - high.astype(F32)).astype(BF16)


def matmul(a, b):
    return lax.dot_general(a, b, (((1,), (0,)), ((), ())), preferred_element_type=F32)


def exact_matmul(a, b):
    return lax.dot_general(
        a,
        b,
        (((1,), (0,)), ((), ())),
        precision=lax.Precision.HIGHEST,
        preferred_element_type=F32,
    )


def transform(values, table):
    high, low = halves(values)
    return matmul(high, table[0]) + matmul(low, table[0]) + matmul(high, table[1])


def call(kernel, out_shapes, *args, scratch=(), flops=1000000):
    shapes = [jax.ShapeDtypeStruct(s, F32) for s in out_shapes]
    return pl.pallas_call(
        kernel,
        out_shape=shapes if len(shapes) > 1 else shapes[0],
        scratch_shapes=list(scratch),
        compiler_params=pltpu.CompilerParams(vmem_limit_bytes=VMEM_BYTES),
        cost_estimate=pl.CostEstimate(flops=flops, bytes_accessed=400000, transcendentals=0),
    )(*args)


def special_kernel(keys_ref, up_ref, out_ref):
    out_ref[...] = jnp.zeros_like(out_ref)
    for k in range(BABY - 1):
        for d in range(DNUM):
            for s in range(2):
                rows = keys_ref[k, d, s].astype(F32)[Q_DEV:]
                at = d * 32 + k * 4 + s * 2
                out_ref[at : at + 2, :] = rows
    out_ref[28:30, 0:24] = up_ref[Q_DEV:, :]


def spread_rows(piece, out_ref):
    for h in range(2):
        parts = [piece(p, r * SIDE + h * LANES) for p in range(2) for r in range(8)]
        for c, part in enumerate(exchange(parts, (6, 5, 4, 3))):
            out_ref[h * 16 + c] = part


def rows_kernel(x_ref, out_ref):
    spread_rows(lambda p, at: x_ref[0, p, :, at : at + LANES], out_ref)


def column_transform(in_ref, table_ref, hold_ref):
    hold_ref[...] = jnp.zeros_like(hold_ref)
    for h in range(2):
        parts = exchange([in_ref[h * 16 + s] for s in range(16)], (6, 2, 1, 0))
        for i, part in enumerate(parts):
            hold_ref[i, 0:Q_DEV, h * LANES : (h + 1) * LANES] = part
    result = transform(hold_ref[...].reshape(128, SIDE), table_ref)
    return result.reshape(16, 8, SIDE)


def columns_kernel(in_ref, table_ref, out_ref, hold_ref):
    result = column_transform(in_ref, table_ref, hold_ref)
    lane = lax.broadcasted_iota(jnp.int32, (8, LANES), 1)
    first = (lane & 8) == 0
    for p in range(2):
        pairs = []
        for h in range(2):
            parts = [result[p * 8 + k][:, h * LANES : (h + 1) * LANES] for k in range(8)]
            pairs += exchange(parts, (6, 5, 4))
        for i in range(16):
            out_ref[2 * i + 1, p] = pairs[i][:Q_DEV]
            both = jnp.where(
                first, pltpu.roll(pairs[i - 1], LANES - 8, 1), pltpu.roll(pairs[i], 8, 1)
            )
            out_ref[2 * i, p] = both[:Q_DEV]


def evals_kernel(in_ref, table_ref, e0_ref, e1_ref, e1x_ref, hold_ref):
    hold_ref[...] = jnp.zeros_like(hold_ref)
    for p in range(2):
        for h in range(2):
            parts = exchange([in_ref[h * 16 + c, p] for c in range(16)], (3, 2, 1, 0))
            for row, part in enumerate(parts):
                hold_ref[p * 16 + row, 0:Q_DEV, h * LANES : (h + 1) * LANES] = part
    result = transform(hold_ref[...].reshape(256, SIDE), table_ref).reshape(32, 8, SIDE)
    for row in range(16):
        at = slice(row * SIDE, (row + 1) * SIDE)
        e0_ref[:, at] = result[row][:Q_DEV]
        second = result[16 + row][:Q_DEV]
        e1_ref[:, at] = second
        for g in range(GROUPS):
            e1x_ref[g, :, at] = second


def babies_kernel(
    e1g_ref, e0_ref, e1_ref, up_ref, rows_ref, pick_ref, mask_ref, down_ref, head_ref,
    keys_ref, special_ref, diag_ref,
    send1_ref, send2_ref, send3_ref, four_ref, zero_ref,
    raised_ref, stage_ref, upx_ref,
):
    step = pl.program_id(0)

    @pl.when(step == 0)
    def _():
        upx_ref[0:8, :] = up_ref[...]
        for g in range(GROUPS):
            upx_ref[8 + 2 * g : 10 + 2 * g, :] = head_ref[g, 4:6, 0:24]
        spread = exact_matmul(upx_ref[...], pick_ref[...])
        factors = exact_matmul(rows_ref[...], spread) * mask_ref[...]
        fh, fl = halves(factors)
        lhs = jnp.concatenate([fh, fh, fl], axis=1)
        stage_ref[...] = jnp.zeros_like(stage_ref)
        for g in range(GROUPS):
            stage_ref[8 * g : 8 * g + Q_DEV, :] = e1g_ref[g]
        for part in range(8):
            at = slice(part * 512, (part + 1) * 512)
            eh, el = halves(stage_ref[:, at])
            raised_ref[:, at] = matmul(lhs, jnp.concatenate([eh, el, eh], axis=0))

    upper = lax.broadcasted_iota(jnp.int32, (8, LANES), 0) < 4
    down = down_ref[...]
    columns = [jnp.broadcast_to(down[:, i : i + 1], (Q_DEV, LANES)) for i in range(8)]

    def body(t, carry):
        lane = pl.multiple_of(t * LANES, LANES)
        base = pl.multiple_of(step * CHUNK + t * LANES, LANES)
        here = pl.ds(lane, LANES)

        def view(ref, first, count, k):
            return ref[first : first + count, pl.ds(base + (8 - k) * SIDE, LANES)]

        babies = [(view(e0_ref, 0, Q_DEV, 0), view(e1_ref, 0, Q_DEV, 0))]
        for pair in range(4):
            spare = []
            for g in range(GROUPS):
                total = None
                for d in range(DNUM):
                    at = 24 + (g * 3 + d) * 8
                    k = 2 * pair + 1
                    both = jnp.where(
                        upper, view(raised_ref, at, 8, k), view(raised_ref, at, 8, k + 1)
                    )
                    row = d * 32 + pair * 8
                    term = both * special_ref[g, row : row + 8, here]
                    total = term if total is None else total + term
                spare.append(total)
            for k in (2 * pair + 1, 2 * pair + 2):
                if k == BABY:
                    continue
                views = [view(raised_ref, d * 8, 8, k) for d in range(DNUM)]
                polys = []
                for s in range(2):
                    total = None
                    for d in range(DNUM):
                        term = views[d] * keys_ref[k - 1, d, s, :, here].astype(F32)
                        total = term if total is None else total + term
                    total = total[:Q_DEV]
                    for g in range(GROUPS):
                        for i in range(2):
                            row = ((k - 1) % 2) * 4 + s * 2 + i
                            total = total - columns[2 * g + i] * spare[g][row : row + 1]
                    polys.append(total)
                polys[0] = polys[0] + view(e0_ref, 0, Q_DEV, k)
                babies.append(tuple(polys))
        sends = (None, send1_ref, send2_ref, send3_ref)
        for j in range(GIANT):
            inner = [None, None]
            for k in range(BABY):
                factor = diag_ref[j, k, :, here].astype(F32)
                for s in range(2):
                    term = factor * babies[k][s]
                    inner[s] = term if inner[s] is None else inner[s] + term
            if j % 4 == 0:
                target = zero_ref if j == 0 else four_ref
                target[0, :, here] = inner[0]
                target[1, :, here] = inner[1]
            else:
                at = 6 * (j // 4)
                sends[j % 4][at : at + 6, here] = inner[1]
                sends[j % 4][12 + at : 18 + at, here] = inner[0]
        return carry

    lax.fori_loop(0, CHUNK // LANES, body, 0)


def babies_call(e1g, e0, e1, up, down, keys, special, diagonals):
    rows, pick, mask = baby_selectors()
    head = special[:, 24:32, 0:LANES]
    whole = lambda a: pl.BlockSpec(a.shape, lambda i, n=a.ndim: (0,) * n)
    lanes = lambda *lead: pl.BlockSpec(lead + (CHUNK,), lambda i, n=len(lead): (0,) * n + (i,))
    consts = (e1g, e0, e1, up, rows, pick, mask, down, head)
    outs = [(24, POINTS_DEV)] * 3 + [(2, Q_DEV, POINTS_DEV)] * 2
    return pl.pallas_call(
        babies_kernel,
        grid=(POINTS_DEV // CHUNK,),
        in_specs=[whole(a) for a in consts]
        + [lanes(7, 3, 2, 8), lanes(4, 96), lanes(8, 8, Q_DEV)],
        out_specs=[lanes(24)] * 3 + [lanes(2, Q_DEV)] * 2,
        out_shape=[jax.ShapeDtypeStruct(s, F32) for s in outs],
        scratch_shapes=[
            pltpu.VMEM((120, HALO), F32),
            pltpu.VMEM((32, HALO), F32),
            pltpu.VMEM((16, 24), F32),
        ],
        compiler_params=pltpu.CompilerParams(vmem_limit_bytes=VMEM_BYTES),
        cost_estimate=pl.CostEstimate(flops=40000000, bytes_accessed=6000000, transcendentals=0),
    )(*consts, keys, special, diagonals)


def sort_kernel(got1_ref, got2_ref, got3_ref, four_ref, near_ref, far_ref):
    gots = (got1_ref, got2_ref, got3_ref)
    far_ref[0:6, :] = four_ref[1]
    rest = four_ref[0]
    for r, got in enumerate(gots):
        far_ref[6 + 6 * r : 12 + 6 * r, :] = got[6:12, :]
        rest = rest + got[18:24, :]
        for g in range(GROUPS):
            near_ref[g, 6 * r : 6 * r + 6, :] = got[0:6, :]
    for g in range(GROUPS):
        near_ref[g, 18:24, :] = jnp.zeros((6, POINTS_DEV), F32)
    far_ref[24:30, :] = rest
    far_ref[30:32, :] = jnp.zeros((2, POINTS_DEV), F32)


def giants_kernel(
    near_ref, far_ref, up_ref, rows_ref, pick_ref, mask_ref,
    keys_ref, zero_ref, got1_ref, got2_ref, got3_ref, moved_ref,
    total_ref, spare_ref,
    raised_ref, factor_ref,
):
    step = pl.program_id(0)

    @pl.when(step == 0)
    def _():
        spread = exact_matmul(up_ref[...], pick_ref[...])
        factors = exact_matmul(rows_ref[...], spread) * mask_ref[...]
        fh, fl = halves(factors)
        factor_ref[0] = fh
        factor_ref[1] = fl

    for part, ref in enumerate((near_ref, far_ref)):
        eh, el = halves(ref[...].reshape(96, CHUNK))
        raised_ref[part] = (
            matmul(factor_ref[0], eh) + matmul(factor_ref[0], el) + matmul(factor_ref[1], eh)
        )

    def body(t, carry):
        here = pl.ds(pl.multiple_of(t * LANES, LANES), LANES)
        sums = [None, None]
        for j in range(1, GIANT):
            part, place = (0, j - 1) if j < 4 else (1, j - 4)
            for d in range(DNUM):
                at = (place * 3 + d) * 8
                value = raised_ref[part, at : at + 8, here]
                for s in range(2):
                    term = value * keys_ref[j - 1, d, s, :, here].astype(F32)
                    sums[s] = term if sums[s] is None else sums[s] + term
        first = zero_ref[0, :, here] + moved_ref[24:30, here]
        for got in (got1_ref, got2_ref, got3_ref):
            first = first + got[12:18, here]
        total_ref[0, :, here] = first + sums[0][:Q_DEV]
        total_ref[1, :, here] = zero_ref[1, :, here] + sums[1][:Q_DEV]
        for g in range(GROUPS):
            spare_ref[g, 0:2, here] = sums[0][Q_DEV:]
            spare_ref[g, 2:4, here] = sums[1][Q_DEV:]
        return carry

    lax.fori_loop(0, CHUNK // LANES, body, 0)


def giants_call(near, far, up, keys, zero, gots, moved):
    rows, pick, mask = giant_selectors()
    whole = lambda a: pl.BlockSpec(a.shape, lambda i, n=a.ndim: (0,) * n)
    lanes = lambda *lead: pl.BlockSpec(lead + (CHUNK,), lambda i, n=len(lead): (0,) * n + (i,))
    consts = (up, rows, pick, mask)
    return pl.pallas_call(
        giants_kernel,
        grid=(POINTS_DEV // CHUNK,),
        in_specs=[lanes(4, 24)] * 2
        + [whole(a) for a in consts]
        + [lanes(7, 3, 2, 8), lanes(2, Q_DEV)]
        + [lanes(24)] * 3
        + [lanes(32)],
        out_specs=[lanes(2, Q_DEV), lanes(4, 4)],
        out_shape=[
            jax.ShapeDtypeStruct((2, Q_DEV, POINTS_DEV), F32),
            jax.ShapeDtypeStruct((4, 4, POINTS_DEV), F32),
        ],
        scratch_shapes=[pltpu.VMEM((2, 96, CHUNK), F32), pltpu.VMEM((2, 96, 96), BF16)],
        compiler_params=pltpu.CompilerParams(vmem_limit_bytes=VMEM_BYTES),
        cost_estimate=pl.CostEstimate(flops=40000000, bytes_accessed=4000000, transcendentals=0),
    )(near, far, *consts, keys, zero, *gots, moved)


def lower_kernel(total_ref, spare_ref, down_ref, out_ref):
    down = down_ref[...]
    columns = [jnp.broadcast_to(down[:, i : i + 1], (Q_DEV, LANES)) for i in range(8)]

    def piece(p, at):
        value = total_ref[p, :, at : at + LANES]
        for g in range(GROUPS):
            rows = spare_ref[g, :, at : at + LANES]
            for i in range(2):
                value = value - columns[2 * g + i] * rows[2 * p + i : 2 * p + i + 1]
        return value

    spread_rows(piece, out_ref)


def inverse_columns_kernel(in_ref, table_ref, out_ref, hold_ref):
    result = column_transform(in_ref, table_ref, hold_ref)
    for h in range(2):
        parts = [result[i][:, h * LANES : (h + 1) * LANES] for i in range(16)]
        for g, part in enumerate(exchange(parts, (6, 5, 4, 3))):
            out_ref[h * 16 + g] = part[:Q_DEV]


def inverse_rows_kernel(in_ref, table_ref, out_ref, hold_ref):
    hold_ref[...] = jnp.zeros_like(hold_ref)
    for h in range(2):
        parts = exchange([in_ref[h * 16 + c] for c in range(16)], (6, 2, 1, 0))
        for i, part in enumerate(parts):
            hold_ref[i, 0:Q_DEV, h * LANES : (h + 1) * LANES] = part
    result = transform(hold_ref[...].reshape(128, SIDE), table_ref).reshape(16, 8, SIDE)
    for p in range(2):
        for r in range(8):
            out_ref[0, p, :, r * SIDE : (r + 1) * SIDE] = result[p * 8 + r][:Q_DEV]


def swap(values, axis):
    return lax.all_to_all(values, axis, split_axis=0, concat_axis=0, tiled=True)


def shifted(block, distance):
    route = [(i, (i + distance) % SLOTS) for i in range(SLOTS)]
    return lax.ppermute(block, "slot", route)


def forward(ciphertexts):
    col_fwd, row_fwd, _, _ = dct_constants()
    hold = [pltpu.VMEM((16, 8, SIDE), F32)]
    sent = call(rows_kernel, [(SLOTS, Q_DEV, LANES)], ciphertexts)
    held = swap(sent, "slot")
    sent = call(
        columns_kernel, [(SLOTS, 2, Q_DEV, LANES)], held, col_fwd, scratch=hold, flops=50000000
    )
    held = swap(sent, "slot")
    return call(
        evals_kernel,
        [(Q_DEV, HALO), (Q_DEV, HALO), (GROUPS, Q_DEV, HALO)],
        held,
        row_fwd,
        scratch=[pltpu.VMEM((32, 8, SIDE), F32)],
        flops=100000000,
    )


def inverse(total, spare, down_factors):
    _, _, col_inv, row_inv = dct_constants()
    hold = [pltpu.VMEM((16, 8, SIDE), F32)]
    message = (SLOTS, Q_DEV, LANES)
    sent = call(lower_kernel, [message], total, spare, down_factors)
    held = swap(sent, "slot")
    sent = call(inverse_columns_kernel, [message], held, col_inv, scratch=hold, flops=50000000)
    held = swap(sent, "slot")
    return call(
        inverse_rows_kernel,
        [(1, 2, Q_DEV, POINTS_DEV)],
        held,
        row_inv,
        scratch=hold,
        flops=50000000,
    )


def per_device(ciphertexts, diagonals, baby_keys, giant_keys, up_factors, down_factors):
    special = call(special_kernel, [(96, POINTS_DEV)], baby_keys, up_factors)
    special = lax.all_gather(special, "limb", axis=0)
    e0, e1, e1x = forward(ciphertexts)
    e1g = swap(e1x, "limb")
    send1, send2, send3, four, zero = babies_call(
        e1g, e0, e1, up_factors, down_factors, baby_keys, special, diagonals
    )
    gots = [shifted(send, r + 1) for r, send in enumerate((send1, send2, send3))]
    near, far = call(
        sort_kernel, [(GROUPS, 24, POINTS_DEV), (32, POINTS_DEV)], *gots, four, flops=10000
    )
    moved = shifted(far, 4)
    near = swap(near, "limb")
    far = swap(jnp.broadcast_to(moved[None, :24], (GROUPS, 24, POINTS_DEV)), "limb")
    total, spare = giants_call(near, far, up_factors, giant_keys, zero, gots, moved)
    return inverse(total, swap(spare, "limb"), down_factors)


def solution(mesh):
    placed = (
        P("ct", None, "limb", "slot"),
        P(None, None, "limb", "slot"),
        P(None, None, None, "limb", "slot"),
        P(None, None, None, "limb", "slot"),
        P("limb", None),
        P("limb", None),
    )
    return jax.shard_map(
        per_device,
        mesh=mesh,
        in_specs=placed,
        out_specs=P("ct", None, "limb", "slot"),
        check_vma=False,
    )
```

time: 283 us -> 174 us (0.61); the launches traced: 278 us -> 173 us
  local copies, waits for them, and re-layouts: 76.4 us -> 12.2 us
  waiting for transfers between devices: 58.9 us -> 27.2 us
  blocking collectives: 62.1 us -> 92.7 us
  starting transfers between devices: 41.4 us -> 12.1 us
  Pallas kernels: 0 us -> 15.2 us
  matrix products: 13.9 us -> 0 us
  other arithmetic: 10.8 us -> 0 us
    all_to_all x2 -> x6, blocking collectives: 36.4 us -> 92.7 us  [swap(): return lax.all_to_all(values, axis, split_axis=0, concat_axis=0, tiled=True)]
    all_gather x2 -> x1, waiting for transfers between devices: 26.5 us -> 0.02 us  [per_device(): special = lax.all_gather(special, 'limb', axis=0)]
    all_gather x2 -> x0, blocking collectives: 25.7 us -> none  [lower_basis(): spare_all = lax.all_gather(spare, 'limb', axis=3, tiled=True)]
    ppermute x9 -> x4, starting transfers between devices: 23 us -> 4.41 us  [shifted(): return lax.ppermute(block, 'slot', route)]
    slice x37 -> x2, local copies, waits for them, and re-layouts: 18.3 us -> 0.73 us  [the longest x1 0.72 us: babies_call(): head = special[:, 24:32, 0:LANES]]
    pallas_call x0 -> x10, Pallas kernels: none -> 15.2 us  [the longest x8 6.34 us: call(): pl.pallas_call(kernel, out_shape=shapes if len(shapes) > 1 else shapes[0]...]
    unnamed x61 -> x48, local copies, waits for them, and re-layouts: 25.7 us -> 10.6 us
    dot_general x8 -> x0, matrix products: 13.9 us -> none  [the longest x2 6.04 us: raise_basis(): jnp.einsum('var,gwri->gwvai', weight_factors, lax.all_gather(limb_rows, '...]
  transfers between devices with their start and end apart: 13 -> 7, of which waited for: 5 -> 6; matrix products, arithmetic and copies ran while one was open for 11% -> 2% of each run, Pallas kernels for 0% -> 1%
where the time goes in v1:
time: 174 us; the launch traced here: 173 us
  blocking collectives  92.7 us (53%)
  waiting for transfers between devices  27.2 us (16%)
  Pallas kernels  15.2 us (9%)
  between operations  13.6 us (8%)
  local copies, waits for them, and re-layouts  12.2 us (7%)
  starting transfers between devices  12.1 us (7%)
    all_to_all x6, blocking collectives, swap(): return lax.all_to_all(values, axis, split_axis=0, concat_axis=0, tiled=True)  92.7 us
    ppermute x4, waiting for transfers between devices, shifted(): return lax.ppermute(block, 'slot', route)  18.6 us
    unnamed x48, local copies, waits for them, and re-layouts  10.6 us
    all_to_all x2, waiting for transfers between devices, swap(): return lax.all_to_all(values, axis, split_axis=0, concat_axis=0, tiled=True)  8.61 us
    all_to_all x2, starting transfers between devices, swap(): return lax.all_to_all(values, axis, split_axis=0, concat_axis=0, tiled=True)  7.68 us
    pallas_call x8, Pallas kernels, call(): pl.pallas_call(kernel, out_shape=shapes if len(shapes) > 1 else shapes[0]...  6.34 us
    pallas_call x1, Pallas kernels, babies_call(): pl.pallas_call(babies_kernel, grid=(POINTS_DEV // CHUNK,), in_specs=[whol...  6.17 us
    ppermute x4, starting transfers between devices, shifted(): return lax.ppermute(block, 'slot', route)  4.41 us
  transfers between devices with their start and end apart: 7, of which 6 were waited for; matrix products, arithmetic and copies ran while one was open for 2% of the time, Pallas kernels for 1%

profile of v1, /device:TPU:1, one launch (start us, length us, event | category | flops | bytes accessed | tf_op | source)
XLA Modules:
  0.0 173.1 jit_solution(2441646261898912639)
XLA Ops:
  6.5 1.3 copy-done
  7.9 0.7 copy-done.16
  8.6 1.1 shard_map.157
  9.7 0.0 all-gather.3.cloned.1.call-update
  9.7 0.1 copy.20.x_ref
  9.8 0.3 shard_map.154
  10.1 23.1 %all_to_all.40.in_ref = f32[32,6,128]{2,1,0:T(8,128)S(1)} all-to-all(f32[32,6,128]{2,1,0:T(8,128)S(1)} %shard_map.154), channel_id=1, replica_groups=mesh['slot'=32,'limb'=4,'ct'=2] {'slot'}, dimensions={0} | all-to-all | bytes 196608 | tf_op jit(solution)/shard_map/all_to_all | solution.py:452
  33.3 0.8 shard_map.155
  34.1 0.1 copy.21
  34.2 15.1 %all_to_all.41 = f32[32,2,6,128]{3,1,2,0:T(2,128)S(1)} all-to-all(f32[32,2,6,128]{3,1,2,0:T(2,128)S(1)} %copy.21), channel_id=1, replica_groups=mesh['slot'=32,'limb'=4,'ct'=2] {'slot'}, dimensions={0} | all-to-all | bytes 393216 | tf_op jit(solution)/shard_map/all_to_all | solution.py:452
  49.4 1.4 shard_map.156
  50.8 0.6 copy-done.6
  51.4 0.6 copy-done.8
  52.1 4.2 %all-to-all-start.2 = ((f32[4,6,4096]{2,1,0:T(8,128)}), f32[4,6,4096]{2,1,0:T(8,128)}, u32[]{:S(2)}, u32[]{:S(2)}) async-start(f32[4,6,4096]{2,1,0:T(8,128)} %get-tuple-element.17), calls=%async_computation.2 | async-start | bytes 1048576 | tf_op jit(solution)/shard_map/all_to_all | solution.py:452
  56.3 2.4 %copy.23.diag_ref = bf16[8,8,6,2048]{3,2,1,0:T(8,128)(2,1)S(1)} copy(bf16[8,8,6,2048]{3,1,2,0:T(8,128)(2,1)} %param.17) | data formatting | bytes 3145728 | tf_op args[1]
  58.7 0.0 all-gather.3.cloned.1.call-done
  58.7 0.7 slice.8.head_ref
  59.5 5.8 %all-to-all-done.2.e1g_ref = f32[4,6,4096]{2,1,0:T(8,128)} async-done(((f32[4,6,4096]{2,1,0:T(8,128)}), f32[4,6,4096]{2,1,0:T(8,128)}, u32[]{:S(2)}, u32[]{:S(2)}) %all-to-all-start.2) | async-done | bytes 393248 | tf_op jit(solution)/shard_map/all_to_all | solution.py:452
  65.3 0.9 copy-done.7
  66.2 0.9 copy-done.9
  67.1 0.8 copy-done.13
  67.9 0.7 copy-done.18
  68.6 0.7 copy-done.21
  69.3 6.2 %shard_map.158 = (f32[24,2048]{1,0:T(8,128)S(1)}, f32[24,2048]{1,0:T(8,128)S(1)}, f32[24,2048]{1,0:T(8,128)S(1)}, f32[2,6,2048]{2,1,0:T(8,128)S(1)}, f32[2,6,2048]{2,1,0:T(8,128)S(1)}) custom-call(f32[4,6,4096]{2,1,0:T(8,128)} %all-to-all-done.2.e1g_ref, f32[6,4096]{1,0:T(8,128)S(1)} %copy-done.7, f32[6,4096]{1,0:T(8,128)S(1)} %copy-done.9, ...), custom_call_target="tpu_custom_call" | custom-call | flops 40000000 | bytes 6000000 | tf_op jit(solution)/shard_map/pallas_call | solution.py:314
  75.5 0.6 copy-done.10
  76.1 2.3 %collective-permute-start = (f32[24,2048]{1,0:T(8,128)S(1)}, f32[24,2048]{1,0:T(8,128)S(1)}, u32[]{:S(2)}, u32[]{:S(2)}) collective-permute-start(f32[24,2048]{1,0:T(8,128)S(1)} %get-tuple-element.20), channel_id=1, source_target_pairs={{0,8},{8,16},{16,24},{24,32},{32,40},{40,48},{48,56},{56,64},{64,7... | collective-permute-start | bytes 589832 | tf_op jit(solution)/shard_map/ppermute | solution.py:457
  78.5 2.0 %collective-permute-start.1 = (f32[24,2048]{1,0:T(8,128)S(1)}, f32[24,2048]{1,0:T(8,128)S(1)}, u32[]{:S(2)}, u32[]{:S(2)}) collective-permute-start(f32[24,2048]{1,0:T(8,128)S(1)} %get-tuple-element.21), channel_id=1, source_target_pairs={{0,16},{8,24},{16,32},{24,40},{32,48},{40,56},{48,64},{56,72},{64,... | collective-permute-start | bytes 589832 | tf_op jit(solution)/shard_map/ppermute | solution.py:457
  80.5 2.2 %collective-permute-done.got1_ref = f32[24,2048]{1,0:T(8,128)S(1)} collective-permute-done((f32[24,2048]{1,0:T(8,128)S(1)}, f32[24,2048]{1,0:T(8,128)S(1)}, u32[]{:S(2)}, u32[]{:S(2)}) %collective-permute-start) | collective-permute-done | bytes 196640 | tf_op jit(solution)/shard_map/ppermute | solution.py:457
  82.6 8.8 %collective-permute-done.1.got2_ref = f32[24,2048]{1,0:T(8,128)S(1)} collective-permute-done((f32[24,2048]{1,0:T(8,128)S(1)}, f32[24,2048]{1,0:T(8,128)S(1)}, u32[]{:S(2)}, u32[]{:S(2)}) %collective-permute-start.1) | collective-permute-done | bytes 196640 | tf_op jit(solution)/shard_map/ppermute | solution.py:457
  91.5 1.1 collective-permute-done.2.got3_ref
  92.6 1.0 shard_map.159
  93.6 3.5 %all-to-all-start.3 = ((f32[4,24,2048]{2,1,0:T(8,128)}), f32[4,24,2048]{2,1,0:T(8,128)S(1)}, u32[]{:S(2)}, u32[]{:S(2)}) async-start(f32[4,24,2048]{2,1,0:T(8,128)} %get-tuple-element.24), calls=%async_computation.3 | async-start | bytes 1572864 | tf_op jit(solution)/shard_map/all_to_all | solution.py:452
  97.1 0.0 copy-start.14
  97.1 0.0 copy-start.15
  97.1 0.0 copy-start.20
  97.2 0.1 collective-permute-start.3
  97.2 6.5 %collective-permute-done.3.moved_ref = f32[32,2048]{1,0:T(8,128)S(1)} collective-permute-done((f32[32,2048]{1,0:T(8,128)S(1)}, f32[32,2048]{1,0:T(8,128)S(1)}, u32[]{:S(2)}, u32[]{:S(2)}) %collective-permute-start.3) | collective-permute-done | bytes 262176 | tf_op jit(solution)/shard_map/ppermute | solution.py:457
  103.7 2.8 %all-to-all-done.3.near_ref = f32[4,24,2048]{2,1,0:T(8,128)S(1)} async-done(((f32[4,24,2048]{2,1,0:T(8,128)}), f32[4,24,2048]{2,1,0:T(8,128)S(1)}, u32[]{:S(2)}, u32[]{:S(2)}) %all-to-all-start.3) | async-done | bytes 786464 | tf_op jit(solution)/shard_map/all_to_all | solution.py:452
  106.5 0.1 broadcast_in_dim.2
  106.6 13.0 %all_to_all.42.far_ref = f32[4,24,2048]{2,1,0:T(8,128)S(1)} all-to-all(f32[4,24,2048]{2,1,0:T(8,128)S(1)} %broadcast_in_dim.2), channel_id=1, replica_groups=mesh['slot'=32,'limb'=4,'ct'=2] {'limb'}, dimensions={0} | all-to-all | bytes 1572864 | tf_op jit(solution)/shard_map/all_to_all | solution.py:452
  119.7 2.6 %shard_map.160 = (f32[2,6,2048]{2,1,0:T(8,128)S(1)}, f32[4,4,2048]{2,1,0:T(4,128)S(1)}) custom-call(f32[4,24,2048]{2,1,0:T(8,128)S(1)} %all-to-all-done.3.near_ref, f32[4,24,2048]{2,1,0:T(8,128)S(1)} %all_to_all.42.far_ref, f32[8,24]{1,0:T(8,128)S(1)} %copy-done.17, f32[96,8]{1,0:T(8,128)S(1)} %copy-done.15, f32[24,96]{1,0:T(8,128)S(1)} %copy-done.20, ...), custom_call_target="tpu_custom_call" | custom-call | flops 40000000 | bytes 4000000 | tf_op jit(solution)/shard_map/pallas_call | solution.py:397
  122.3 7.2 %all_to_all.43.spare_ref = f32[4,4,2048]{2,1,0:T(4,128)S(1)} all-to-all(f32[4,4,2048]{2,1,0:T(4,128)S(1)} %get-tuple-element.28), channel_id=1, replica_groups=mesh['slot'=32,'limb'=4,'ct'=2] {'limb'}, dimensions={0} | all-to-all | bytes 262144 | tf_op jit(solution)/shard_map/all_to_all | solution.py:452
  129.5 0.4 shard_map.161
  130.0 20.2 %all_to_all.44.in_ref = f32[32,6,128]{2,1,0:T(8,128)S(1)} all-to-all(f32[32,6,128]{2,1,0:T(8,128)S(1)} %shard_map.161), channel_id=1, replica_groups=mesh['slot'=32,'limb'=4,'ct'=2] {'slot'}, dimensions={0} | all-to-all | bytes 196608 | tf_op jit(solution)/shard_map/all_to_all | solution.py:452
  150.2 0.8 shard_map.162
  151.0 14.1 %all_to_all.45.in_ref = f32[32,6,128]{2,1,0:T(8,128)S(1)} all-to-all(f32[32,6,128]{2,1,0:T(8,128)S(1)} %shard_map.162), channel_id=1, replica_groups=mesh['slot'=32,'limb'=4,'ct'=2] {'slot'}, dimensions={0} | all-to-all | bytes 196608 | tf_op jit(solution)/shard_map/all_to_all | solution.py:452
  165.0 0.5 shard_map.163
  165.5 0.7 copy.24
  (37 shorter events, 0.1 us)
Async XLA Ops:
  6.5 52.2 %all-gather.3.cloned.1.call-start = ((), (), s32[]{:S(2)}) async-start(), calls=%async_computation.8 | async-start | bytes 3932160 | tf_op jit(solution)/shard_map/all_gather | solution.py:499
  6.5 1.3 copy-start
  7.9 0.7 copy-start.16
  8.6 1.2 copy-start.22
  8.6 24.7 %copy-start.5 = (bf16[2,256,256]{2,1,0:T(8,128)(2,1)S(1)}, bf16[2,256,256]{2,1,0:T(8,128)(2,1)}, u32[]{:S(2)}) copy-start(bf16[2,256,256]{2,1,0:T(8,128)(2,1)} %constant.18.clone.table_ref) | copy-start | bytes 786436
  9.7 39.7 %copy-start.4 = (bf16[2,256,256]{2,1,0:T(8,128)(2,1)S(1)}, bf16[2,256,256]{2,1,0:T(8,128)(2,1)}, u32[]{:S(2)}) copy-start(bf16[2,256,256]{2,1,0:T(8,128)(2,1)} %constant.19.clone.table_ref) | copy-start | bytes 786436
  50.8 0.7 copy-start.6
  51.4 0.7 copy-start.8
  52.1 13.2 %all-to-all-start.2 = ((f32[4,6,4096]{2,1,0:T(8,128)}), f32[4,6,4096]{2,1,0:T(8,128)}, u32[]{:S(2)}, u32[]{:S(2)}) async-start(f32[4,6,4096]{2,1,0:T(8,128)} %get-tuple-element.17), calls=%async_computation.2 | async-start | bytes 1048576 | tf_op jit(solution)/shard_map/all_to_all | solution.py:452
  56.3 9.0 %copy-start.1 = (bf16[7,3,2,8,2048]{4,3,2,1,0:T(8,128)(2,1)S(1)}, bf16[7,3,2,8,2048]{4,3,2,1,0:T(8,128)(2,1)}, u32[]{:S(2)}) copy-start(bf16[7,3,2,8,2048]{4,3,2,1,0:T(8,128)(2,1)} %keys_ref.4) | copy-start | bytes 4128772
  56.3 9.0 %copy-start.12 = (f32[120,32]{1,0:T(8,128)S(1)}, f32[120,32]{1,0:T(8,128)}, u32[]{:S(2)}) copy-start(f32[120,32]{1,0:T(8,128)} %constant.22.clone.mask_ref) | copy-start | bytes 46084
  56.3 9.0 %copy-start.17 = (f32[8,24]{1,0:T(8,128)S(1)}, f32[8,24]{1,0:T(8,128)}, u32[]{:S(2)}) copy-start(f32[8,24]{1,0:T(8,128)} %up_ref.5) | copy-start | bytes 2308
  65.3 0.9 copy-start.7
  66.2 0.9 copy-start.9
  67.1 0.8 copy-start.13
  67.9 0.7 copy-start.18
  68.6 0.7 copy-start.21
  75.5 0.7 copy-start.10
  76.1 6.5 %collective-permute-start = (f32[24,2048]{1,0:T(8,128)S(1)}, f32[24,2048]{1,0:T(8,128)S(1)}, u32[]{:S(2)}, u32[]{:S(2)}) collective-permute-start(f32[24,2048]{1,0:T(8,128)S(1)} %get-tuple-element.20), channel_id=1, source_target_pairs={{0,8},{8,16},{16,24},{24,32},{32,40},{40,48},{48,56},{56,64},{64,7... | collective-permute-start | bytes 589832 | tf_op jit(solution)/shard_map/ppermute | solution.py:457
  78.5 13.0 %collective-permute-start.1 = (f32[24,2048]{1,0:T(8,128)S(1)}, f32[24,2048]{1,0:T(8,128)S(1)}, u32[]{:S(2)}, u32[]{:S(2)}) collective-permute-start(f32[24,2048]{1,0:T(8,128)S(1)} %get-tuple-element.21), channel_id=1, source_target_pairs={{0,16},{8,24},{16,32},{24,40},{32,48},{40,56},{48,64},{56,72},{64,... | collective-permute-start | bytes 589832 | tf_op jit(solution)/shard_map/ppermute | solution.py:457
  80.5 12.1 %collective-permute-start.2 = (f32[24,2048]{1,0:T(8,128)S(1)}, f32[24,2048]{1,0:T(8,128)S(1)}, u32[]{:S(2)}, u32[]{:S(2)}) collective-permute-start(f32[24,2048]{1,0:T(8,128)S(1)} %get-tuple-element.22), channel_id=1, source_target_pairs={{0,24},{8,32},{16,40},{24,48},{32,56},{40,64},{48,72},{56,80},{64,... | collective-permute-start | bytes 589832 | tf_op jit(solution)/shard_map/ppermute | solution.py:457
  93.6 13.0 %all-to-all-start.3 = ((f32[4,24,2048]{2,1,0:T(8,128)}), f32[4,24,2048]{2,1,0:T(8,128)S(1)}, u32[]{:S(2)}, u32[]{:S(2)}) async-start(f32[4,24,2048]{2,1,0:T(8,128)} %get-tuple-element.24), calls=%async_computation.3 | async-start | bytes 1572864 | tf_op jit(solution)/shard_map/all_to_all | solution.py:452
  97.1 22.5 %copy-start.2 = (bf16[7,3,2,8,2048]{4,3,2,1,0:T(8,128)(2,1)S(1)}, bf16[7,3,2,8,2048]{4,3,2,1,0:T(8,128)(2,1)}, u32[]{:S(2)}) copy-start(bf16[7,3,2,8,2048]{4,3,2,1,0:T(8,128)(2,1)} %keys_ref.5) | copy-start | bytes 4128772
  97.1 22.5 %copy-start.11 = (f32[2,6,2048]{2,1,0:T(8,128)S(1)}, f32[2,6,2048]{2,1,0:T(8,128)}, u32[]{:S(2)}) copy-start(f32[2,6,2048]{2,1,0:T(8,128)} %copy-done.10) | copy-start | bytes 294916
  97.1 22.5 %copy-start.14 = (f32[96,96]{1,0:T(8,128)S(1)}, f32[96,96]{1,0:T(8,128)}, u32[]{:S(2)}) copy-start(f32[96,96]{1,0:T(8,128)} %constant.25.clone.mask_ref) | copy-start | bytes 110596
  97.1 22.5 %copy-start.15 = (f32[96,8]{1,0:T(8,128)S(1)}, f32[96,8]{1,0:T(8,128)}, u32[]{:S(2)}) copy-start(f32[96,8]{1,0:T(8,128)} %constant.23.clone.rows_ref) | copy-start | bytes 9220
  97.1 22.5 %copy-start.20 = (f32[24,96]{1,0:T(8,128)S(1)}, f32[24,96]{1,0:T(8,128)}, u32[]{:S(2)}) copy-start(f32[24,96]{1,0:T(8,128)} %constant.24.clone.pick_ref) | copy-start | bytes 27652
  97.2 6.6 %collective-permute-start.3 = (f32[32,2048]{1,0:T(8,128)S(1)}, f32[32,2048]{1,0:T(8,128)S(1)}, u32[]{:S(2)}, u32[]{:S(2)}) collective-permute-start(f32[32,2048]{1,0:T(8,128)S(1)} %get-tuple-element.25), channel_id=1, source_target_pairs={{0,32},{8,40},{16,48},{24,56},{32,64},{40,72},{48,80},{56,88},{64,... | collective-permute-start | bytes 786440 | tf_op jit(solution)/shard_map/ppermute | solution.py:457
  119.6 9.9 %copy-start.19 = (f32[6,8]{1,0:T(8,128)S(1)}, f32[6,8]{1,0:T(8,128)}, u32[]{:S(2)}) copy-start(f32[6,8]{1,0:T(8,128)} %down_ref.3) | copy-start | bytes 580
  119.6 30.5 %copy-start.3 = (bf16[2,256,256]{2,1,0:T(8,128)(2,1)S(1)}, bf16[2,256,256]{2,1,0:T(8,128)(2,1)}, u32[]{:S(2)}) copy-start(bf16[2,256,256]{2,1,0:T(8,128)(2,1)} %constant.26.clone.table_ref) | copy-start | bytes 786436
Sparse Core Ops, SparseCore 0:
  9.8 45.9 all-gather.2

commit v2 on v1

v2 whole, which is shorter than its diff:
```python
import numpy as np
import jax
import jax.numpy as jnp
import ml_dtypes
from jax import lax
from jax.experimental import pallas as pl
from jax.experimental.pallas import tpu as pltpu
from jax.sharding import PartitionSpec as P

SIDE = 256
DNUM = 3
BABY = 8
GIANT = 8
Q_DEV = 6
LANES = 128
POINTS_DEV = 2048
HALO = 2 * POINTS_DEV
SLOTS = 32
GROUPS = 4
CHUNK = 512
VMEM_BYTES = 8 * 1024 * 1024
F32 = jnp.float32
BF16 = jnp.bfloat16


def split_constant(values):
    high = values.astype(ml_dtypes.bfloat16)
    low = (values - high.astype(np.float64)).astype(ml_dtypes.bfloat16)
    return np.stack([high, low])


def cosine_matrix():
    k = np.arange(SIDE, dtype=np.float64)[:, None]
    n = np.arange(SIDE, dtype=np.float64)[None, :]
    scale = np.where(k == 0, np.sqrt(1.0 / SIDE), np.sqrt(2.0 / SIDE))
    return scale * np.cos(np.pi * (n + 0.5) * k / SIDE)


def lane_orders():
    lane = np.arange(SIDE)
    half, low = lane // LANES, lane % LANES
    block, rest = low // 64, low % 64
    rows = half * 128 + block * 64 + (rest % 8) * 8 + rest // 8
    cols_fwd = half * 128 + (low % 16) * 8 + low // 16
    c = (low // 64) * 8 + low % 8
    k = (low // 8) % 8
    cols_inv = half * 128 + c * 8 + k
    return rows, cols_fwd, cols_inv


def dct_constants():
    c = cosine_matrix()
    rows, cols_fwd, cols_inv = lane_orders()
    return (
        split_constant(c.T[rows]),
        split_constant(c.T[cols_fwd]),
        split_constant(c[rows]),
        split_constant(c[cols_inv]),
    )


def exchange(values, bits, axis=1):
    values = list(values)
    size = values[0].shape[axis]
    index = lax.broadcasted_iota(jnp.int32, values[0].shape, axis)
    for place, bit in enumerate(reversed(bits)):
        step, span = 1 << place, 1 << bit
        keep = (index & span) == 0
        for i in range(len(values)):
            if i & step:
                continue
            a, b = values[i], values[i + step]
            values[i] = jnp.where(keep, a, pltpu.roll(b, span, axis))
            values[i + step] = jnp.where(keep, pltpu.roll(a, size - span, axis), b)
    return values


def halves(values):
    high = values.astype(BF16)
    return high, (values - high.astype(F32)).astype(BF16)


def matmul(a, b):
    return lax.dot_general(a, b, (((1,), (0,)), ((), ())), preferred_element_type=F32)


def exact_matmul(a, b):
    return lax.dot_general(
        a,
        b,
        (((1,), (0,)), ((), ())),
        precision=lax.Precision.HIGHEST,
        preferred_element_type=F32,
    )


def transform(values, table):
    high, low = halves(values)
    return matmul(high, table[0]) + matmul(low, table[0]) + matmul(high, table[1])


def call(kernel, out_shapes, *args, scratch=(), flops=1000000):
    shapes = [jax.ShapeDtypeStruct(s, F32) for s in out_shapes]
    return pl.pallas_call(
        kernel,
        out_shape=shapes if len(shapes) > 1 else shapes[0],
        scratch_shapes=list(scratch),
        compiler_params=pltpu.CompilerParams(vmem_limit_bytes=VMEM_BYTES),
        cost_estimate=pl.CostEstimate(flops=flops, bytes_accessed=400000, transcendentals=0),
    )(*args)


def group_of(place_ref, m):
    return (place_ref[0] - m) & 3


def down_columns(place_ref, down_ref):
    down = down_ref[...]
    lane = lax.broadcasted_iota(jnp.int32, down.shape, 1)
    columns = []
    for m in range(GROUPS):
        for i in range(2):
            pick = jnp.where(lane == 2 * group_of(place_ref, m) + i, down, 0.0)
            column = jnp.sum(pick, axis=1, keepdims=True)
            columns.append(jnp.broadcast_to(column, (Q_DEV, LANES)))
    return columns


def lowered(kept, rows, columns):
    total = kept
    for g in range(GROUPS):
        for i in range(2):
            total = total - columns[2 * g + i] * rows(g, i)
    return total


def spread_rows(piece, out_ref):
    for h in range(2):
        parts = [piece(p, r * SIDE + h * LANES) for p in range(2) for r in range(8)]
        for c, part in enumerate(exchange(parts, (6, 5, 4, 3))):
            out_ref[h * 16 + c] = part


def rows_kernel(x_ref, out_ref):
    spread_rows(lambda p, at: x_ref[0, p, :, at : at + LANES], out_ref)


def column_transform(in_ref, table_ref, hold_ref):
    hold_ref[...] = jnp.zeros_like(hold_ref)
    for h in range(2):
        parts = exchange([in_ref[h * 16 + s] for s in range(16)], (6, 2, 1, 0))
        for i, part in enumerate(parts):
            hold_ref[i, 0:Q_DEV, h * LANES : (h + 1) * LANES] = part
    result = transform(hold_ref[...].reshape(128, SIDE), table_ref)
    return result.reshape(16, 8, SIDE)


def columns_kernel(in_ref, table_ref, out_ref, hold_ref):
    result = column_transform(in_ref, table_ref, hold_ref)
    lane = lax.broadcasted_iota(jnp.int32, (8, LANES), 1)
    first = (lane & 8) == 0
    for p in range(2):
        pairs = []
        for h in range(2):
            parts = [result[p * 8 + k][:, h * LANES : (h + 1) * LANES] for k in range(8)]
            pairs += exchange(parts, (6, 5, 4))
        for i in range(16):
            out_ref[2 * i + 1, p] = pairs[i][:Q_DEV]
            both = jnp.where(
                first, pltpu.roll(pairs[i - 1], LANES - 8, 1), pltpu.roll(pairs[i], 8, 1)
            )
            out_ref[2 * i, p] = both[:Q_DEV]


def evals_kernel(in_ref, table_ref, e0_ref, e1_ref, hold_ref):
    hold_ref[...] = jnp.zeros_like(hold_ref)
    for p in range(2):
        for h in range(2):
            parts = exchange([in_ref[h * 16 + c, p] for c in range(16)], (3, 2, 1, 0))
            for row, part in enumerate(parts):
                hold_ref[p * 16 + row, 0:Q_DEV, h * LANES : (h + 1) * LANES] = part
    result = transform(hold_ref[...].reshape(256, SIDE), table_ref).reshape(32, 8, SIDE)
    for row in range(16):
        at = slice(row * SIDE, (row + 1) * SIDE)
        e0_ref[:, at] = result[row][:Q_DEV]
        e1_ref[:, at] = result[16 + row][:Q_DEV]


def products_kernel(
    place_ref, e1a_ref, e1b_ref, e1c_ref, e1d_ref, up_ref, keys_ref,
    kept_ref, spare_ref, raised_ref, stage_ref,
):
    step = pl.program_id(0)

    @pl.when(step == 0)
    def _():
        iota = lambda shape, axis: lax.broadcasted_iota(jnp.int32, shape, axis)

        def limb(q):
            group = group_of(place_ref, q >> 3)
            return jnp.where((q & 7) < Q_DEV, 6 * group + (q & 7), -1)

        pick = (iota((24, 32), 0) == limb(iota((24, 32), 1))).astype(F32)
        spread = exact_matmul(up_ref[...], pick)
        digit = limb(iota((8, 32), 1)) >> 3
        factors = jnp.concatenate(
            [jnp.where(digit == d, spread, 0.0) for d in range(DNUM)], axis=0
        )
        fh, fl = halves(factors)
        lhs = jnp.concatenate([fh, fh, fl], axis=1)
        stage_ref[...] = jnp.zeros_like(stage_ref)
        for m, ref in enumerate((e1a_ref, e1b_ref, e1c_ref, e1d_ref)):
            stage_ref[8 * m : 8 * m + Q_DEV, :] = ref[...]
        for part in range(8):
            at = slice(part * 512, (part + 1) * 512)
            eh, el = halves(stage_ref[:, at])
            raised_ref[:, at] = matmul(lhs, jnp.concatenate([eh, el, eh], axis=0))

    def body(t, carry):
        base = pl.multiple_of(step * CHUNK + t * LANES, LANES)
        here = pl.ds(pl.multiple_of(t * LANES, LANES), LANES)
        for k in range(1, BABY):
            at = pl.ds(base + (8 - k) * SIDE, LANES)
            views = [raised_ref[d * 8 : d * 8 + 8, at] for d in range(DNUM)]
            for s in range(2):
                total = None
                for d in range(DNUM):
                    term = views[d] * keys_ref[k - 1, d, s, :, here].astype(F32)
                    total = term if total is None else total + term
                unit = 2 * (k - 1) + s
                kept_ref[unit, :, here] = total
                spare_ref[2 * unit : 2 * unit + 2, here] = total[Q_DEV:]
        return carry

    lax.fori_loop(0, CHUNK // LANES, body, 0)


def babies_kernel(
    place_ref, kept_ref, spare0_ref, spare1_ref, spare2_ref, spare3_ref,
    e0_ref, e1_ref, down_ref, diag_ref,
    send1_ref, send2_ref, send3_ref, four_ref, zero_ref,
):
    step = pl.program_id(0)
    columns = down_columns(place_ref, down_ref)
    spares = (spare0_ref, spare1_ref, spare2_ref, spare3_ref)

    def body(t, carry):
        base = pl.multiple_of(step * CHUNK + t * LANES, LANES)
        here = pl.ds(pl.multiple_of(t * LANES, LANES), LANES)
        own = pl.ds(base + POINTS_DEV, LANES)
        babies = [(e0_ref[:, own], e1_ref[:, own])]
        for k in range(1, BABY):
            polys = []
            for s in range(2):
                unit = 2 * (k - 1) + s
                rows = lambda m, i: spares[m][2 * unit + i : 2 * unit + i + 1, here]
                polys.append(lowered(kept_ref[unit, 0:Q_DEV, here], rows, columns))
            polys[0] = polys[0] + e0_ref[:, pl.ds(base + (8 - k) * SIDE, LANES)]
            babies.append(tuple(polys))
        sends = (None, send1_ref, send2_ref, send3_ref)
        for j in range(GIANT):
            inner = [None, None]
            for k in range(BABY):
                factor = diag_ref[j, k, :, here].astype(F32)
                for s in range(2):
                    term = factor * babies[k][s]
                    inner[s] = term if inner[s] is None else inner[s] + term
            if j % 4 == 0:
                target = zero_ref if j == 0 else four_ref
                target[0, :, here] = inner[0]
                target[1, :, here] = inner[1]
            else:
                at = 6 * (j // 4)
                sends[j % 4][at : at + 6, here] = inner[1]
                sends[j % 4][12 + at : 18 + at, here] = inner[0]
        return carry

    lax.fori_loop(0, CHUNK // LANES, body, 0)


def whole(a):
    return pl.BlockSpec(a.shape, lambda i, n=a.ndim: (0,) * n)


def lanes(*lead):
    return pl.BlockSpec(lead + (CHUNK,), lambda i, n=len(lead): (0,) * n + (i,))


PLACE = pl.BlockSpec(memory_space=pltpu.SMEM)


def products_call(place, evals, up, keys):
    return pl.pallas_call(
        products_kernel,
        grid=(POINTS_DEV // CHUNK,),
        in_specs=[PLACE] + [whole(e) for e in evals] + [whole(up), lanes(7, 3, 2, 8)],
        out_specs=[lanes(14, 8), lanes(28)],
        out_shape=[
            jax.ShapeDtypeStruct((14, 8, POINTS_DEV), F32),
            jax.ShapeDtypeStruct((28, POINTS_DEV), F32),
        ],
        scratch_shapes=[pltpu.VMEM((24, HALO), F32), pltpu.VMEM((32, HALO), F32)],
        compiler_params=pltpu.CompilerParams(vmem_limit_bytes=VMEM_BYTES),
        cost_estimate=pl.CostEstimate(flops=40000000, bytes_accessed=4000000, transcendentals=0),
    )(place, *evals, up, keys)


def babies_call(place, kept, spares, e0, e1, down, diagonals):
    outs = [(24, POINTS_DEV)] * 3 + [(2, Q_DEV, POINTS_DEV)] * 2
    return pl.pallas_call(
        babies_kernel,
        grid=(POINTS_DEV // CHUNK,),
        in_specs=[PLACE, lanes(14, 8)]
        + [lanes(28)] * 4
        + [whole(a) for a in (e0, e1, down)]
        + [lanes(8, 8, Q_DEV)],
        out_specs=[lanes(24)] * 3 + [lanes(2, Q_DEV)] * 2,
        out_shape=[jax.ShapeDtypeStruct(s, F32) for s in outs],
        compiler_params=pltpu.CompilerParams(vmem_limit_bytes=VMEM_BYTES),
        cost_estimate=pl.CostEstimate(flops=40000000, bytes_accessed=6000000, transcendentals=0),
    )(place, kept, *spares, e0, e1, down, diagonals)


def sort_kernel(got1_ref, got2_ref, got3_ref, four_ref, near_ref, far_ref, rest_ref):
    gots = (got1_ref, got2_ref, got3_ref)
    far_ref[0:6, :] = four_ref[1]
    rest = four_ref[0]
    for r, got in enumerate(gots):
        near_ref[6 * r : 6 * r + 6, :] = got[0:6, :]
        far_ref[6 + 6 * r : 12 + 6 * r, :] = got[6:12, :]
        rest = rest + got[18:24, :]
    near_ref[18:24, :] = jnp.zeros((6, POINTS_DEV), F32)
    rest_ref[...] = rest


def giants_kernel(
    place_ref, near0_ref, near1_ref, near2_ref, near3_ref,
    far0_ref, far1_ref, far2_ref, far3_ref, up_ref, keys_ref,
    zero_ref, got1_ref, got2_ref, got3_ref, moved_ref,
    total_ref, spare_ref,
    raised_ref, factor_ref,
):
    step = pl.program_id(0)

    @pl.when(step == 0)
    def _():
        iota = lambda shape, axis: lax.broadcasted_iota(jnp.int32, shape, axis)

        def source(q):
            block = (q >= 24).astype(jnp.int32) + (q >= 48) + (q >= 72)
            rest = q - 24 * block
            giant = (rest * 43) >> 8
            return giant, 6 * group_of(place_ref, block) + rest - 6 * giant

        pick = (iota((24, 96), 0) == source(iota((24, 96), 1))[1]).astype(F32)
        spread = exact_matmul(up_ref[...], pick)
        held, limb = source(iota((8, 96), 1))
        for j in range(4):
            parts = [
                jnp.where((held == j) & ((limb >> 3) == d), spread, 0.0) for d in range(DNUM)
            ]
            at = slice(j * 24, j * 24 + 24)
            fh, fl = halves(jnp.concatenate(parts, axis=0))
            factor_ref[0, at], factor_ref[1, at] = fh.astype(F32), fl.astype(F32)

    fh, fl = factor_ref[0].astype(BF16), factor_ref[1].astype(BF16)
    nears = (near0_ref, near1_ref, near2_ref, near3_ref)
    fars = (far0_ref, far1_ref, far2_ref, far3_ref)
    for part, refs in enumerate((nears, fars)):
        eh, el = halves(jnp.concatenate([ref[...] for ref in refs], axis=0))
        raised_ref[part] = matmul(fh, eh) + matmul(fh, el) + matmul(fl, eh)

    def body(t, carry):
        here = pl.ds(pl.multiple_of(t * LANES, LANES), LANES)
        sums = [None, None]
        for j in range(1, GIANT):
            for d in range(DNUM):
                at = (j - 1 if j < 4 else j - 4) * 24 + d * 8
                value = raised_ref[j // 4, at : at + 8, here]
                for s in range(2):
                    term = value * keys_ref[j - 1, d, s, :, here].astype(F32)
                    sums[s] = term if sums[s] is None else sums[s] + term
        first = zero_ref[0, :, here] + moved_ref[:, here]
        for got in (got1_ref, got2_ref, got3_ref):
            first = first + got[12:18, here]
        total_ref[0, :, here] = first + sums[0][:Q_DEV]
        total_ref[1, :, here] = zero_ref[1, :, here] + sums[1][:Q_DEV]
        spare_ref[0:2, here] = sums[0][Q_DEV:]
        spare_ref[2:4, here] = sums[1][Q_DEV:]
        return carry

    lax.fori_loop(0, CHUNK // LANES, body, 0)


def giants_call(place, nears, fars, up, keys, zero, gots, moved):
    return pl.pallas_call(
        giants_kernel,
        grid=(POINTS_DEV // CHUNK,),
        in_specs=[PLACE]
        + [lanes(24)] * 8
        + [whole(up), lanes(7, 3, 2, 8), lanes(2, Q_DEV)]
        + [lanes(24)] * 3
        + [lanes(Q_DEV)],
        out_specs=[lanes(2, Q_DEV), lanes(4)],
        out_shape=[
            jax.ShapeDtypeStruct((2, Q_DEV, POINTS_DEV), F32),
            jax.ShapeDtypeStruct((4, POINTS_DEV), F32),
        ],
        scratch_shapes=[pltpu.VMEM((2, 96, CHUNK), F32), pltpu.VMEM((2, 96, 96), F32)],
        compiler_params=pltpu.CompilerParams(vmem_limit_bytes=VMEM_BYTES),
        cost_estimate=pl.CostEstimate(flops=40000000, bytes_accessed=4000000, transcendentals=0),
    )(place, *nears, *fars, up, keys, zero, *gots, moved)


def lower_kernel(
    place_ref, total_ref, spare0_ref, spare1_ref, spare2_ref, spare3_ref, down_ref, out_ref
):
    columns = down_columns(place_ref, down_ref)
    spares = (spare0_ref, spare1_ref, spare2_ref, spare3_ref)

    def piece(p, at):
        rows = lambda m, i: spares[m][2 * p + i : 2 * p + i + 1, at : at + LANES]
        return lowered(total_ref[p, :, at : at + LANES], rows, columns)

    spread_rows(piece, out_ref)


def lower_call(place, total, spares, down):
    out = (SLOTS, Q_DEV, LANES)
    return pl.pallas_call(
        lower_kernel,
        in_specs=[PLACE] + [pl.BlockSpec(memory_space=pltpu.VMEM)] * 6,
        out_specs=pl.BlockSpec(memory_space=pltpu.VMEM),
        out_shape=jax.ShapeDtypeStruct(out, F32),
        compiler_params=pltpu.CompilerParams(vmem_limit_bytes=VMEM_BYTES),
        cost_estimate=pl.CostEstimate(flops=1000000, bytes_accessed=400000, transcendentals=0),
    )(place, total, *spares, down)


def inverse_columns_kernel(in_ref, table_ref, out_ref, hold_ref):
    result = column_transform(in_ref, table_ref, hold_ref)
    for h in range(2):
        parts = [result[i][:, h * LANES : (h + 1) * LANES] for i in range(16)]
        for g, part in enumerate(exchange(parts, (6, 5, 4, 3))):
            out_ref[h * 16 + g] = part[:Q_DEV]


def inverse_rows_kernel(in_ref, table_ref, out_ref, hold_ref):
    hold_ref[...] = jnp.zeros_like(hold_ref)
    for h in range(2):
        parts = exchange([in_ref[h * 16 + c] for c in range(16)], (6, 2, 1, 0))
        for i, part in enumerate(parts):
            hold_ref[i, 0:Q_DEV, h * LANES : (h + 1) * LANES] = part
    result = transform(hold_ref[...].reshape(128, SIDE), table_ref).reshape(16, 8, SIDE)
    for p in range(2):
        for r in range(8):
            out_ref[0, p, :, r * SIDE : (r + 1) * SIDE] = result[p * 8 + r][:Q_DEV]


def swap(values, axis):
    return lax.all_to_all(values, axis, split_axis=0, concat_axis=0, tiled=True)


def shifted(block, distance):
    route = [(i, (i + distance) % SLOTS) for i in range(SLOTS)]
    return lax.ppermute(block, "slot", route)


def forward(ciphertexts):
    col_fwd, row_fwd, _, _ = dct_constants()
    hold = [pltpu.VMEM((16, 8, SIDE), F32)]
    sent = call(rows_kernel, [(SLOTS, Q_DEV, LANES)], ciphertexts)
    held = swap(sent, "slot")
    sent = call(
        columns_kernel, [(SLOTS, 2, Q_DEV, LANES)], held, col_fwd, scratch=hold, flops=50000000
    )
    held = swap(sent, "slot")
    return call(
        evals_kernel,
        [(Q_DEV, HALO), (Q_DEV, HALO)],
        held,
        row_fwd,
        scratch=[pltpu.VMEM((32, 8, SIDE), F32)],
        flops=100000000,
    )


def inverse(sent):
    _, _, col_inv, row_inv = dct_constants()
    hold = [pltpu.VMEM((16, 8, SIDE), F32)]
    held = swap(sent, "slot")
    sent = call(
        inverse_columns_kernel,
        [(SLOTS, Q_DEV, LANES)],
        held,
        col_inv,
        scratch=hold,
        flops=50000000,
    )
    held = swap(sent, "slot")
    return call(
        inverse_rows_kernel,
        [(1, 2, Q_DEV, POINTS_DEV)],
        held,
        row_inv,
        scratch=hold,
        flops=50000000,
    )


def gathered(block):
    routes = [[(i, (i + m) % GROUPS) for i in range(GROUPS)] for m in range(GROUPS)]
    return [block] + [lax.ppermute(block, "limb", routes[m]) for m in range(1, GROUPS)]


def per_device(ciphertexts, diagonals, baby_keys, giant_keys, up, down):
    place = lax.axis_index("limb").astype(jnp.int32).reshape(1)
    e0, e1 = forward(ciphertexts)
    kept, spare = products_call(place, gathered(e1), up, baby_keys)
    *sends, four, zero = babies_call(place, kept, gathered(spare), e0, e1, down, diagonals)
    gots = [shifted(send, r + 1) for r, send in enumerate(sends)]
    near, far, rest = call(
        sort_kernel,
        [(24, POINTS_DEV), (24, POINTS_DEV), (Q_DEV, POINTS_DEV)],
        *gots,
        four,
        flops=10000,
    )
    far, rest = shifted(far, 4), shifted(rest, 4)
    total, spare = giants_call(
        place, gathered(near), gathered(far), up, giant_keys, zero, gots, rest
    )
    return inverse(lower_call(place, total, gathered(spare), down))


def solution(mesh):
    placed = (
        P("ct", None, "limb", "slot"),
        P(None, None, "limb", "slot"),
        P(None, None, None, "limb", "slot"),
        P(None, None, None, "limb", "slot"),
        P("limb", None),
        P("limb", None),
    )
    return jax.shard_map(
        per_device,
        mesh=mesh,
        in_specs=placed,
        out_specs=P("ct", None, "limb", "slot"),
        check_vma=False,
    )
```

time: 174 us -> 154 us (0.89)
  waiting for transfers between devices: 27.2 us -> 54.4 us
  blocking collectives: 92.7 us -> 71.7 us
  between operations: 13.6 us -> 0.16 us
  local copies, waits for them, and re-layouts: 12.2 us -> 3.96 us
  Pallas kernels: 15.2 us -> 9.59 us
    ppermute x0 -> x15, waiting for transfers between devices: none -> 37.3 us  [gathered(): lax.ppermute(block, 'limb', routes[m])]
    all_to_all x6 -> x4, blocking collectives: 92.7 us -> 71.7 us  [swap(): return lax.all_to_all(values, axis, split_axis=0, concat_axis=0, tiled=True)]
    ppermute x0 -> x15, starting transfers between devices: none -> 10.7 us  [gathered(): lax.ppermute(block, 'limb', routes[m])]
    all_to_all x2 -> x0, waiting for transfers between devices: 8.61 us -> none  [swap(): return lax.all_to_all(values, axis, split_axis=0, concat_axis=0, tiled=True)]
    all_to_all x2 -> x0, starting transfers between devices: 7.68 us -> none  [swap(): return lax.all_to_all(values, axis, split_axis=0, concat_axis=0, tiled=True)]
    unnamed x48 -> x18, local copies, waits for them, and re-layouts: 10.6 us -> 3.1 us
    pallas_call x8 -> x6, Pallas kernels: 6.34 us -> 3.07 us  [call(): pl.pallas_call(kernel, out_shape=shapes if len(shapes) > 1 else shapes[0]...]
    pallas_call x2 -> x4, Pallas kernels: 8.82 us -> 6.52 us  [the longest x1 2.54 us: giants_call(): pl.pallas_call(giants_kernel, grid=(POINTS_DEV // CHUNK,), in_specs=[PLAC...]
  transfers between devices with their start and end apart: 7 -> 20, of which waited for: 6 -> 18; matrix products, arithmetic and copies ran while one was open for 2% -> 1% of each run, Pallas kernels for 1% -> 0%
where the time goes in v2:
time: 154 us; the launch traced here: 153 us
  blocking collectives  71.7 us (47%)
  waiting for transfers between devices  54.4 us (35%)
  starting transfers between devices  13.4 us (9%)
  Pallas kernels  9.59 us (6%)
  local copies, waits for them, and re-layouts  3.96 us (3%)
    all_to_all x4, blocking collectives, swap(): return lax.all_to_all(values, axis, split_axis=0, concat_axis=0, tiled=True)  71.7 us
    ppermute x15, waiting for transfers between devices, gathered(): lax.ppermute(block, 'limb', routes[m])  37.3 us
    ppermute x5, waiting for transfers between devices, shifted(): return lax.ppermute(block, 'slot', route)  17.1 us
    ppermute x15, starting transfers between devices, gathered(): lax.ppermute(block, 'limb', routes[m])  10.7 us
    unnamed x18, local copies, waits for them, and re-layouts  3.1 us
  transfers between devices with their start and end apart: 20, of which 18 were waited for; matrix products, arithmetic and copies ran while one was open for 1% of the time, Pallas kernels for 0%

profile of v2, /device:TPU:1, one launch (start us, length us, event | category | flops | bytes accessed | tf_op | source)
XLA Modules:
  0.0 153.3 jit_solution(18168690149714958741)
XLA Ops:
  0.0 1.1 copy.14.x_ref
  1.1 0.3 shard_map.100
  1.4 23.1 %all_to_all.20.in_ref = f32[32,6,128]{2,1,0:T(8,128)S(1)} all-to-all(f32[32,6,128]{2,1,0:T(8,128)S(1)} %shard_map.100), channel_id=1, replica_groups=mesh['slot'=32,'limb'=4,'ct'=2] {'slot'}, dimensions={0} | all-to-all | bytes 196608 | tf_op jit(solution)/shard_map/all_to_all | solution.py:461
  24.6 0.9 copy-done.4
  25.5 0.8 shard_map.101
  26.4 15.1 %all_to_all.21 = f32[32,2,6,128]{3,1,2,0:T(2,128)S(1)} all-to-all(f32[32,2,6,128]{3,1,2,0:T(2,128)S(1)} %copy.15), channel_id=1, replica_groups=mesh['slot'=32,'limb'=4,'ct'=2] {'slot'}, dimensions={0} | all-to-all | bytes 393216 | tf_op jit(solution)/shard_map/all_to_all | solution.py:461
  41.6 0.6 shard_map.102
  42.2 2.8 %collective-permute-start.2 = (f32[6,4096]{1,0:T(8,128)S(1)}, f32[6,4096]{1,0:T(8,128)S(1)}, u32[]{:S(2)}, u32[]{:S(2)}) collective-permute-start(f32[6,4096]{1,0:T(8,128)S(1)} %get-tuple-element.19.e1a_ref.e1_ref), channel_id=1, source_target_pairs={{0,6},{2,0},{4,2},{6,4},{1,7},{3,1},{5,3},{7,5},{8,14},{10,8},{12,... | collective-permute-start | bytes 294920 | tf_op jit(solution)/shard_map/ppermute | solution.py:513
  45.0 0.4 collective-permute-start.1
  45.4 0.7 collective-permute-start
  46.1 4.1 %collective-permute-done.2.e1d_ref = f32[6,4096]{1,0:T(8,128)S(1)} collective-permute-done((f32[6,4096]{1,0:T(8,128)S(1)}, f32[6,4096]{1,0:T(8,128)S(1)}, u32[]{:S(2)}, u32[]{:S(2)}) %collective-permute-start.2) | collective-permute-done | bytes 98336 | tf_op jit(solution)/shard_map/ppermute | solution.py:513
  50.2 0.7 collective-permute-done.1.e1c_ref
  50.9 3.9 %collective-permute-done.e1b_ref = f32[6,4096]{1,0:T(8,128)S(1)} collective-permute-done((f32[6,4096]{1,0:T(8,128)S(1)}, f32[6,4096]{1,0:T(8,128)S(1)}, u32[]{:S(2)}, u32[]{:S(2)}) %collective-permute-start) | collective-permute-done | bytes 98336 | tf_op jit(solution)/shard_map/ppermute | solution.py:513
  54.8 1.2 shard_map.103
  56.2 1.4 collective-permute-start.3
  57.6 1.0 copy.17.diag_ref
  58.6 4.9 %collective-permute-done.5.spare3_ref = f32[28,2048]{1,0:T(8,128)S(1)} collective-permute-done((f32[28,2048]{1,0:T(8,128)S(1)}, f32[28,2048]{1,0:T(8,128)S(1)}, u32[]{:S(2)}, u32[]{:S(2)}) %collective-permute-start.5) | collective-permute-done | bytes 229408 | tf_op jit(solution)/shard_map/ppermute | solution.py:513
  63.5 1.1 collective-permute-done.4.spare2_ref
  64.6 7.0 %collective-permute-done.3.spare1_ref = f32[28,2048]{1,0:T(8,128)S(1)} collective-permute-done((f32[28,2048]{1,0:T(8,128)S(1)}, f32[28,2048]{1,0:T(8,128)S(1)}, u32[]{:S(2)}, u32[]{:S(2)}) %collective-permute-start.3) | collective-permute-done | bytes 229408 | tf_op jit(solution)/shard_map/ppermute | solution.py:513
  71.6 2.3 %shard_map.104 = (f32[24,2048]{1,0:T(8,128)S(1)}, f32[24,2048]{1,0:T(8,128)S(1)}, f32[24,2048]{1,0:T(8,128)S(1)}, f32[2,6,2048]{2,1,0:T(8,128)S(1)}, f32[2,6,2048]{2,1,0:T(8,128)S(1)}) custom-call(s32[1]{0:T(128)} %bitcast.place_ref, f32[14,8,2048]{2,1,0:T(8,128)S(1)} %get-tuple-element.20.kept_ref, f32[28,2048]{1,0:T(8,128)S(1)} %get-tuple-element.21.spare0_ref, ...), custom_call_target="tpu_custom_call" | custom-call | flops 40000000 | bytes 6000000 | tf_op jit(solution)/shard_map/pallas_call | solution.py:310
  73.9 0.7 collective-permute-start.6
  74.6 1.7 %collective-permute-start.7 = (f32[24,2048]{1,0:T(8,128)S(1)}, f32[24,2048]{1,0:T(8,128)S(1)}, u32[]{:S(2)}, u32[]{:S(2)}) collective-permute-start(f32[24,2048]{1,0:T(8,128)S(1)} %get-tuple-element.24), channel_id=1, source_target_pairs={{0,16},{8,24},{16,32},{24,40},{32,48},{40,56},{48,64},{56,72},{64,... | collective-permute-start | bytes 589832 | tf_op jit(solution)/shard_map/ppermute | solution.py:466
  76.3 0.1 collective-permute-start.8
  76.4 2.2 %collective-permute-done.6.got1_ref = f32[24,2048]{1,0:T(8,128)S(1)} collective-permute-done((f32[24,2048]{1,0:T(8,128)S(1)}, f32[24,2048]{1,0:T(8,128)S(1)}, u32[]{:S(2)}, u32[]{:S(2)}) %collective-permute-start.6) | collective-permute-done | bytes 196640 | tf_op jit(solution)/shard_map/ppermute | solution.py:466
  78.7 9.5 %collective-permute-done.7.got2_ref = f32[24,2048]{1,0:T(8,128)S(1)} collective-permute-done((f32[24,2048]{1,0:T(8,128)S(1)}, f32[24,2048]{1,0:T(8,128)S(1)}, u32[]{:S(2)}, u32[]{:S(2)}) %collective-permute-start.7) | collective-permute-done | bytes 196640 | tf_op jit(solution)/shard_map/ppermute | solution.py:466
  88.2 1.2 collective-permute-done.8.got3_ref
  89.6 0.9 collective-permute-start.11
  90.6 0.9 collective-permute-start.9
  91.4 4.2 %collective-permute-done.12.far0_ref = f32[24,2048]{1,0:T(8,128)S(1)} collective-permute-done((f32[24,2048]{1,0:T(8,128)S(1)}, f32[24,2048]{1,0:T(8,128)S(1)}, u32[]{:S(2)}, u32[]{:S(2)}) %collective-permute-start.12) | collective-permute-done | bytes 196640 | tf_op jit(solution)/shard_map/ppermute | solution.py:466
  95.6 0.8 collective-permute-start.15
  96.5 1.1 collective-permute-start.13
  97.6 1.5 collective-permute-done.10.near2_ref
  99.1 4.2 %collective-permute-done.9.near1_ref = f32[24,2048]{1,0:T(8,128)S(1)} collective-permute-done((f32[24,2048]{1,0:T(8,128)S(1)}, f32[24,2048]{1,0:T(8,128)S(1)}, u32[]{:S(2)}, u32[]{:S(2)}) %collective-permute-start.9) | collective-permute-done | bytes 196640 | tf_op jit(solution)/shard_map/ppermute | solution.py:513
  103.3 0.3 collective-permute-done.15.far3_ref
  103.5 3.5 %collective-permute-done.14.far2_ref = f32[24,2048]{1,0:T(8,128)S(1)} collective-permute-done((f32[24,2048]{1,0:T(8,128)S(1)}, f32[24,2048]{1,0:T(8,128)S(1)}, u32[]{:S(2)}, u32[]{:S(2)}) %collective-permute-start.14) | collective-permute-done | bytes 196640 | tf_op jit(solution)/shard_map/ppermute | solution.py:513
  107.1 2.2 %collective-permute-done.13.far1_ref = f32[24,2048]{1,0:T(8,128)S(1)} collective-permute-done((f32[24,2048]{1,0:T(8,128)S(1)}, f32[24,2048]{1,0:T(8,128)S(1)}, u32[]{:S(2)}, u32[]{:S(2)}) %collective-permute-start.13) | collective-permute-done | bytes 196640 | tf_op jit(solution)/shard_map/ppermute | solution.py:513
  109.2 2.5 %shard_map.106 = (f32[2,6,2048]{2,1,0:T(8,128)S(1)}, f32[4,2048]{1,0:T(4,128)S(1)}) custom-call(s32[1]{0:T(128)} %bitcast.place_ref, f32[24,2048]{1,0:T(8,128)S(1)} %get-tuple-element.27.near0_ref, f32[24,2048]{1,0:T(8,128)S(1)} %collective-permute-done.9.near1_ref, f32[24,2048]{1,0:T(8,128)S(1)} %collective-permute-done.10.near2_ref, ...), custom_call_target="tpu_custom_call" | custom-call | flops 40000000 | bytes 4000000 | tf_op jit(solution)/shard_map/pallas_call | solution.py:396
  111.8 0.3 collective-permute-start.19
  112.1 1.3 collective-permute-start.17
  113.3 1.3 collective-permute-done.19.spare3_ref
  114.6 1.7 %collective-permute-done.18.spare2_ref = f32[4,2048]{1,0:T(4,128)S(1)} collective-permute-done((f32[4,2048]{1,0:T(4,128)S(1)}, f32[4,2048]{1,0:T(4,128)S(1)}, u32[]{:S(2)}, u32[]{:S(2)}) %collective-permute-start.18) | collective-permute-done | bytes 32800 | tf_op jit(solution)/shard_map/ppermute | solution.py:513
  116.4 1.0 collective-permute-done.17.spare1_ref
  117.4 0.4 shard_map.107
  117.8 19.4 %all_to_all.22.in_ref = f32[32,6,128]{2,1,0:T(8,128)S(1)} all-to-all(f32[32,6,128]{2,1,0:T(8,128)S(1)} %shard_map.107), channel_id=1, replica_groups=mesh['slot'=32,'limb'=4,'ct'=2] {'slot'}, dimensions={0} | all-to-all | bytes 196608 | tf_op jit(solution)/shard_map/all_to_all | solution.py:461
  137.2 0.8 shard_map.108
  138.0 14.1 %all_to_all.23.in_ref = f32[32,6,128]{2,1,0:T(8,128)S(1)} all-to-all(f32[32,6,128]{2,1,0:T(8,128)S(1)} %shard_map.108), channel_id=1, replica_groups=mesh['slot'=32,'limb'=4,'ct'=2] {'slot'}, dimensions={0} | all-to-all | bytes 196608 | tf_op jit(solution)/shard_map/all_to_all | solution.py:461
  152.1 0.5 shard_map.109
  152.6 0.7 copy.18
  (27 shorter events, 0.7 us)
Async XLA Ops:
  0.0 41.6 %copy-start.3 = (bf16[2,256,256]{2,1,0:T(8,128)(2,1)S(1)}, bf16[2,256,256]{2,1,0:T(8,128)(2,1)}, u32[]{:S(2)}) copy-start(bf16[2,256,256]{2,1,0:T(8,128)(2,1)} %constant.13.clone.table_ref) | copy-start | bytes 786436
  0.0 54.8 %copy-start.1 = (bf16[7,3,2,8,2048]{4,3,2,1,0:T(8,128)(2,1)S(1)}, bf16[7,3,2,8,2048]{4,3,2,1,0:T(8,128)(2,1)}, u32[]{:S(2)}) copy-start(bf16[7,3,2,8,2048]{4,3,2,1,0:T(8,128)(2,1)} %keys_ref.2) | copy-start | bytes 4128772
  24.6 1.0 copy-start.4
  25.5 29.3 %copy-start.5 = (f32[8,24]{1,0:T(8,128)S(1)}, f32[8,24]{1,0:T(8,128)}, u32[]{:S(2)}) copy-start(f32[8,24]{1,0:T(8,128)} %up_ref.3) | copy-start | bytes 2308
  42.2 8.0 %collective-permute-start.2 = (f32[6,4096]{1,0:T(8,128)S(1)}, f32[6,4096]{1,0:T(8,128)S(1)}, u32[]{:S(2)}, u32[]{:S(2)}) collective-permute-start(f32[6,4096]{1,0:T(8,128)S(1)} %get-tuple-element.19.e1a_ref.e1_ref), channel_id=1, source_target_pairs={{0,6},{2,0},{4,2},{6,4},{1,7},{3,1},{5,3},{7,5},{8,14},{10,8},{12,... | collective-permute-start | bytes 294920 | tf_op jit(solution)/shard_map/ppermute | solution.py:513
  45.0 5.9 %collective-permute-start.1 = (f32[6,4096]{1,0:T(8,128)S(1)}, f32[6,4096]{1,0:T(8,128)S(1)}, u32[]{:S(2)}, u32[]{:S(2)}) collective-permute-start(f32[6,4096]{1,0:T(8,128)S(1)} %get-tuple-element.19.e1a_ref.e1_ref), channel_id=1, source_target_pairs={{0,4},{2,6},{4,0},{6,2},{1,5},{3,7},{5,1},{7,3},{8,12},{10,14},{12... | collective-permute-start | bytes 294920 | tf_op jit(solution)/shard_map/ppermute | solution.py:513
  45.4 9.4 %collective-permute-start = (f32[6,4096]{1,0:T(8,128)S(1)}, f32[6,4096]{1,0:T(8,128)S(1)}, u32[]{:S(2)}, u32[]{:S(2)}) collective-permute-start(f32[6,4096]{1,0:T(8,128)S(1)} %get-tuple-element.19.e1a_ref.e1_ref), channel_id=1, source_target_pairs={{0,2},{2,4},{4,6},{6,0},{1,3},{3,5},{5,7},{7,1},{8,10},{10,12},{12... | collective-permute-start | bytes 294920 | tf_op jit(solution)/shard_map/ppermute | solution.py:513
  46.1 11.5 %copy-start.7 = (bf16[8,8,6,2048]{3,1,2,0:T(8,128)(2,1)S(1)}, bf16[8,8,6,2048]{3,1,2,0:T(8,128)(2,1)}, u32[]{:S(2)}) copy-start(bf16[8,8,6,2048]{3,1,2,0:T(8,128)(2,1)} %param.11) | copy-start | bytes 4718596
  56.0 15.5 %copy-start.6 = (f32[6,8]{1,0:T(8,128)S(1)}, f32[6,8]{1,0:T(8,128)}, u32[]{:S(2)}) copy-start(f32[6,8]{1,0:T(8,128)} %down_ref.3) | copy-start | bytes 580
  56.0 7.5 %collective-permute-start.5 = (f32[28,2048]{1,0:T(8,128)S(1)}, f32[28,2048]{1,0:T(8,128)S(1)}, u32[]{:S(2)}, u32[]{:S(2)}) collective-permute-start(f32[28,2048]{1,0:T(8,128)S(1)} %get-tuple-element.21.spare0_ref), channel_id=1, source_target_pairs={{0,6},{2,0},{4,2},{6,4},{1,7},{3,1},{5,3},{7,5},{8,14},{10,8},{12,... | collective-permute-start | bytes 688136 | tf_op jit(solution)/shard_map/ppermute | solution.py:513
  56.1 8.5 %collective-permute-start.4 = (f32[28,2048]{1,0:T(8,128)S(1)}, f32[28,2048]{1,0:T(8,128)S(1)}, u32[]{:S(2)}, u32[]{:S(2)}) collective-permute-start(f32[28,2048]{1,0:T(8,128)S(1)} %get-tuple-element.21.spare0_ref), channel_id=1, source_target_pairs={{0,4},{2,6},{4,0},{6,2},{1,5},{3,7},{5,1},{7,3},{8,12},{10,14},{12... | collective-permute-start | bytes 688136 | tf_op jit(solution)/shard_map/ppermute | solution.py:513
  56.2 15.3 %collective-permute-start.3 = (f32[28,2048]{1,0:T(8,128)S(1)}, f32[28,2048]{1,0:T(8,128)S(1)}, u32[]{:S(2)}, u32[]{:S(2)}) collective-permute-start(f32[28,2048]{1,0:T(8,128)S(1)} %get-tuple-element.21.spare0_ref), channel_id=1, source_target_pairs={{0,2},{2,4},{4,6},{6,0},{1,3},{3,5},{5,7},{7,1},{8,10},{10,12},{12... | collective-permute-start | bytes 688136 | tf_op jit(solution)/shard_map/ppermute | solution.py:513
  71.6 37.7 %copy-start = (bf16[7,3,2,8,2048]{4,3,2,1,0:T(8,128)(2,1)S(1)}, bf16[7,3,2,8,2048]{4,3,2,1,0:T(8,128)(2,1)}, u32[]{:S(2)}) copy-start(bf16[7,3,2,8,2048]{4,3,2,1,0:T(8,128)(2,1)} %keys_ref.3) | copy-start | bytes 4128772
  73.9 4.8 %collective-permute-start.6 = (f32[24,2048]{1,0:T(8,128)S(1)}, f32[24,2048]{1,0:T(8,128)S(1)}, u32[]{:S(2)}, u32[]{:S(2)}) collective-permute-start(f32[24,2048]{1,0:T(8,128)S(1)} %get-tuple-element.23), channel_id=1, source_target_pairs={{0,8},{8,16},{16,24},{24,32},{32,40},{40,48},{48,56},{56,64},{64,7... | collective-permute-start | bytes 589832 | tf_op jit(solution)/shard_map/ppermute | solution.py:466
  74.6 13.6 %collective-permute-start.7 = (f32[24,2048]{1,0:T(8,128)S(1)}, f32[24,2048]{1,0:T(8,128)S(1)}, u32[]{:S(2)}, u32[]{:S(2)}) collective-permute-start(f32[24,2048]{1,0:T(8,128)S(1)} %get-tuple-element.24), channel_id=1, source_target_pairs={{0,16},{8,24},{16,32},{24,40},{32,48},{40,56},{48,64},{56,72},{64,... | collective-permute-start | bytes 589832 | tf_op jit(solution)/shard_map/ppermute | solution.py:466
  76.3 13.1 %collective-permute-start.8 = (f32[24,2048]{1,0:T(8,128)S(1)}, f32[24,2048]{1,0:T(8,128)S(1)}, u32[]{:S(2)}, u32[]{:S(2)}) collective-permute-start(f32[24,2048]{1,0:T(8,128)S(1)} %get-tuple-element.25), channel_id=1, source_target_pairs={{0,24},{8,32},{16,40},{24,48},{32,56},{40,64},{48,72},{56,80},{64,... | collective-permute-start | bytes 589832 | tf_op jit(solution)/shard_map/ppermute | solution.py:466
  89.5 6.1 %collective-permute-start.12 = (f32[24,2048]{1,0:T(8,128)S(1)}, f32[24,2048]{1,0:T(8,128)S(1)}, u32[]{:S(2)}, u32[]{:S(2)}) collective-permute-start(f32[24,2048]{1,0:T(8,128)S(1)} %get-tuple-element.28), channel_id=1, source_target_pairs={{0,32},{8,40},{16,48},{24,56},{32,64},{40,72},{48,80},{56,88},{64,... | collective-permute-start | bytes 589832 | tf_op jit(solution)/shard_map/ppermute | solution.py:466
  89.6 6.9 %collective-permute-start.11 = (f32[24,2048]{1,0:T(8,128)S(1)}, f32[24,2048]{1,0:T(8,128)S(1)}, u32[]{:S(2)}, u32[]{:S(2)}) collective-permute-start(f32[24,2048]{1,0:T(8,128)S(1)} %get-tuple-element.27.near0_ref), channel_id=1, source_target_pairs={{0,6},{2,0},{4,2},{6,4},{1,7},{3,1},{5,3},{7,5},{8,14},{10,8},{12,... | collective-permute-start | bytes 589832 | tf_op jit(solution)/shard_map/ppermute | solution.py:513
  90.5 5.9 %collective-permute-start.16 = (f32[6,2048]{1,0:T(8,128)S(1)}, f32[6,2048]{1,0:T(8,128)S(1)}, u32[]{:S(2)}, u32[]{:S(2)}) collective-permute-start(f32[6,2048]{1,0:T(8,128)S(1)} %get-tuple-element.30), channel_id=1, source_target_pairs={{0,32},{8,40},{16,48},{24,56},{32,64},{40,72},{48,80},{56,88},{64,... | collective-permute-start | bytes 147464 | tf_op jit(solution)/shard_map/ppermute | solution.py:466
  90.6 8.5 %collective-permute-start.10 = (f32[24,2048]{1,0:T(8,128)S(1)}, f32[24,2048]{1,0:T(8,128)S(1)}, u32[]{:S(2)}, u32[]{:S(2)}) collective-permute-start(f32[24,2048]{1,0:T(8,128)S(1)} %get-tuple-element.27.near0_ref), channel_id=1, source_target_pairs={{0,4},{2,6},{4,0},{6,2},{1,5},{3,7},{5,1},{7,3},{8,12},{10,14},{12... | collective-permute-start | bytes 589832 | tf_op jit(solution)/shard_map/ppermute | solution.py:513
  90.6 12.7 %collective-permute-start.9 = (f32[24,2048]{1,0:T(8,128)S(1)}, f32[24,2048]{1,0:T(8,128)S(1)}, u32[]{:S(2)}, u32[]{:S(2)}) collective-permute-start(f32[24,2048]{1,0:T(8,128)S(1)} %get-tuple-element.27.near0_ref), channel_id=1, source_target_pairs={{0,2},{2,4},{4,6},{6,0},{1,3},{3,5},{5,7},{7,1},{8,10},{10,12},{12... | collective-permute-start | bytes 589832 | tf_op jit(solution)/shard_map/ppermute | solution.py:513
  95.6 7.9 %collective-permute-start.15 = (f32[24,2048]{1,0:T(8,128)S(1)}, f32[24,2048]{1,0:T(8,128)S(1)}, u32[]{:S(2)}, u32[]{:S(2)}) collective-permute-start(f32[24,2048]{1,0:T(8,128)S(1)} %collective-permute-done.12.far0_ref), channel_id=1, source_target_pairs={{0,6},{2,0},{4,2},{6,4},{1,7},{3,1},{5,3},{7,5},{8,14},{10,8},{12,... | collective-permute-start | bytes 589832 | tf_op jit(solution)/shard_map/ppermute | solution.py:513
  96.4 10.6 %collective-permute-start.14 = (f32[24,2048]{1,0:T(8,128)S(1)}, f32[24,2048]{1,0:T(8,128)S(1)}, u32[]{:S(2)}, u32[]{:S(2)}) collective-permute-start(f32[24,2048]{1,0:T(8,128)S(1)} %collective-permute-done.12.far0_ref), channel_id=1, source_target_pairs={{0,4},{2,6},{4,0},{6,2},{1,5},{3,7},{5,1},{7,3},{8,12},{10,14},{12... | collective-permute-start | bytes 589832 | tf_op jit(solution)/shard_map/ppermute | solution.py:513
  96.5 12.7 %collective-permute-start.13 = (f32[24,2048]{1,0:T(8,128)S(1)}, f32[24,2048]{1,0:T(8,128)S(1)}, u32[]{:S(2)}, u32[]{:S(2)}) collective-permute-start(f32[24,2048]{1,0:T(8,128)S(1)} %collective-permute-done.12.far0_ref), channel_id=1, source_target_pairs={{0,2},{2,4},{4,6},{6,0},{1,3},{3,5},{5,7},{7,1},{8,10},{10,12},{12... | collective-permute-start | bytes 589832 | tf_op jit(solution)/shard_map/ppermute | solution.py:513
  109.2 28.0 %copy-start.2 = (bf16[2,256,256]{2,1,0:T(8,128)(2,1)S(1)}, bf16[2,256,256]{2,1,0:T(8,128)(2,1)}, u32[]{:S(2)}) copy-start(bf16[2,256,256]{2,1,0:T(8,128)(2,1)} %constant.14.clone.table_ref) | copy-start | bytes 786436
  111.8 2.8 %collective-permute-start.19 = (f32[4,2048]{1,0:T(4,128)S(1)}, f32[4,2048]{1,0:T(4,128)S(1)}, u32[]{:S(2)}, u32[]{:S(2)}) collective-permute-start(f32[4,2048]{1,0:T(4,128)S(1)} %get-tuple-element.32.spare0_ref), channel_id=1, source_target_pairs={{0,6},{2,0},{4,2},{6,4},{1,7},{3,1},{5,3},{7,5},{8,14},{10,8},{12,... | collective-permute-start | bytes 98312 | tf_op jit(solution)/shard_map/ppermute | solution.py:513
  112.1 4.3 %collective-permute-start.18 = (f32[4,2048]{1,0:T(4,128)S(1)}, f32[4,2048]{1,0:T(4,128)S(1)}, u32[]{:S(2)}, u32[]{:S(2)}) collective-permute-start(f32[4,2048]{1,0:T(4,128)S(1)} %get-tuple-element.32.spare0_ref), channel_id=1, source_target_pairs={{0,4},{2,6},{4,0},{6,2},{1,5},{3,7},{5,1},{7,3},{8,12},{10,14},{12... | collective-permute-start | bytes 98312 | tf_op jit(solution)/shard_map/ppermute | solution.py:513
  112.1 5.3 %collective-permute-start.17 = (f32[4,2048]{1,0:T(4,128)S(1)}, f32[4,2048]{1,0:T(4,128)S(1)}, u32[]{:S(2)}, u32[]{:S(2)}) collective-permute-start(f32[4,2048]{1,0:T(4,128)S(1)} %get-tuple-element.32.spare0_ref), channel_id=1, source_target_pairs={{0,2},{2,4},{4,6},{6,0},{1,3},{3,5},{5,7},{7,1},{8,10},{10,12},{12... | collective-permute-start | bytes 98312 | tf_op jit(solution)/shard_map/ppermute | solution.py:513

commit v3 on v2

--- a/solution.py
+++ b/solution.py
@@ -1,3 +1,5 @@
+import functools
+
 import numpy as np
 import jax
 import jax.numpy as jnp
@@ -17,8 +19,8 @@
 HALO = 2 * POINTS_DEV
 SLOTS = 32
 GROUPS = 4
-CHUNK = 512
-VMEM_BYTES = 8 * 1024 * 1024
+CHUNK = 1024
+VMEM_BYTES = 14 * 1024 * 1024
 F32 = jnp.float32
 BF16 = jnp.bfloat16
 
@@ -142,7 +144,7 @@
 
 
 def rows_kernel(x_ref, out_ref):
-    spread_rows(lambda p, at: x_ref[0, p, :, at : at + LANES], out_ref)
+    spread_rows(lambda p, at: x_ref[0, :, p, at : at + LANES], out_ref)
 
 
 def column_transform(in_ref, table_ref, hold_ref):
@@ -188,7 +190,7 @@
 
 def products_kernel(
     place_ref, e1a_ref, e1b_ref, e1c_ref, e1d_ref, up_ref, keys_ref,
-    kept_ref, spare_ref, raised_ref, stage_ref,
+    kept_ref, spare0_ref, spare1_ref, raised_ref, stage_ref,
 ):
     step = pl.program_id(0)
 
@@ -216,6 +218,8 @@
             eh, el = halves(stage_ref[:, at])
             raised_ref[:, at] = matmul(lhs, jnp.concatenate([eh, el, eh], axis=0))
 
+    spares = (spare0_ref, spare1_ref)
+
     def body(t, carry):
         base = pl.multiple_of(step * CHUNK + t * LANES, LANES)
         here = pl.ds(pl.multiple_of(t * LANES, LANES), LANES)
@@ -227,18 +231,16 @@
                 for d in range(DNUM):
                     term = views[d] * keys_ref[k - 1, d, s, :, here].astype(F32)
                     total = term if total is None else total + term
-                unit = 2 * (k - 1) + s
-                kept_ref[unit, :, here] = total
-                spare_ref[2 * unit : 2 * unit + 2, here] = total[Q_DEV:]
+                kept_ref[s, k - 1, :, here] = total
+                spares[s][2 * k - 2 : 2 * k, here] = total[Q_DEV:]
         return carry
 
     lax.fori_loop(0, CHUNK // LANES, body, 0)
 
 
 def babies_kernel(
-    place_ref, kept_ref, spare0_ref, spare1_ref, spare2_ref, spare3_ref,
-    e0_ref, e1_ref, down_ref, diag_ref,
-    send1_ref, send2_ref, send3_ref, four_ref, zero_ref,
+    poly, place_ref, kept_ref, spare0_ref, spare1_ref, spare2_ref, spare3_ref,
+    evals_ref, down_ref, diag_ref, *out_refs,
 ):
     step = pl.program_id(0)
     columns = down_columns(place_ref, down_ref)
@@ -247,32 +249,26 @@
     def body(t, carry):
         base = pl.multiple_of(step * CHUNK + t * LANES, LANES)
         here = pl.ds(pl.multiple_of(t * LANES, LANES), LANES)
-        own = pl.ds(base + POINTS_DEV, LANES)
-        babies = [(e0_ref[:, own], e1_ref[:, own])]
+        babies = [evals_ref[:, pl.ds(base + POINTS_DEV, LANES)]]
         for k in range(1, BABY):
-            polys = []
-            for s in range(2):
-                unit = 2 * (k - 1) + s
-                rows = lambda m, i: spares[m][2 * unit + i : 2 * unit + i + 1, here]
-                polys.append(lowered(kept_ref[unit, 0:Q_DEV, here], rows, columns))
-            polys[0] = polys[0] + e0_ref[:, pl.ds(base + (8 - k) * SIDE, LANES)]
-            babies.append(tuple(polys))
-        sends = (None, send1_ref, send2_ref, send3_ref)
+            rows = lambda m, i: spares[m][2 * k - 2 + i : 2 * k - 1 + i, here]
+            baby = lowered(kept_ref[0, k - 1, 0:Q_DEV, here], rows, columns)
+            if poly == 0:
+                baby = baby + evals_ref[:, pl.ds(base + (8 - k) * SIDE, LANES)]
+            babies.append(baby)
         for j in range(GIANT):
-            inner = [None, None]
+            inner = None
             for k in range(BABY):
-                factor = diag_ref[j, k, :, here].astype(F32)
-                for s in range(2):
-                    term = factor * babies[k][s]
-                    inner[s] = term if inner[s] is None else inner[s] + term
-            if j % 4 == 0:
-                target = zero_ref if j == 0 else four_ref
-                target[0, :, here] = inner[0]
-                target[1, :, here] = inner[1]
+                term = diag_ref[j, k, :, here].astype(F32) * babies[k]
+                inner = term if inner is None else inner + term
+            if poly == 0:
+                at = 6 * (j % 4)
+                out_refs[j // 4][at : at + 6, here] = inner
+            elif j % 4 == 0:
+                out_refs[3 + j // 4][:, here] = inner
             else:
                 at = 6 * (j // 4)
-                sends[j % 4][at : at + 6, here] = inner[1]
-                sends[j % 4][12 + at : 18 + at, here] = inner[0]
+                out_refs[j % 4 - 1][at : at + 6, here] = inner
         return carry
 
     lax.fori_loop(0, CHUNK // LANES, body, 0)
@@ -294,10 +290,11 @@
         products_kernel,
         grid=(POINTS_DEV // CHUNK,),
         in_specs=[PLACE] + [whole(e) for e in evals] + [whole(up), lanes(7, 3, 2, 8)],
-        out_specs=[lanes(14, 8), lanes(28)],
+        out_specs=[lanes(2, 7, 8), lanes(14), lanes(14)],
         out_shape=[
-            jax.ShapeDtypeStruct((14, 8, POINTS_DEV), F32),
-            jax.ShapeDtypeStruct((28, POINTS_DEV), F32),
+            jax.ShapeDtypeStruct((2, 7, 8, POINTS_DEV), F32),
+            jax.ShapeDtypeStruct((14, POINTS_DEV), F32),
+            jax.ShapeDtypeStruct((14, POINTS_DEV), F32),
         ],
         scratch_shapes=[pltpu.VMEM((24, HALO), F32), pltpu.VMEM((32, HALO), F32)],
         compiler_params=pltpu.CompilerParams(vmem_limit_bytes=VMEM_BYTES),
@@ -305,41 +302,44 @@
     )(place, *evals, up, keys)
 
 
-def babies_call(place, kept, spares, e0, e1, down, diagonals):
-    outs = [(24, POINTS_DEV)] * 3 + [(2, Q_DEV, POINTS_DEV)] * 2
+def babies_call(poly, place, kept, spares, evals, down, diagonals):
+    rows = (24, 24) if poly == 0 else (12, 12, 12, 6, 6)
+    part = pl.BlockSpec((1, 7, 8, CHUNK), lambda i: (poly, 0, 0, i))
     return pl.pallas_call(
-        babies_kernel,
+        functools.partial(babies_kernel, poly),
         grid=(POINTS_DEV // CHUNK,),
-        in_specs=[PLACE, lanes(14, 8)]
-        + [lanes(28)] * 4
-        + [whole(a) for a in (e0, e1, down)]
-        + [lanes(8, 8, Q_DEV)],
-        out_specs=[lanes(24)] * 3 + [lanes(2, Q_DEV)] * 2,
-        out_shape=[jax.ShapeDtypeStruct(s, F32) for s in outs],
+        in_specs=[PLACE, part]
+        + [lanes(14)] * 4
+        + [whole(evals), whole(down), lanes(8, 8, Q_DEV)],
+        out_specs=[lanes(r) for r in rows],
+        out_shape=[jax.ShapeDtypeStruct((r, POINTS_DEV), F32) for r in rows],
         compiler_params=pltpu.CompilerParams(vmem_limit_bytes=VMEM_BYTES),
         cost_estimate=pl.CostEstimate(flops=40000000, bytes_accessed=6000000, transcendentals=0),
-    )(place, kept, *spares, e0, e1, down, diagonals)
-
-
-def sort_kernel(got1_ref, got2_ref, got3_ref, four_ref, near_ref, far_ref, rest_ref):
-    gots = (got1_ref, got2_ref, got3_ref)
-    far_ref[0:6, :] = four_ref[1]
-    rest = four_ref[0]
-    for r, got in enumerate(gots):
+    )(place, kept, *spares, evals, down, diagonals)
+
+
+def sort_kernel(got1_ref, got2_ref, got3_ref, four_ref, near_ref, far_ref):
+    far_ref[0:6, :] = four_ref[...]
+    for r, got in enumerate((got1_ref, got2_ref, got3_ref)):
         near_ref[6 * r : 6 * r + 6, :] = got[0:6, :]
         far_ref[6 + 6 * r : 12 + 6 * r, :] = got[6:12, :]
-        rest = rest + got[18:24, :]
     near_ref[18:24, :] = jnp.zeros((6, POINTS_DEV), F32)
-    rest_ref[...] = rest
+
+
+def pair_sum_kernel(low_ref, high_ref, *out_refs):
+    for r, out_ref in enumerate(out_refs):
+        at = slice(6 * r, 6 * r + 6)
+        out_ref[...] = low_ref[at, :] + high_ref[at, :]
 
 
 def giants_kernel(
-    place_ref, near0_ref, near1_ref, near2_ref, near3_ref,
-    far0_ref, far1_ref, far2_ref, far3_ref, up_ref, keys_ref,
-    zero_ref, got1_ref, got2_ref, got3_ref, moved_ref,
-    total_ref, spare_ref,
-    raised_ref, factor_ref,
+    first, place_ref, part0_ref, part1_ref, part2_ref, part3_ref, up_ref, keys_ref, *refs
 ):
+    before_ref = spare_ref = None
+    if first == 1:
+        total_ref, raised_ref, factor_ref = refs
+    else:
+        before_ref, total_ref, spare_ref, raised_ref, factor_ref = refs
     step = pl.program_id(0)
 
     @pl.when(step == 0)
@@ -364,77 +364,82 @@
             factor_ref[0, at], factor_ref[1, at] = fh.astype(F32), fl.astype(F32)
 
     fh, fl = factor_ref[0].astype(BF16), factor_ref[1].astype(BF16)
-    nears = (near0_ref, near1_ref, near2_ref, near3_ref)
-    fars = (far0_ref, far1_ref, far2_ref, far3_ref)
-    for part, refs in enumerate((nears, fars)):
-        eh, el = halves(jnp.concatenate([ref[...] for ref in refs], axis=0))
-        raised_ref[part] = matmul(fh, eh) + matmul(fh, el) + matmul(fl, eh)
+    parts = (part0_ref, part1_ref, part2_ref, part3_ref)
+    eh, el = halves(jnp.concatenate([ref[...] for ref in parts], axis=0))
+    raised_ref[...] = matmul(fh, eh) + matmul(fh, el) + matmul(fl, eh)
 
     def body(t, carry):
         here = pl.ds(pl.multiple_of(t * LANES, LANES), LANES)
         sums = [None, None]
-        for j in range(1, GIANT):
+        if before_ref is not None:
+            sums = [before_ref[s, :, here] for s in range(2)]
+        for j in range(3 if first == 1 else 4):
             for d in range(DNUM):
-                at = (j - 1 if j < 4 else j - 4) * 24 + d * 8
-                value = raised_ref[j // 4, at : at + 8, here]
+                at = j * 24 + d * 8
+                value = raised_ref[at : at + 8, here]
                 for s in range(2):
-                    term = value * keys_ref[j - 1, d, s, :, here].astype(F32)
-                    sums[s] = term if sums[s] is None else sums[s] + term
-        first = zero_ref[0, :, here] + moved_ref[:, here]
-        for got in (got1_ref, got2_ref, got3_ref):
-            first = first + got[12:18, here]
-        total_ref[0, :, here] = first + sums[0][:Q_DEV]
-        total_ref[1, :, here] = zero_ref[1, :, here] + sums[1][:Q_DEV]
-        spare_ref[0:2, here] = sums[0][Q_DEV:]
-        spare_ref[2:4, here] = sums[1][Q_DEV:]
+                    key = keys_ref[first - 1 + j, d, s, :, here].astype(F32)
+                    sums[s] = value * key if sums[s] is None else sums[s] + value * key
+        if before_ref is None:
+            total_ref[0, :, here], total_ref[1, :, here] = sums
+        else:
+            for s in range(2):
+                total_ref[s, :, here] = sums[s][:Q_DEV]
+                spare_ref[2 * s : 2 * s + 2, here] = sums[s][Q_DEV:]
         return carry
 
     lax.fori_loop(0, CHUNK // LANES, body, 0)
 
 
-def giants_call(place, nears, fars, up, keys, zero, gots, moved):
+def giants_call(first, place, parts, up, keys, before=None):
+    more = [] if before is None else [before]
+    shapes = [(2, 8)] if before is None else [(2, Q_DEV), (4,)]
     return pl.pallas_call(
-        giants_kernel,
+        functools.partial(giants_kernel, first),
         grid=(POINTS_DEV // CHUNK,),
         in_specs=[PLACE]
-        + [lanes(24)] * 8
-        + [whole(up), lanes(7, 3, 2, 8), lanes(2, Q_DEV)]
-        + [lanes(24)] * 3
-        + [lanes(Q_DEV)],
-        out_specs=[lanes(2, Q_DEV), lanes(4)],
-        out_shape=[
-            jax.ShapeDtypeStruct((2, Q_DEV, POINTS_DEV), F32),
-            jax.ShapeDtypeStruct((4, POINTS_DEV), F32),
-        ],
-        scratch_shapes=[pltpu.VMEM((2, 96, CHUNK), F32), pltpu.VMEM((2, 96, 96), F32)],
+        + [lanes(24)] * 4
+        + [whole(up), lanes(7, 3, 2, 8)]
+        + [lanes(2, 8) for _ in more],
+        out_specs=[lanes(*shape) for shape in shapes],
+        out_shape=[jax.ShapeDtypeStruct(shape + (POINTS_DEV,), F32) for shape in shapes],
+        scratch_shapes=[pltpu.VMEM((96, CHUNK), F32), pltpu.VMEM((2, 96, 96), F32)],
         compiler_params=pltpu.CompilerParams(vmem_limit_bytes=VMEM_BYTES),
-        cost_estimate=pl.CostEstimate(flops=40000000, bytes_accessed=4000000, transcendentals=0),
-    )(place, *nears, *fars, up, keys, zero, *gots, moved)
+        cost_estimate=pl.CostEstimate(flops=20000000, bytes_accessed=2000000, transcendentals=0),
+    )(place, *parts, up, keys, *more)
 
 
 def lower_kernel(
-    place_ref, total_ref, spare0_ref, spare1_ref, spare2_ref, spare3_ref, down_ref, out_ref
+    place_ref, total_ref, spare0_ref, spare1_ref, spare2_ref, spare3_ref, down_ref,
+    zero_ref, rest0_ref, rest1_ref, rest2_ref, rest3_ref, out_ref,
 ):
     columns = down_columns(place_ref, down_ref)
     spares = (spare0_ref, spare1_ref, spare2_ref, spare3_ref)
 
     def piece(p, at):
-        rows = lambda m, i: spares[m][2 * p + i : 2 * p + i + 1, at : at + LANES]
-        return lowered(total_ref[p, :, at : at + LANES], rows, columns)
+        here = slice(at, at + LANES)
+        rows = lambda m, i: spares[m][2 * p + i : 2 * p + i + 1, here]
+        value = total_ref[p, :, here]
+        if p == 0:
+            for rest in (rest0_ref, rest1_ref, rest2_ref, rest3_ref):
+                value = value + rest[:, here]
+        else:
+            value = value + zero_ref[:, here]
+        return lowered(value, rows, columns)
 
     spread_rows(piece, out_ref)
 
 
-def lower_call(place, total, spares, down):
+def lower_call(place, total, spares, down, zero, rests):
     out = (SLOTS, Q_DEV, LANES)
     return pl.pallas_call(
         lower_kernel,
-        in_specs=[PLACE] + [pl.BlockSpec(memory_space=pltpu.VMEM)] * 6,
+        in_specs=[PLACE] + [pl.BlockSpec(memory_space=pltpu.VMEM)] * 11,
         out_specs=pl.BlockSpec(memory_space=pltpu.VMEM),
         out_shape=jax.ShapeDtypeStruct(out, F32),
         compiler_params=pltpu.CompilerParams(vmem_limit_bytes=VMEM_BYTES),
         cost_estimate=pl.CostEstimate(flops=1000000, bytes_accessed=400000, transcendentals=0),
-    )(place, total, *spares, down)
+    )(place, total, *spares, down, zero, *rests)
 
 
 def inverse_columns_kernel(in_ref, table_ref, out_ref, hold_ref):
@@ -454,7 +459,7 @@
     result = transform(hold_ref[...].reshape(128, SIDE), table_ref).reshape(16, 8, SIDE)
     for p in range(2):
         for r in range(8):
-            out_ref[0, p, :, r * SIDE : (r + 1) * SIDE] = result[p * 8 + r][:Q_DEV]
+            out_ref[0, :, p, r * SIDE : (r + 1) * SIDE] = result[p * 8 + r][:Q_DEV]
 
 
 def swap(values, axis):
@@ -469,7 +474,8 @@
 def forward(ciphertexts):
     col_fwd, row_fwd, _, _ = dct_constants()
     hold = [pltpu.VMEM((16, 8, SIDE), F32)]
-    sent = call(rows_kernel, [(SLOTS, Q_DEV, LANES)], ciphertexts)
+    parts = jnp.transpose(ciphertexts, (0, 2, 1, 3))
+    sent = call(rows_kernel, [(SLOTS, Q_DEV, LANES)], parts)
     held = swap(sent, "slot")
     sent = call(
         columns_kernel, [(SLOTS, 2, Q_DEV, LANES)], held, col_fwd, scratch=hold, flops=50000000
@@ -498,14 +504,15 @@
         flops=50000000,
     )
     held = swap(sent, "slot")
-    return call(
+    out = call(
         inverse_rows_kernel,
-        [(1, 2, Q_DEV, POINTS_DEV)],
+        [(1, Q_DEV, 2, POINTS_DEV)],
         held,
         row_inv,
         scratch=hold,
         flops=50000000,
     )
+    return jnp.transpose(out, (0, 2, 1, 3))
 
 
 def gathered(block):
@@ -513,24 +520,34 @@
     return [block] + [lax.ppermute(block, "limb", routes[m]) for m in range(1, GROUPS)]
 
 
+def after(values, others):
+    return lax.optimization_barrier((*values, *others))[: len(values)]
+
+
+def together(*groups):
+    flat = lax.optimization_barrier([value for group in groups for value in group])
+    return [[flat.pop(0) for _ in group] for group in groups]
+
+
 def per_device(ciphertexts, diagonals, baby_keys, giant_keys, up, down):
     place = lax.axis_index("limb").astype(jnp.int32).reshape(1)
     e0, e1 = forward(ciphertexts)
-    kept, spare = products_call(place, gathered(e1), up, baby_keys)
-    *sends, four, zero = babies_call(place, kept, gathered(spare), e0, e1, down, diagonals)
+    kept, spare0, spare1 = products_call(place, gathered(e1), up, baby_keys)
+    *sends, zero, four = babies_call(1, place, kept, gathered(spare1), e1, down, diagonals)
+    spares0 = gathered(spare0)
     gots = [shifted(send, r + 1) for r, send in enumerate(sends)]
-    near, far, rest = call(
-        sort_kernel,
-        [(24, POINTS_DEV), (24, POINTS_DEV), (Q_DEV, POINTS_DEV)],
-        *gots,
-        four,
-        flops=10000,
-    )
-    far, rest = shifted(far, 4), shifted(rest, 4)
-    total, spare = giants_call(
-        place, gathered(near), gathered(far), up, giant_keys, zero, gots, rest
-    )
-    return inverse(lower_call(place, total, gathered(spare), down))
+    gots, spares0 = together(gots, spares0)
+    low, high = babies_call(0, place, kept, spares0, e0, down, diagonals)
+    near, far = call(sort_kernel, [(24, POINTS_DEV)] * 2, *gots, four, flops=10000)
+    far = shifted(far, 4)
+    high = shifted(high, 4)
+    nears = gathered(near)
+    (before,) = giants_call(1, place, nears, up, giant_keys)
+    (high,), (before,) = together([high], [before])
+    rests = call(pair_sum_kernel, [(Q_DEV, POINTS_DEV)] * 4, low, high, flops=10000)
+    rests = [rests[0]] + [shifted(rests[r], r) for r in range(1, 4)]
+    total, spare = giants_call(4, place, gathered(far), up, giant_keys, before)
+    return inverse(lower_call(place, total, gathered(spare), down, zero, rests))
 
 
 def solution(mesh):

time: 154 us -> 144 us (0.935)
  waiting for transfers between devices: 54.4 us -> 33.7 us
  starting transfers between devices: 13.4 us -> 24.4 us
  Pallas kernels: 9.59 us -> 11.3 us
    ppermute x15 -> x18, waiting for transfers between devices: 37.3 us -> 17 us  [gathered(): lax.ppermute(block, 'limb', routes[m])]
    ppermute x5 -> x8, starting transfers between devices: 2.72 us -> 9.43 us  [shifted(): return lax.ppermute(block, 'slot', route)]
    ppermute x15 -> x18, starting transfers between devices: 10.7 us -> 14.9 us  [gathered(): lax.ppermute(block, 'limb', routes[m])]
    pallas_call x2 -> x4, Pallas kernels: 4.85 us -> 5.67 us  [the longest x2 2.86 us: babies_call(): pl.pallas_call(functools.partial(babies_kernel, poly), grid=(POINTS_DEV /...]
    pallas_call x6 -> x7, Pallas kernels: 3.07 us -> 3.82 us  [call(): pl.pallas_call(kernel, out_shape=shapes if len(shapes) > 1 else shapes[0]...]
    ppermute x5 -> x8, waiting for transfers between devices: 17.1 us -> 16.8 us  [shifted(): return lax.ppermute(block, 'slot', route)]
    unnamed x18 -> x19, local copies, waits for them, and re-layouts: 3.1 us -> 3.03 us
  transfers between devices with their start and end apart: 20 -> 26, of which waited for: 18 -> 16; matrix products, arithmetic and copies ran while one was open for 1% -> 1% of each run, Pallas kernels for 0% -> 4%
where the time goes in v3:
time: 144 us
  blocking collectives  71.3 us (50%)
  waiting for transfers between devices  33.7 us (23%)
  starting transfers between devices  24.4 us (17%)
  Pallas kernels  11.3 us (8%)
  local copies, waits for them, and re-layouts  3.17 us (2%)
    all_to_all x4, blocking collectives, swap(): return lax.all_to_all(values, axis, split_axis=0, concat_axis=0, tiled=True)  71.3 us
    ppermute x18, waiting for transfers between devices, gathered(): lax.ppermute(block, 'limb', routes[m])  17 us
    ppermute x8, waiting for transfers between devices, shifted(): return lax.ppermute(block, 'slot', route)  16.8 us
    ppermute x18, starting transfers between devices, gathered(): lax.ppermute(block, 'limb', routes[m])  14.9 us
    ppermute x8, starting transfers between devices, shifted(): return lax.ppermute(block, 'slot', route)  9.43 us
    pallas_call x7, Pallas kernels, call(): pl.pallas_call(kernel, out_shape=shapes if len(shapes) > 1 else shapes[0]...  3.82 us
    unnamed x19, local copies, waits for them, and re-layouts  3.03 us
  transfers between devices with their start and end apart: 26, of which 16 were waited for; matrix products, arithmetic and copies ran while one was open for 1% of the time, Pallas kernels for 4%

profile of v3, /device:TPU:1, one launch (start us, length us, event | category | flops | bytes accessed | tf_op | source)
XLA Modules:
  0.0 144.0 jit_solution(2128909182672938125)
XLA Ops:
  0.0 1.0 copy-done.5
  1.0 0.4 shard_map.100
  1.4 23.1 %all_to_all.20.in_ref = f32[32,6,128]{2,1,0:T(8,128)S(1)} all-to-all(f32[32,6,128]{2,1,0:T(8,128)S(1)} %shard_map.100), channel_id=1, replica_groups=mesh['slot'=32,'limb'=4,'ct'=2] {'slot'}, dimensions={0} | all-to-all | bytes 196608 | tf_op jit(solution)/shard_map/all_to_all | solution.py:466
  24.5 0.9 copy-done.4
  25.5 0.8 shard_map.101
  26.4 15.1 %all_to_all.21 = f32[32,2,6,128]{3,1,2,0:T(2,128)S(1)} all-to-all(f32[32,2,6,128]{3,1,2,0:T(2,128)S(1)} %copy.13), channel_id=1, replica_groups=mesh['slot'=32,'limb'=4,'ct'=2] {'slot'}, dimensions={0} | all-to-all | bytes 393216 | tf_op jit(solution)/shard_map/all_to_all | solution.py:466
  41.6 0.6 shard_map.102
  42.2 2.8 %collective-permute-start.2 = (f32[6,4096]{1,0:T(8,128)S(1)}, f32[6,4096]{1,0:T(8,128)S(1)}, u32[]{:S(2)}, u32[]{:S(2)}) collective-permute-start(f32[6,4096]{1,0:T(8,128)S(1)} %get-tuple-element.34.e1a_ref.evals_ref), channel_id=1, source_target_pairs={{0,6},{2,0},{4,2},{6,4},{1,7},{3,1},{5,3},{7,5},{8,14},{10,8},{12,... | collective-permute-start | bytes 294920 | tf_op jit(solution)/shard_map/ppermute | solution.py:520
  45.4 0.7 collective-permute-start
  46.1 4.1 %collective-permute-done.2.e1d_ref = f32[6,4096]{1,0:T(8,128)S(1)} collective-permute-done((f32[6,4096]{1,0:T(8,128)S(1)}, f32[6,4096]{1,0:T(8,128)S(1)}, u32[]{:S(2)}, u32[]{:S(2)}) %collective-permute-start.2) | collective-permute-done | bytes 98336 | tf_op jit(solution)/shard_map/ppermute | solution.py:520
  50.2 0.7 collective-permute-done.1.e1c_ref
  50.9 3.9 %collective-permute-done.e1b_ref = f32[6,4096]{1,0:T(8,128)S(1)} collective-permute-done((f32[6,4096]{1,0:T(8,128)S(1)}, f32[6,4096]{1,0:T(8,128)S(1)}, u32[]{:S(2)}, u32[]{:S(2)}) %collective-permute-start) | collective-permute-done | bytes 98336 | tf_op jit(solution)/shard_map/ppermute | solution.py:520
  54.8 1.4 shard_map.103
  56.3 1.4 collective-permute-start.3
  57.7 2.4 %collective-permute-start.11 = (f32[14,2048]{1,0:T(8,128)S(1)}, f32[14,2048]{1,0:T(8,128)S(1)}, u32[]{:S(2)}, u32[]{:S(2)}) collective-permute-start(f32[14,2048]{1,0:T(8,128)S(1)} %get-tuple-element.46.spare0_ref), channel_id=1, source_target_pairs={{0,6},{2,0},{4,2},{6,4},{1,7},{3,1},{5,3},{7,5},{8,14},{10,8},{12,... | collective-permute-start | bytes 344072 | tf_op jit(solution)/shard_map/ppermute | solution.py:520
  60.1 1.2 collective-permute-start.10
  61.3 0.9 collective-permute-start.9
  62.1 1.0 copy.15.diag_ref
  63.2 3.7 %collective-permute-done.3.spare1_ref = f32[14,2048]{1,0:T(8,128)S(1)} collective-permute-done((f32[14,2048]{1,0:T(8,128)S(1)}, f32[14,2048]{1,0:T(8,128)S(1)}, u32[]{:S(2)}, u32[]{:S(2)}) %collective-permute-start.3) | collective-permute-done | bytes 114720 | tf_op jit(solution)/shard_map/ppermute | solution.py:520
  66.9 1.4 shard_map.104
  68.3 2.1 %collective-permute-start.6 = (f32[12,2048]{1,0:T(8,128)S(1)}, f32[12,2048]{1,0:T(8,128)S(1)}, u32[]{:S(2)}, u32[]{:S(2)}) collective-permute-start(f32[12,2048]{1,0:T(8,128)S(1)} %get-tuple-element.37), channel_id=1, source_target_pairs={{0,8},{8,16},{16,24},{24,32},{32,40},{40,48},{48,56},{56,64},{64,7... | collective-permute-start | bytes 294920 | tf_op jit(solution)/shard_map/ppermute | solution.py:471
  70.4 1.6 %collective-permute-start.7 = (f32[12,2048]{1,0:T(8,128)S(1)}, f32[12,2048]{1,0:T(8,128)S(1)}, u32[]{:S(2)}, u32[]{:S(2)}) collective-permute-start(f32[12,2048]{1,0:T(8,128)S(1)} %get-tuple-element.38), channel_id=1, source_target_pairs={{0,16},{8,24},{16,32},{24,40},{32,48},{40,56},{48,64},{56,72},{64,... | collective-permute-start | bytes 294920 | tf_op jit(solution)/shard_map/ppermute | solution.py:471
  72.1 1.0 collective-permute-done.6.got1_ref
  73.1 7.9 %collective-permute-done.7.got2_ref = f32[12,2048]{1,0:T(8,128)S(1)} collective-permute-done((f32[12,2048]{1,0:T(8,128)S(1)}, f32[12,2048]{1,0:T(8,128)S(1)}, u32[]{:S(2)}, u32[]{:S(2)}) %collective-permute-start.7) | collective-permute-done | bytes 98336 | tf_op jit(solution)/shard_map/ppermute | solution.py:471
  81.0 1.2 collective-permute-done.8.got3_ref
  82.5 0.7 collective-permute-start.18
  83.2 0.8 collective-permute-start.17
  84.0 1.5 %shard_map.106 = (f32[24,2048]{1,0:T(8,128)S(1)}, f32[24,2048]{1,0:T(8,128)S(1)}) custom-call(s32[1]{0:T(128)} %bitcast.place_ref, f32[2,7,8,2048]{3,2,1,0:T(8,128)S(1)} %get-tuple-element.35.kept_ref, f32[14,2048]{1,0:T(8,128)S(1)} %get-tuple-element.46.spare0_ref, f32[14,2048]{1,0:T(8,128)S(1)} %collective-permute-done.9.spare1_ref, ...), custom_call_target="tpu_custom_call" | custom-call | flops 40000000 | bytes 6000000 | tf_op jit(solution)/shard_map/pallas_call | solution.py:308
  85.6 3.4 %collective-permute-done.12.part0_ref = f32[24,2048]{1,0:T(8,128)S(1)} collective-permute-done((f32[24,2048]{1,0:T(8,128)S(1)}, f32[24,2048]{1,0:T(8,128)S(1)}, u32[]{:S(2)}, u32[]{:S(2)}) %collective-permute-start.12) | collective-permute-done | bytes 196640 | tf_op jit(solution)/shard_map/ppermute | solution.py:471
  89.0 0.4 collective-permute-done.19.part3_ref
  89.4 1.3 collective-permute-done.18.part2_ref
  90.7 2.0 %collective-permute-start.13 = (f32[24,2048]{1,0:T(8,128)S(1)}, f32[24,2048]{1,0:T(8,128)S(1)}, u32[]{:S(2)}, u32[]{:S(2)}) collective-permute-start(f32[24,2048]{1,0:T(8,128)S(1)} %collective-permute-done.12.part0_ref), channel_id=1, source_target_pairs={{0,2},{2,4},{4,6},{6,0},{1,3},{3,5},{5,7},{7,1},{8,10},{10,12},{12... | collective-permute-start | bytes 589832 | tf_op jit(solution)/shard_map/ppermute | solution.py:520
  92.7 2.2 %collective-permute-done.17.part1_ref = f32[24,2048]{1,0:T(8,128)S(1)} collective-permute-done((f32[24,2048]{1,0:T(8,128)S(1)}, f32[24,2048]{1,0:T(8,128)S(1)}, u32[]{:S(2)}, u32[]{:S(2)}) %collective-permute-start.17) | collective-permute-done | bytes 196640 | tf_op jit(solution)/shard_map/ppermute | solution.py:520
  94.9 1.3 shard_map.107.refs_0_
  96.4 3.8 %collective-permute-start.23 = (f32[6,2048]{1,0:T(8,128)S(1)}, f32[6,2048]{1,0:T(8,128)S(1)}, u32[]{:S(2)}, u32[]{:S(2)}) collective-permute-start(f32[6,2048]{1,0:T(8,128)S(1)} %get-tuple-element.60), channel_id=1, source_target_pairs={{0,8},{8,16},{16,24},{24,32},{32,40},{40,48},{48,56},{56,64},{64,7... | collective-permute-start | bytes 147464 | tf_op jit(solution)/shard_map/ppermute | solution.py:471
  100.2 1.5 %collective-permute-start.25 = (f32[6,2048]{1,0:T(8,128)S(1)}, f32[6,2048]{1,0:T(8,128)S(1)}, u32[]{:S(2)}, u32[]{:S(2)}) collective-permute-start(f32[6,2048]{1,0:T(8,128)S(1)} %get-tuple-element.62), channel_id=1, source_target_pairs={{0,24},{8,32},{16,40},{24,48},{32,56},{40,64},{48,72},{56,80},{64,... | collective-permute-start | bytes 147464 | tf_op jit(solution)/shard_map/ppermute | solution.py:471
  102.0 1.5 %shard_map.108 = (f32[2,6,2048]{2,1,0:T(8,128)S(1)}, f32[4,2048]{1,0:T(4,128)S(1)}) custom-call(s32[1]{0:T(128)} %bitcast.place_ref, f32[24,2048]{1,0:T(8,128)S(1)} %collective-permute-done.12.part0_ref, f32[24,2048]{1,0:T(8,128)S(1)} %collective-permute-done.13.part1_ref, f32[24,2048]{1,0:T(8,128)S(1)} %collective-permute-done.14.part2_ref, ...), custom_call_target="tpu_custom_call" | custom-call | flops 20000000 | bytes 2000000 | tf_op jit(solution)/shard_map/pallas_call | solution.py:397
  103.4 0.6 collective-permute-start.22
  104.1 0.4 collective-permute-start.21
  104.5 0.5 collective-permute-start.20
  105.0 2.0 %collective-permute-done.24.rest2_ref = f32[6,2048]{1,0:T(8,128)S(1)} collective-permute-done((f32[6,2048]{1,0:T(8,128)S(1)}, f32[6,2048]{1,0:T(8,128)S(1)}, u32[]{:S(2)}, u32[]{:S(2)}) %collective-permute-start.24) | collective-permute-done | bytes 49184 | tf_op jit(solution)/shard_map/ppermute | solution.py:471
  107.0 1.2 collective-permute-done.25.rest3_ref
  108.3 0.4 collective-permute-done.20.spare1_ref
  108.7 0.4 shard_map.110
  109.1 18.9 %all_to_all.22.in_ref = f32[32,6,128]{2,1,0:T(8,128)S(1)} all-to-all(f32[32,6,128]{2,1,0:T(8,128)S(1)} %shard_map.110), channel_id=1, replica_groups=mesh['slot'=32,'limb'=4,'ct'=2] {'slot'}, dimensions={0} | all-to-all | bytes 196608 | tf_op jit(solution)/shard_map/all_to_all | solution.py:466
  128.0 0.8 shard_map.111
  128.8 14.1 %all_to_all.23.in_ref = f32[32,6,128]{2,1,0:T(8,128)S(1)} all-to-all(f32[32,6,128]{2,1,0:T(8,128)S(1)} %shard_map.111), channel_id=1, replica_groups=mesh['slot'=32,'limb'=4,'ct'=2] {'slot'}, dimensions={0} | all-to-all | bytes 196608 | tf_op jit(solution)/shard_map/all_to_all | solution.py:466
  142.9 1.1 shard_map.112
  (42 shorter events, 1.5 us)
Async XLA Ops:
  0.0 41.6 %copy-start.3 = (bf16[2,256,256]{2,1,0:T(8,128)(2,1)S(1)}, bf16[2,256,256]{2,1,0:T(8,128)(2,1)}, u32[]{:S(2)}) copy-start(bf16[2,256,256]{2,1,0:T(8,128)(2,1)} %constant.13.clone.table_ref) | copy-start | bytes 786436
  0.0 54.8 %copy-start.1 = (bf16[7,3,2,8,2048]{4,3,2,1,0:T(8,128)(2,1)S(1)}, bf16[7,3,2,8,2048]{4,3,2,1,0:T(8,128)(2,1)}, u32[]{:S(2)}) copy-start(bf16[7,3,2,8,2048]{4,3,2,1,0:T(8,128)(2,1)} %keys_ref.3) | copy-start | bytes 4128772
  0.0 1.0 copy-start.5
  24.5 1.0 copy-start.4
  25.5 29.3 %copy-start.6 = (f32[8,24]{1,0:T(8,128)S(1)}, f32[8,24]{1,0:T(8,128)}, u32[]{:S(2)}) copy-start(f32[8,24]{1,0:T(8,128)} %up_ref.5) | copy-start | bytes 2308
  42.2 8.0 %collective-permute-start.2 = (f32[6,4096]{1,0:T(8,128)S(1)}, f32[6,4096]{1,0:T(8,128)S(1)}, u32[]{:S(2)}, u32[]{:S(2)}) collective-permute-start(f32[6,4096]{1,0:T(8,128)S(1)} %get-tuple-element.34.e1a_ref.evals_ref), channel_id=1, source_target_pairs={{0,6},{2,0},{4,2},{6,4},{1,7},{3,1},{5,3},{7,5},{8,14},{10,8},{12,... | collective-permute-start | bytes 294920 | tf_op jit(solution)/shard_map/ppermute | solution.py:520
  45.0 5.9 %collective-permute-start.1 = (f32[6,4096]{1,0:T(8,128)S(1)}, f32[6,4096]{1,0:T(8,128)S(1)}, u32[]{:S(2)}, u32[]{:S(2)}) collective-permute-start(f32[6,4096]{1,0:T(8,128)S(1)} %get-tuple-element.34.e1a_ref.evals_ref), channel_id=1, source_target_pairs={{0,4},{2,6},{4,0},{6,2},{1,5},{3,7},{5,1},{7,3},{8,12},{10,14},{12... | collective-permute-start | bytes 294920 | tf_op jit(solution)/shard_map/ppermute | solution.py:520
  45.4 9.4 %collective-permute-start = (f32[6,4096]{1,0:T(8,128)S(1)}, f32[6,4096]{1,0:T(8,128)S(1)}, u32[]{:S(2)}, u32[]{:S(2)}) collective-permute-start(f32[6,4096]{1,0:T(8,128)S(1)} %get-tuple-element.34.e1a_ref.evals_ref), channel_id=1, source_target_pairs={{0,2},{2,4},{4,6},{6,0},{1,3},{3,5},{5,7},{7,1},{8,10},{10,12},{12... | collective-permute-start | bytes 294920 | tf_op jit(solution)/shard_map/ppermute | solution.py:520
  46.1 16.1 %copy-start.8 = (bf16[8,8,6,2048]{3,1,2,0:T(8,128)(2,1)S(1)}, bf16[8,8,6,2048]{3,1,2,0:T(8,128)(2,1)}, u32[]{:S(2)}) copy-start(bf16[8,8,6,2048]{3,1,2,0:T(8,128)(2,1)} %param.11) | copy-start | bytes 4718596
  56.2 5.1 %collective-permute-start.5 = (f32[14,2048]{1,0:T(8,128)S(1)}, f32[14,2048]{1,0:T(8,128)S(1)}, u32[]{:S(2)}, u32[]{:S(2)}) collective-permute-start(f32[14,2048]{1,0:T(8,128)S(1)} %get-tuple-element.36.spare0_ref), channel_id=1, source_target_pairs={{0,6},{2,0},{4,2},{6,4},{1,7},{3,1},{5,3},{7,5},{8,14},{10,8},{12,... | collective-permute-start | bytes 344072 | tf_op jit(solution)/shard_map/ppermute | solution.py:520
  56.2 7.0 %collective-permute-start.4 = (f32[14,2048]{1,0:T(8,128)S(1)}, f32[14,2048]{1,0:T(8,128)S(1)}, u32[]{:S(2)}, u32[]{:S(2)}) collective-permute-start(f32[14,2048]{1,0:T(8,128)S(1)} %get-tuple-element.36.spare0_ref), channel_id=1, source_target_pairs={{0,4},{2,6},{4,0},{6,2},{1,5},{3,7},{5,1},{7,3},{8,12},{10,14},{12... | collective-permute-start | bytes 344072 | tf_op jit(solution)/shard_map/ppermute | solution.py:520
  56.3 10.5 %collective-permute-start.3 = (f32[14,2048]{1,0:T(8,128)S(1)}, f32[14,2048]{1,0:T(8,128)S(1)}, u32[]{:S(2)}, u32[]{:S(2)}) collective-permute-start(f32[14,2048]{1,0:T(8,128)S(1)} %get-tuple-element.36.spare0_ref), channel_id=1, source_target_pairs={{0,2},{2,4},{4,6},{6,0},{1,3},{3,5},{5,7},{7,1},{8,10},{10,12},{12... | collective-permute-start | bytes 344072 | tf_op jit(solution)/shard_map/ppermute | solution.py:520
  57.7 9.2 %copy-start.7 = (f32[6,8]{1,0:T(8,128)S(1)}, f32[6,8]{1,0:T(8,128)}, u32[]{:S(2)}) copy-start(f32[6,8]{1,0:T(8,128)} %down_ref.5) | copy-start | bytes 580
  57.7 14.3 %collective-permute-start.11 = (f32[14,2048]{1,0:T(8,128)S(1)}, f32[14,2048]{1,0:T(8,128)S(1)}, u32[]{:S(2)}, u32[]{:S(2)}) collective-permute-start(f32[14,2048]{1,0:T(8,128)S(1)} %get-tuple-element.46.spare0_ref), channel_id=1, source_target_pairs={{0,6},{2,0},{4,2},{6,4},{1,7},{3,1},{5,3},{7,5},{8,14},{10,8},{12,... | collective-permute-start | bytes 344072 | tf_op jit(solution)/shard_map/ppermute | solution.py:520
  60.1 12.0 %collective-permute-start.10 = (f32[14,2048]{1,0:T(8,128)S(1)}, f32[14,2048]{1,0:T(8,128)S(1)}, u32[]{:S(2)}, u32[]{:S(2)}) collective-permute-start(f32[14,2048]{1,0:T(8,128)S(1)} %get-tuple-element.46.spare0_ref), channel_id=1, source_target_pairs={{0,4},{2,6},{4,0},{6,2},{1,5},{3,7},{5,1},{7,3},{8,12},{10,14},{12... | collective-permute-start | bytes 344072 | tf_op jit(solution)/shard_map/ppermute | solution.py:520
  61.3 10.8 %collective-permute-start.9 = (f32[14,2048]{1,0:T(8,128)S(1)}, f32[14,2048]{1,0:T(8,128)S(1)}, u32[]{:S(2)}, u32[]{:S(2)}) collective-permute-start(f32[14,2048]{1,0:T(8,128)S(1)} %get-tuple-element.46.spare0_ref), channel_id=1, source_target_pairs={{0,2},{2,4},{4,6},{6,0},{1,3},{3,5},{5,7},{7,1},{8,10},{10,12},{12... | collective-permute-start | bytes 344072 | tf_op jit(solution)/shard_map/ppermute | solution.py:520
  68.3 4.8 %collective-permute-start.6 = (f32[12,2048]{1,0:T(8,128)S(1)}, f32[12,2048]{1,0:T(8,128)S(1)}, u32[]{:S(2)}, u32[]{:S(2)}) collective-permute-start(f32[12,2048]{1,0:T(8,128)S(1)} %get-tuple-element.37), channel_id=1, source_target_pairs={{0,8},{8,16},{16,24},{24,32},{32,40},{40,48},{48,56},{56,64},{64,7... | collective-permute-start | bytes 294920 | tf_op jit(solution)/shard_map/ppermute | solution.py:471
  70.4 10.6 %collective-permute-start.7 = (f32[12,2048]{1,0:T(8,128)S(1)}, f32[12,2048]{1,0:T(8,128)S(1)}, u32[]{:S(2)}, u32[]{:S(2)}) collective-permute-start(f32[12,2048]{1,0:T(8,128)S(1)} %get-tuple-element.38), channel_id=1, source_target_pairs={{0,16},{8,24},{16,32},{24,40},{32,48},{40,56},{48,64},{56,72},{64,... | collective-permute-start | bytes 294920 | tf_op jit(solution)/shard_map/ppermute | solution.py:471
  72.0 10.2 %collective-permute-start.8 = (f32[12,2048]{1,0:T(8,128)S(1)}, f32[12,2048]{1,0:T(8,128)S(1)}, u32[]{:S(2)}, u32[]{:S(2)}) collective-permute-start(f32[12,2048]{1,0:T(8,128)S(1)} %get-tuple-element.39), channel_id=1, source_target_pairs={{0,24},{8,32},{16,40},{24,48},{32,56},{40,64},{48,72},{56,80},{64,... | collective-permute-start | bytes 294920 | tf_op jit(solution)/shard_map/ppermute | solution.py:471
  82.3 6.7 %collective-permute-start.12 = (f32[24,2048]{1,0:T(8,128)S(1)}, f32[24,2048]{1,0:T(8,128)S(1)}, u32[]{:S(2)}, u32[]{:S(2)}) collective-permute-start(f32[24,2048]{1,0:T(8,128)S(1)} %get-tuple-element.45), channel_id=1, source_target_pairs={{0,32},{8,40},{16,48},{24,56},{32,64},{40,72},{48,80},{56,88},{64,... | collective-permute-start | bytes 589832 | tf_op jit(solution)/shard_map/ppermute | solution.py:471
  82.4 7.1 %collective-permute-start.19 = (f32[24,2048]{1,0:T(8,128)S(1)}, f32[24,2048]{1,0:T(8,128)S(1)}, u32[]{:S(2)}, u32[]{:S(2)}) collective-permute-start(f32[24,2048]{1,0:T(8,128)S(1)} %get-tuple-element.52.part0_ref), channel_id=1, source_target_pairs={{0,6},{2,0},{4,2},{6,4},{1,7},{3,1},{5,3},{7,5},{8,14},{10,8},{12,... | collective-permute-start | bytes 589832 | tf_op jit(solution)/shard_map/ppermute | solution.py:520
  82.5 8.3 %collective-permute-start.18 = (f32[24,2048]{1,0:T(8,128)S(1)}, f32[24,2048]{1,0:T(8,128)S(1)}, u32[]{:S(2)}, u32[]{:S(2)}) collective-permute-start(f32[24,2048]{1,0:T(8,128)S(1)} %get-tuple-element.52.part0_ref), channel_id=1, source_target_pairs={{0,4},{2,6},{4,0},{6,2},{1,5},{3,7},{5,1},{7,3},{8,12},{10,14},{12... | collective-permute-start | bytes 589832 | tf_op jit(solution)/shard_map/ppermute | solution.py:520
  83.2 11.7 %collective-permute-start.17 = (f32[24,2048]{1,0:T(8,128)S(1)}, f32[24,2048]{1,0:T(8,128)S(1)}, u32[]{:S(2)}, u32[]{:S(2)}) collective-permute-start(f32[24,2048]{1,0:T(8,128)S(1)} %get-tuple-element.52.part0_ref), channel_id=1, source_target_pairs={{0,2},{2,4},{4,6},{6,0},{1,3},{3,5},{5,7},{7,1},{8,10},{10,12},{12... | collective-permute-start | bytes 589832 | tf_op jit(solution)/shard_map/ppermute | solution.py:520
  84.0 11.0 %copy-start = (bf16[7,3,2,8,2048]{4,3,2,1,0:T(8,128)(2,1)S(1)}, bf16[7,3,2,8,2048]{4,3,2,1,0:T(8,128)(2,1)}, u32[]{:S(2)}) copy-start(bf16[7,3,2,8,2048]{4,3,2,1,0:T(8,128)(2,1)} %keys_ref.5) | copy-start | bytes 4128772
  85.4 10.8 %collective-permute-start.16 = (f32[24,2048]{1,0:T(8,128)S(1)}, f32[24,2048]{1,0:T(8,128)S(1)}, u32[]{:S(2)}, u32[]{:S(2)}) collective-permute-start(f32[24,2048]{1,0:T(8,128)S(1)} %get-tuple-element.51), channel_id=1, source_target_pairs={{0,32},{8,40},{16,48},{24,56},{32,64},{40,72},{48,80},{56,88},{64,... | collective-permute-start | bytes 589832 | tf_op jit(solution)/shard_map/ppermute | solution.py:471
  89.0 11.2 %collective-permute-start.15 = (f32[24,2048]{1,0:T(8,128)S(1)}, f32[24,2048]{1,0:T(8,128)S(1)}, u32[]{:S(2)}, u32[]{:S(2)}) collective-permute-start(f32[24,2048]{1,0:T(8,128)S(1)} %collective-permute-done.12.part0_ref), channel_id=1, source_target_pairs={{0,6},{2,0},{4,2},{6,4},{1,7},{3,1},{5,3},{7,5},{8,14},{10,8},{12,... | collective-permute-start | bytes 589832 | tf_op jit(solution)/shard_map/ppermute | solution.py:520
  89.4 12.3 %collective-permute-start.14 = (f32[24,2048]{1,0:T(8,128)S(1)}, f32[24,2048]{1,0:T(8,128)S(1)}, u32[]{:S(2)}, u32[]{:S(2)}) collective-permute-start(f32[24,2048]{1,0:T(8,128)S(1)} %collective-permute-done.12.part0_ref), channel_id=1, source_target_pairs={{0,4},{2,6},{4,0},{6,2},{1,5},{3,7},{5,1},{7,3},{8,12},{10,14},{12... | collective-permute-start | bytes 589832 | tf_op jit(solution)/shard_map/ppermute | solution.py:520
  90.7 11.2 %collective-permute-start.13 = (f32[24,2048]{1,0:T(8,128)S(1)}, f32[24,2048]{1,0:T(8,128)S(1)}, u32[]{:S(2)}, u32[]{:S(2)}) collective-permute-start(f32[24,2048]{1,0:T(8,128)S(1)} %collective-permute-done.12.part0_ref), channel_id=1, source_target_pairs={{0,2},{2,4},{4,6},{6,0},{1,3},{3,5},{5,7},{7,1},{8,10},{10,12},{12... | collective-permute-start | bytes 589832 | tf_op jit(solution)/shard_map/ppermute | solution.py:520
  96.4 8.1 %collective-permute-start.23 = (f32[6,2048]{1,0:T(8,128)S(1)}, f32[6,2048]{1,0:T(8,128)S(1)}, u32[]{:S(2)}, u32[]{:S(2)}) collective-permute-start(f32[6,2048]{1,0:T(8,128)S(1)} %get-tuple-element.60), channel_id=1, source_target_pairs={{0,8},{8,16},{16,24},{24,32},{32,40},{40,48},{48,56},{56,64},{64,7... | collective-permute-start | bytes 147464 | tf_op jit(solution)/shard_map/ppermute | solution.py:471
  100.2 6.8 %collective-permute-start.24 = (f32[6,2048]{1,0:T(8,128)S(1)}, f32[6,2048]{1,0:T(8,128)S(1)}, u32[]{:S(2)}, u32[]{:S(2)}) collective-permute-start(f32[6,2048]{1,0:T(8,128)S(1)} %get-tuple-element.61), channel_id=1, source_target_pairs={{0,16},{8,24},{16,32},{24,40},{32,48},{40,56},{48,64},{56,72},{64,... | collective-permute-start | bytes 147464 | tf_op jit(solution)/shard_map/ppermute | solution.py:471
  100.2 27.8 %copy-start.2 = (bf16[2,256,256]{2,1,0:T(8,128)(2,1)S(1)}, bf16[2,256,256]{2,1,0:T(8,128)(2,1)}, u32[]{:S(2)}) copy-start(bf16[2,256,256]{2,1,0:T(8,128)(2,1)} %constant.14.clone.table_ref) | copy-start | bytes 786436
  100.2 8.0 %collective-permute-start.25 = (f32[6,2048]{1,0:T(8,128)S(1)}, f32[6,2048]{1,0:T(8,128)S(1)}, u32[]{:S(2)}, u32[]{:S(2)}) collective-permute-start(f32[6,2048]{1,0:T(8,128)S(1)} %get-tuple-element.62), channel_id=1, source_target_pairs={{0,24},{8,32},{16,40},{24,48},{32,56},{40,64},{48,72},{56,80},{64,... | collective-permute-start | bytes 147464 | tf_op jit(solution)/shard_map/ppermute | solution.py:471
  103.4 4.8 %collective-permute-start.22 = (f32[4,2048]{1,0:T(4,128)S(1)}, f32[4,2048]{1,0:T(4,128)S(1)}, u32[]{:S(2)}, u32[]{:S(2)}) collective-permute-start(f32[4,2048]{1,0:T(4,128)S(1)} %get-tuple-element.55.spare0_ref), channel_id=1, source_target_pairs={{0,6},{2,0},{4,2},{6,4},{1,7},{3,1},{5,3},{7,5},{8,14},{10,8},{12,... | collective-permute-start | bytes 98312 | tf_op jit(solution)/shard_map/ppermute | solution.py:520
  104.1 4.3 %collective-permute-start.21 = (f32[4,2048]{1,0:T(4,128)S(1)}, f32[4,2048]{1,0:T(4,128)S(1)}, u32[]{:S(2)}, u32[]{:S(2)}) collective-permute-start(f32[4,2048]{1,0:T(4,128)S(1)} %get-tuple-element.55.spare0_ref), channel_id=1, source_target_pairs={{0,4},{2,6},{4,0},{6,2},{1,5},{3,7},{5,1},{7,3},{8,12},{10,14},{12... | collective-permute-start | bytes 98312 | tf_op jit(solution)/shard_map/ppermute | solution.py:520
  104.5 4.2 %collective-permute-start.20 = (f32[4,2048]{1,0:T(4,128)S(1)}, f32[4,2048]{1,0:T(4,128)S(1)}, u32[]{:S(2)}, u32[]{:S(2)}) collective-permute-start(f32[4,2048]{1,0:T(4,128)S(1)} %get-tuple-element.55.spare0_ref), channel_id=1, source_target_pairs={{0,2},{2,4},{4,6},{6,0},{1,3},{3,5},{5,7},{7,1},{8,10},{10,12},{12... | collective-permute-start | bytes 98312 | tf_op jit(solution)/shard_map/ppermute | solution.py:520

commit v4 on v3

--- a/solution.py
+++ b/solution.py
@@ -174,7 +174,7 @@
             out_ref[2 * i, p] = both[:Q_DEV]
 
 
-def evals_kernel(in_ref, table_ref, e0_ref, e1_ref, hold_ref):
+def evals_kernel(in_ref, table_ref, e0_ref, e1_ref, sent_ref, hold_ref):
     hold_ref[...] = jnp.zeros_like(hold_ref)
     for p in range(2):
         for h in range(2):
@@ -186,33 +186,64 @@
         at = slice(row * SIDE, (row + 1) * SIDE)
         e0_ref[:, at] = result[row][:Q_DEV]
         e1_ref[:, at] = result[16 + row][:Q_DEV]
+        for i in range(3):
+            sent_ref[i, :, at] = result[16 + row][2 * i : 2 * i + 2]
+
+
+def factors_kernel(place_ref, up_ref, baby_ref, giant_ref):
+    iota = lambda shape, axis: lax.broadcasted_iota(jnp.int32, shape, axis)
+    up = up_ref[...]
+
+    def spread(held, limb, columns):
+        pick = (iota((24, columns), 0) == limb).astype(F32)
+        wide = exact_matmul(up, pick)
+        digit = limb[0:8] >> 3
+        return [jnp.where(held[0:8] & (digit == d), wide, 0.0) for d in range(DNUM)]
+
+    q = iota((24, 32), 1)
+    used = (q & 7) < Q_DEV
+    limb = jnp.where(used, 6 * group_of(place_ref, q >> 3) + (q & 7), -8)
+    fh, fl = halves(jnp.concatenate(spread(used, limb, 32), axis=0))
+    baby_ref[...] = jnp.concatenate([fh, fh, fl], axis=1).astype(F32)
+    q = iota((24, 96), 1)
+    block = (q >= 24).astype(jnp.int32) + (q >= 48) + (q >= 72)
+    rest = q - 24 * block
+    giant = (rest * 43) >> 8
+    limb = 6 * group_of(place_ref, block) + rest - 6 * giant
+    for j in range(4):
+        at = slice(j * 24, j * 24 + 24)
+        fh, fl = halves(jnp.concatenate(spread(giant == j, limb, 96), axis=0))
+        giant_ref[0, at], giant_ref[1, at] = fh.astype(F32), fl.astype(F32)
+
+
+def factors_call(place, up):
+    return pl.pallas_call(
+        factors_kernel,
+        in_specs=[pl.BlockSpec(memory_space=pltpu.SMEM), pl.BlockSpec(memory_space=pltpu.VMEM)],
+        out_specs=[pl.BlockSpec(memory_space=pltpu.VMEM)] * 2,
+        out_shape=[
+            jax.ShapeDtypeStruct((24, 96), F32),
+            jax.ShapeDtypeStruct((2, 96, 96), F32),
+        ],
+        compiler_params=pltpu.CompilerParams(vmem_limit_bytes=VMEM_BYTES),
+        cost_estimate=pl.CostEstimate(flops=1000000, bytes_accessed=100000, transcendentals=0),
+    )(place, up)
 
 
 def products_kernel(
-    place_ref, e1a_ref, e1b_ref, e1c_ref, e1d_ref, up_ref, keys_ref,
+    e1a_ref, e1b_ref, e1c_ref, e1d_ref, factors_ref, keys_ref,
     kept_ref, spare0_ref, spare1_ref, raised_ref, stage_ref,
 ):
     step = pl.program_id(0)
 
     @pl.when(step == 0)
     def _():
-        iota = lambda shape, axis: lax.broadcasted_iota(jnp.int32, shape, axis)
-
-        def limb(q):
-            group = group_of(place_ref, q >> 3)
-            return jnp.where((q & 7) < Q_DEV, 6 * group + (q & 7), -1)
-
-        pick = (iota((24, 32), 0) == limb(iota((24, 32), 1))).astype(F32)
-        spread = exact_matmul(up_ref[...], pick)
-        digit = limb(iota((8, 32), 1)) >> 3
-        factors = jnp.concatenate(
-            [jnp.where(digit == d, spread, 0.0) for d in range(DNUM)], axis=0
-        )
-        fh, fl = halves(factors)
-        lhs = jnp.concatenate([fh, fh, fl], axis=1)
+        lhs = factors_ref[...].astype(BF16)
         stage_ref[...] = jnp.zeros_like(stage_ref)
-        for m, ref in enumerate((e1a_ref, e1b_ref, e1c_ref, e1d_ref)):
-            stage_ref[8 * m : 8 * m + Q_DEV, :] = ref[...]
+        stage_ref[0:Q_DEV, :] = e1a_ref[...]
+        for m, ref in enumerate((e1b_ref, e1c_ref, e1d_ref), 1):
+            for i in range(3):
+                stage_ref[8 * m + 2 * i : 8 * m + 2 * i + 2, :] = ref[i]
         for part in range(8):
             at = slice(part * 512, (part + 1) * 512)
             eh, el = halves(stage_ref[:, at])
@@ -232,7 +263,7 @@
                     term = views[d] * keys_ref[k - 1, d, s, :, here].astype(F32)
                     total = term if total is None else total + term
                 kept_ref[s, k - 1, :, here] = total
-                spares[s][2 * k - 2 : 2 * k, here] = total[Q_DEV:]
+                spares[s][k - 1, :, here] = total[Q_DEV:]
         return carry
 
     lax.fori_loop(0, CHUNK // LANES, body, 0)
@@ -251,7 +282,7 @@
         here = pl.ds(pl.multiple_of(t * LANES, LANES), LANES)
         babies = [evals_ref[:, pl.ds(base + POINTS_DEV, LANES)]]
         for k in range(1, BABY):
-            rows = lambda m, i: spares[m][2 * k - 2 + i : 2 * k - 1 + i, here]
+            rows = lambda m, i: spares[m][k - 1, i : i + 1, here]
             baby = lowered(kept_ref[0, k - 1, 0:Q_DEV, here], rows, columns)
             if poly == 0:
                 baby = baby + evals_ref[:, pl.ds(base + (8 - k) * SIDE, LANES)]
@@ -267,8 +298,8 @@
             elif j % 4 == 0:
                 out_refs[3 + j // 4][:, here] = inner
             else:
-                at = 6 * (j // 4)
-                out_refs[j % 4 - 1][at : at + 6, here] = inner
+                for i in range(3):
+                    out_refs[j % 4 - 1][3 * (j // 4) + i, :, here] = inner[2 * i : 2 * i + 2]
         return carry
 
     lax.fori_loop(0, CHUNK // LANES, body, 0)
@@ -285,34 +316,34 @@
 PLACE = pl.BlockSpec(memory_space=pltpu.SMEM)
 
 
-def products_call(place, evals, up, keys):
+def products_call(evals, factors, keys):
     return pl.pallas_call(
         products_kernel,
         grid=(POINTS_DEV // CHUNK,),
-        in_specs=[PLACE] + [whole(e) for e in evals] + [whole(up), lanes(7, 3, 2, 8)],
-        out_specs=[lanes(2, 7, 8), lanes(14), lanes(14)],
+        in_specs=[whole(e) for e in evals] + [whole(factors), lanes(7, 3, 2, 8)],
+        out_specs=[lanes(2, 7, 8), lanes(7, 2), lanes(7, 2)],
         out_shape=[
             jax.ShapeDtypeStruct((2, 7, 8, POINTS_DEV), F32),
-            jax.ShapeDtypeStruct((14, POINTS_DEV), F32),
-            jax.ShapeDtypeStruct((14, POINTS_DEV), F32),
+            jax.ShapeDtypeStruct((7, 2, POINTS_DEV), F32),
+            jax.ShapeDtypeStruct((7, 2, POINTS_DEV), F32),
         ],
         scratch_shapes=[pltpu.VMEM((24, HALO), F32), pltpu.VMEM((32, HALO), F32)],
         compiler_params=pltpu.CompilerParams(vmem_limit_bytes=VMEM_BYTES),
         cost_estimate=pl.CostEstimate(flops=40000000, bytes_accessed=4000000, transcendentals=0),
-    )(place, *evals, up, keys)
+    )(*evals, factors, keys)
 
 
 def babies_call(poly, place, kept, spares, evals, down, diagonals):
-    rows = (24, 24) if poly == 0 else (12, 12, 12, 6, 6)
+    rows = [(24,), (24,)] if poly == 0 else [(6, 2)] * 3 + [(6,)] * 2
     part = pl.BlockSpec((1, 7, 8, CHUNK), lambda i: (poly, 0, 0, i))
     return pl.pallas_call(
         functools.partial(babies_kernel, poly),
         grid=(POINTS_DEV // CHUNK,),
         in_specs=[PLACE, part]
-        + [lanes(14)] * 4
+        + [lanes(7, 2)] * 4
         + [whole(evals), whole(down), lanes(8, 8, Q_DEV)],
-        out_specs=[lanes(r) for r in rows],
-        out_shape=[jax.ShapeDtypeStruct((r, POINTS_DEV), F32) for r in rows],
+        out_specs=[lanes(*r) for r in rows],
+        out_shape=[jax.ShapeDtypeStruct((*r, POINTS_DEV), F32) for r in rows],
         compiler_params=pltpu.CompilerParams(vmem_limit_bytes=VMEM_BYTES),
         cost_estimate=pl.CostEstimate(flops=40000000, bytes_accessed=6000000, transcendentals=0),
     )(place, kept, *spares, evals, down, diagonals)
@@ -321,9 +352,9 @@
 def sort_kernel(got1_ref, got2_ref, got3_ref, four_ref, near_ref, far_ref):
     far_ref[0:6, :] = four_ref[...]
     for r, got in enumerate((got1_ref, got2_ref, got3_ref)):
-        near_ref[6 * r : 6 * r + 6, :] = got[0:6, :]
-        far_ref[6 + 6 * r : 12 + 6 * r, :] = got[6:12, :]
-    near_ref[18:24, :] = jnp.zeros((6, POINTS_DEV), F32)
+        for i in range(3):
+            near_ref[3 * r + i] = got[i]
+            far_ref[6 + 6 * r + 2 * i : 8 + 6 * r + 2 * i, :] = got[3 + i]
 
 
 def pair_sum_kernel(low_ref, high_ref, *out_refs):
@@ -333,39 +364,24 @@
 
 
 def giants_kernel(
-    first, place_ref, part0_ref, part1_ref, part2_ref, part3_ref, up_ref, keys_ref, *refs
+    first, part0_ref, part1_ref, part2_ref, part3_ref, factor_ref, keys_ref, *refs
 ):
     before_ref = spare_ref = None
     if first == 1:
-        total_ref, raised_ref, factor_ref = refs
+        total_ref, raised_ref, stage_ref = refs
     else:
-        before_ref, total_ref, spare_ref, raised_ref, factor_ref = refs
-    step = pl.program_id(0)
-
-    @pl.when(step == 0)
-    def _():
-        iota = lambda shape, axis: lax.broadcasted_iota(jnp.int32, shape, axis)
-
-        def source(q):
-            block = (q >= 24).astype(jnp.int32) + (q >= 48) + (q >= 72)
-            rest = q - 24 * block
-            giant = (rest * 43) >> 8
-            return giant, 6 * group_of(place_ref, block) + rest - 6 * giant
-
-        pick = (iota((24, 96), 0) == source(iota((24, 96), 1))[1]).astype(F32)
-        spread = exact_matmul(up_ref[...], pick)
-        held, limb = source(iota((8, 96), 1))
-        for j in range(4):
-            parts = [
-                jnp.where((held == j) & ((limb >> 3) == d), spread, 0.0) for d in range(DNUM)
-            ]
-            at = slice(j * 24, j * 24 + 24)
-            fh, fl = halves(jnp.concatenate(parts, axis=0))
-            factor_ref[0, at], factor_ref[1, at] = fh.astype(F32), fl.astype(F32)
-
+        before_ref, total_ref, spare_ref, raised_ref = refs
     fh, fl = factor_ref[0].astype(BF16), factor_ref[1].astype(BF16)
     parts = (part0_ref, part1_ref, part2_ref, part3_ref)
-    eh, el = halves(jnp.concatenate([ref[...] for ref in parts], axis=0))
+    if first == 1:
+        for m, ref in enumerate(parts):
+            for i in range(9):
+                stage_ref[24 * m + 2 * i : 24 * m + 2 * i + 2, :] = ref[i]
+            stage_ref[24 * m + 18 : 24 * m + 24, :] = jnp.zeros((6, CHUNK), F32)
+        held = stage_ref[...]
+    else:
+        held = jnp.concatenate([ref[...] for ref in parts], axis=0)
+    eh, el = halves(held)
     raised_ref[...] = matmul(fh, eh) + matmul(fh, el) + matmul(fl, eh)
 
     def body(t, carry):
@@ -391,22 +407,21 @@
     lax.fori_loop(0, CHUNK // LANES, body, 0)
 
 
-def giants_call(first, place, parts, up, keys, before=None):
+def giants_call(first, parts, factors, keys, before=None):
     more = [] if before is None else [before]
     shapes = [(2, 8)] if before is None else [(2, Q_DEV), (4,)]
     return pl.pallas_call(
         functools.partial(giants_kernel, first),
         grid=(POINTS_DEV // CHUNK,),
-        in_specs=[PLACE]
-        + [lanes(24)] * 4
-        + [whole(up), lanes(7, 3, 2, 8)]
+        in_specs=[lanes(9, 2) if first == 1 else lanes(24)] * 4
+        + [whole(factors), lanes(7, 3, 2, 8)]
         + [lanes(2, 8) for _ in more],
         out_specs=[lanes(*shape) for shape in shapes],
         out_shape=[jax.ShapeDtypeStruct(shape + (POINTS_DEV,), F32) for shape in shapes],
-        scratch_shapes=[pltpu.VMEM((96, CHUNK), F32), pltpu.VMEM((2, 96, 96), F32)],
+        scratch_shapes=[pltpu.VMEM((96, CHUNK), F32)] * (2 if first == 1 else 1),
         compiler_params=pltpu.CompilerParams(vmem_limit_bytes=VMEM_BYTES),
         cost_estimate=pl.CostEstimate(flops=20000000, bytes_accessed=2000000, transcendentals=0),
-    )(place, *parts, up, keys, *more)
+    )(*parts, factors, keys, *more)
 
 
 def lower_kernel(
@@ -483,7 +498,7 @@
     held = swap(sent, "slot")
     return call(
         evals_kernel,
-        [(Q_DEV, HALO), (Q_DEV, HALO)],
+        [(Q_DEV, HALO), (Q_DEV, HALO), (3, 2, HALO)],
         held,
         row_fwd,
         scratch=[pltpu.VMEM((32, 8, SIDE), F32)],
@@ -531,22 +546,28 @@
 
 def per_device(ciphertexts, diagonals, baby_keys, giant_keys, up, down):
     place = lax.axis_index("limb").astype(jnp.int32).reshape(1)
-    e0, e1 = forward(ciphertexts)
-    kept, spare0, spare1 = products_call(place, gathered(e1), up, baby_keys)
+    e0, e1, sent = forward(ciphertexts)
+    evals = [e1] + gathered(sent)[1:]
+    (late_up,), _ = together([up], [e1])
+    factors, giant_factors = factors_call(place, late_up)
+    kept, spare0, spare1 = products_call(evals, factors, baby_keys)
     *sends, zero, four = babies_call(1, place, kept, gathered(spare1), e1, down, diagonals)
     spares0 = gathered(spare0)
     gots = [shifted(send, r + 1) for r, send in enumerate(sends)]
-    gots, spares0 = together(gots, spares0)
-    low, high = babies_call(0, place, kept, spares0, e0, down, diagonals)
-    near, far = call(sort_kernel, [(24, POINTS_DEV)] * 2, *gots, four, flops=10000)
+    sums = babies_call(0, place, kept, spares0, e0, down, diagonals)
+    low, high = sums
+    gots, (low,) = together(gots, [low])
+    shapes = [(9, 2, POINTS_DEV), (24, POINTS_DEV)]
+    near, far = call(sort_kernel, shapes, *gots, four, flops=10000)
     far = shifted(far, 4)
     high = shifted(high, 4)
     nears = gathered(near)
-    (before,) = giants_call(1, place, nears, up, giant_keys)
+    nears[1:], (far,) = together(nears[1:], [far])
+    (before,) = giants_call(1, nears, giant_factors, giant_keys)
     (high,), (before,) = together([high], [before])
     rests = call(pair_sum_kernel, [(Q_DEV, POINTS_DEV)] * 4, low, high, flops=10000)
     rests = [rests[0]] + [shifted(rests[r], r) for r in range(1, 4)]
-    total, spare = giants_call(4, place, gathered(far), up, giant_keys, before)
+    total, spare = giants_call(4, gathered(far), giant_factors, giant_keys, before)
     return inverse(lower_call(place, total, gathered(spare), down, zero, rests))
 
 

time: 144 us -> 142 us (0.986)
  waiting for transfers between devices: 33.7 us -> 22 us
  starting transfers between devices: 24.4 us -> 35.5 us
  blocking collectives: 71.3 us -> 69.4 us
    ppermute x8, waiting for transfers between devices: 16.8 us -> 6.14 us  [shifted(): return lax.ppermute(block, 'slot', route)]
    ppermute x18, starting transfers between devices: 14.9 us -> 23.7 us  [gathered(): lax.ppermute(block, 'limb', routes[m])]
    ppermute x8, starting transfers between devices: 9.43 us -> 11.9 us  [shifted(): return lax.ppermute(block, 'slot', route)]
    all_to_all x4, blocking collectives: 71.3 us -> 69.4 us  [swap(): return lax.all_to_all(values, axis, split_axis=0, concat_axis=0, tiled=True)]
  transfers between devices with their start and end apart: 26 -> 26, of which waited for: 16 -> 11; matrix products, arithmetic and copies ran while one was open for 1% -> 1% of each run, Pallas kernels for 4% -> 4%
where the time goes in v4:
time: 142 us
  blocking collectives  69.4 us (49%)
  starting transfers between devices  35.5 us (25%)
  waiting for transfers between devices  22 us (15%)
  Pallas kernels  11.4 us (8%)
  local copies, waits for them, and re-layouts  3.05 us (2%)
    all_to_all x4, blocking collectives, swap(): return lax.all_to_all(values, axis, split_axis=0, concat_axis=0, tiled=True)  69.4 us
    ppermute x18, starting transfers between devices, gathered(): lax.ppermute(block, 'limb', routes[m])  23.7 us
    ppermute x18, waiting for transfers between devices, gathered(): lax.ppermute(block, 'limb', routes[m])  15.8 us
    ppermute x8, starting transfers between devices, shifted(): return lax.ppermute(block, 'slot', route)  11.9 us
    ppermute x8, waiting for transfers between devices, shifted(): return lax.ppermute(block, 'slot', route)  6.14 us
    pallas_call x7, Pallas kernels, call(): pl.pallas_call(kernel, out_shape=shapes if len(shapes) > 1 else shapes[0]...  3.81 us
    pallas_call x2, Pallas kernels, babies_call(): pl.pallas_call(functools.partial(babies_kernel, poly), grid=(POINTS_DEV /...  2.97 us
    unnamed x19, local copies, waits for them, and re-layouts  2.91 us
  transfers between devices with their start and end apart: 26, of which 11 were waited for; matrix products, arithmetic and copies ran while one was open for 1% of the time, Pallas kernels for 4%

profile of v4, /device:TPU:1, one launch (start us, length us, event | category | flops | bytes accessed | tf_op | source)
XLA Modules:
  0.0 141.5 jit_solution(14605825805979319515)
XLA Ops:
  0.0 1.0 copy-done.5
  1.0 0.4 shard_map.100
  1.4 23.1 %all_to_all.20.in_ref = f32[32,6,128]{2,1,0:T(8,128)S(1)} all-to-all(f32[32,6,128]{2,1,0:T(8,128)S(1)} %shard_map.100), channel_id=1, replica_groups=mesh['slot'=32,'limb'=4,'ct'=2] {'slot'}, dimensions={0} | all-to-all | bytes 196608 | tf_op jit(solution)/shard_map/all_to_all | solution.py:481
  24.5 0.9 copy-done.4
  25.5 0.8 shard_map.101
  26.4 15.1 %all_to_all.21 = f32[32,2,6,128]{3,1,2,0:T(2,128)S(1)} all-to-all(f32[32,2,6,128]{3,1,2,0:T(2,128)S(1)} %copy.13), channel_id=1, replica_groups=mesh['slot'=32,'limb'=4,'ct'=2] {'slot'}, dimensions={0} | all-to-all | bytes 393216 | tf_op jit(solution)/shard_map/all_to_all | solution.py:481
  41.6 0.6 shard_map.102
  42.2 1.4 collective-permute-start
  43.6 2.6 %collective-permute-start.1 = (f32[3,2,4096]{2,1,0:T(2,128)S(1)}, f32[3,2,4096]{2,1,0:T(2,128)S(1)}, u32[]{:S(2)}, u32[]{:S(2)}) collective-permute-start(f32[3,2,4096]{2,1,0:T(2,128)S(1)} %get-tuple-element.40), channel_id=1, source_target_pairs={{0,4},{2,6},{4,0},{6,2},{1,5},{3,7},{5,1},{7,3},{8,12},{10,14},{12... | collective-permute-start | bytes 294920 | tf_op jit(solution)/shard_map/ppermute | solution.py:535
  46.2 1.1 collective-permute-start.2
  47.3 0.2 shard_map.103
  47.6 3.2 %collective-permute-done.1.e1c_ref = f32[3,2,4096]{2,1,0:T(2,128)S(1)} collective-permute-done((f32[3,2,4096]{2,1,0:T(2,128)S(1)}, f32[3,2,4096]{2,1,0:T(2,128)S(1)}, u32[]{:S(2)}, u32[]{:S(2)}) %collective-permute-start.1) | collective-permute-done | bytes 98336 | tf_op jit(solution)/shard_map/ppermute | solution.py:535
  50.8 1.2 shard_map.104
  52.1 0.5 collective-permute-start.3
  52.6 2.1 %collective-permute-start.4 = (f32[7,2,2048]{2,1,0:T(2,128)S(1)}, f32[7,2,2048]{2,1,0:T(2,128)S(1)}, u32[]{:S(2)}, u32[]{:S(2)}) collective-permute-start(f32[7,2,2048]{2,1,0:T(2,128)S(1)} %get-tuple-element.44.spare0_ref), channel_id=1, source_target_pairs={{0,4},{2,6},{4,0},{6,2},{1,5},{3,7},{5,1},{7,3},{8,12},{10,14},{12... | collective-permute-start | bytes 344072 | tf_op jit(solution)/shard_map/ppermute | solution.py:535
  54.7 1.3 collective-permute-start.5
  56.0 1.2 collective-permute-start.10
  57.2 1.4 collective-permute-start.11
  58.7 0.9 copy.15.diag_ref
  59.6 1.4 %shard_map.105 = (f32[6,2,2048]{2,1,0:T(2,128)S(1)}, f32[6,2,2048]{2,1,0:T(2,128)S(1)}, f32[6,2,2048]{2,1,0:T(2,128)S(1)}, f32[6,2048]{1,0:T(8,128)S(1)}, f32[6,2048]{1,0:T(8,128)S(1)}) custom-call(s32[1]{0:T(128)} %bitcast.place_ref, f32[2,7,8,2048]{3,2,1,0:T(8,128)S(1)} %get-tuple-element.43.kept_ref, f32[7,2,2048]{2,1,0:T(2,128)S(1)} %get-tuple-element.44.spare0_ref, ...), custom_call_target="tpu_custom_call" | custom-call | flops 40000000 | bytes 6000000 | tf_op jit(solution)/shard_map/pallas_call | solution.py:339
  61.1 5.6 %collective-permute-start.6 = (f32[6,2,2048]{2,1,0:T(2,128)S(1)}, f32[6,2,2048]{2,1,0:T(2,128)S(1)}, u32[]{:S(2)}, u32[]{:S(2)}) collective-permute-start(f32[6,2,2048]{2,1,0:T(2,128)S(1)} %get-tuple-element.45), channel_id=1, source_target_pairs={{0,8},{8,16},{16,24},{24,32},{32,40},{40,48},{48,56},{56,64},{64,7... | collective-permute-start | bytes 294920 | tf_op jit(solution)/shard_map/ppermute | solution.py:486
  66.7 2.2 %collective-permute-start.7 = (f32[6,2,2048]{2,1,0:T(2,128)S(1)}, f32[6,2,2048]{2,1,0:T(2,128)S(1)}, u32[]{:S(2)}, u32[]{:S(2)}) collective-permute-start(f32[6,2,2048]{2,1,0:T(2,128)S(1)} %get-tuple-element.46), channel_id=1, source_target_pairs={{0,16},{8,24},{16,32},{24,40},{32,48},{40,56},{48,64},{56,72},{64,... | collective-permute-start | bytes 294920 | tf_op jit(solution)/shard_map/ppermute | solution.py:486
  69.0 1.5 %shard_map.106 = (f32[24,2048]{1,0:T(8,128)S(1)}, f32[24,2048]{1,0:T(8,128)S(1)}) custom-call(s32[1]{0:T(128)} %bitcast.place_ref, f32[2,7,8,2048]{3,2,1,0:T(8,128)S(1)} %get-tuple-element.43.kept_ref, f32[7,2,2048]{2,1,0:T(2,128)S(1)} %get-tuple-element.48.spare0_ref, f32[7,2,2048]{2,1,0:T(2,128)S(1)} %collective-permute-done.9.spare1_ref, ...), custom_call_target="tpu_custom_call" | custom-call | flops 40000000 | bytes 6000000 | tf_op jit(solution)/shard_map/pallas_call | solution.py:339
  70.6 4.0 %collective-permute-done.7.got2_ref = f32[6,2,2048]{2,1,0:T(2,128)S(1)} collective-permute-done((f32[6,2,2048]{2,1,0:T(2,128)S(1)}, f32[6,2,2048]{2,1,0:T(2,128)S(1)}, u32[]{:S(2)}, u32[]{:S(2)}) %collective-permute-start.7) | collective-permute-done | bytes 98336 | tf_op jit(solution)/shard_map/ppermute | solution.py:486
  74.6 2.1 %collective-permute-done.8.got3_ref = f32[6,2,2048]{2,1,0:T(2,128)S(1)} collective-permute-done((f32[6,2,2048]{2,1,0:T(2,128)S(1)}, f32[6,2,2048]{2,1,0:T(2,128)S(1)}, u32[]{:S(2)}, u32[]{:S(2)}) %collective-permute-start.8) | collective-permute-done | bytes 98336 | tf_op jit(solution)/shard_map/ppermute | solution.py:486
  76.8 1.7 %collective-permute-start.12 = (f32[9,2,2048]{2,1,0:T(2,128)S(1)}, f32[9,2,2048]{2,1,0:T(2,128)S(1)}, u32[]{:S(2)}, u32[]{:S(2)}) collective-permute-start(f32[9,2,2048]{2,1,0:T(2,128)S(1)} %get-tuple-element.55.part0_ref), channel_id=1, source_target_pairs={{0,2},{2,4},{4,6},{6,0},{1,3},{3,5},{5,7},{7,1},{8,10},{10,12},{12... | collective-permute-start | bytes 442376 | tf_op jit(solution)/shard_map/ppermute | solution.py:535
  78.5 2.8 %collective-permute-start.13 = (f32[9,2,2048]{2,1,0:T(2,128)S(1)}, f32[9,2,2048]{2,1,0:T(2,128)S(1)}, u32[]{:S(2)}, u32[]{:S(2)}) collective-permute-start(f32[9,2,2048]{2,1,0:T(2,128)S(1)} %get-tuple-element.55.part0_ref), channel_id=1, source_target_pairs={{0,4},{2,6},{4,0},{6,2},{1,5},{3,7},{5,1},{7,3},{8,12},{10,14},{12... | collective-permute-start | bytes 442376 | tf_op jit(solution)/shard_map/ppermute | solution.py:535
  81.3 1.7 %collective-permute-done.12.part1_ref = f32[9,2,2048]{2,1,0:T(2,128)S(1)} collective-permute-done((f32[9,2,2048]{2,1,0:T(2,128)S(1)}, f32[9,2,2048]{2,1,0:T(2,128)S(1)}, u32[]{:S(2)}, u32[]{:S(2)}) %collective-permute-start.12) | collective-permute-done | bytes 147488 | tf_op jit(solution)/shard_map/ppermute | solution.py:535
  83.1 4.2 %collective-permute-done.13.part2_ref = f32[9,2,2048]{2,1,0:T(2,128)S(1)} collective-permute-done((f32[9,2,2048]{2,1,0:T(2,128)S(1)}, f32[9,2,2048]{2,1,0:T(2,128)S(1)}, u32[]{:S(2)}, u32[]{:S(2)}) %collective-permute-start.13) | collective-permute-done | bytes 147488 | tf_op jit(solution)/shard_map/ppermute | solution.py:535
  87.2 1.0 collective-permute-start.16
  88.2 2.4 %collective-permute-start.17 = (f32[24,2048]{1,0:T(8,128)S(1)}, f32[24,2048]{1,0:T(8,128)S(1)}, u32[]{:S(2)}, u32[]{:S(2)}) collective-permute-start(f32[24,2048]{1,0:T(8,128)S(1)} %collective-permute-done.15.part0_ref), channel_id=1, source_target_pairs={{0,4},{2,6},{4,0},{6,2},{1,5},{3,7},{5,1},{7,3},{8,12},{10,14},{12... | collective-permute-start | bytes 589832 | tf_op jit(solution)/shard_map/ppermute | solution.py:535
  90.6 0.3 collective-permute-start.18
  90.9 1.4 shard_map.108.refs_0_
  92.4 1.2 collective-permute-start.23
  93.6 2.6 %collective-permute-start.24 = (f32[6,2048]{1,0:T(8,128)S(1)}, f32[6,2048]{1,0:T(8,128)S(1)}, u32[]{:S(2)}, u32[]{:S(2)}) collective-permute-start(f32[6,2048]{1,0:T(8,128)S(1)} %get-tuple-element.71), channel_id=1, source_target_pairs={{0,16},{8,24},{16,32},{24,40},{32,48},{40,56},{48,64},{56,72},{64,... | collective-permute-start | bytes 147464 | tf_op jit(solution)/shard_map/ppermute | solution.py:486
  96.3 3.2 %collective-permute-done.17.part2_ref = f32[24,2048]{1,0:T(8,128)S(1)} collective-permute-done((f32[24,2048]{1,0:T(8,128)S(1)}, f32[24,2048]{1,0:T(8,128)S(1)}, u32[]{:S(2)}, u32[]{:S(2)}) %collective-permute-start.17) | collective-permute-done | bytes 196640 | tf_op jit(solution)/shard_map/ppermute | solution.py:535
  99.5 0.3 collective-permute-done.18.part3_ref
  99.9 1.3 shard_map.109
  101.2 1.3 collective-permute-start.20
  102.5 2.6 %collective-permute-start.21 = (f32[4,2048]{1,0:T(4,128)S(1)}, f32[4,2048]{1,0:T(4,128)S(1)}, u32[]{:S(2)}, u32[]{:S(2)}) collective-permute-start(f32[4,2048]{1,0:T(4,128)S(1)} %get-tuple-element.65.spare0_ref), channel_id=1, source_target_pairs={{0,4},{2,6},{4,0},{6,2},{1,5},{3,7},{5,1},{7,3},{8,12},{10,14},{12... | collective-permute-start | bytes 98312 | tf_op jit(solution)/shard_map/ppermute | solution.py:535
  105.0 0.2 collective-permute-done.20.spare1_ref
  105.2 1.6 %collective-permute-done.21.spare2_ref = f32[4,2048]{1,0:T(4,128)S(1)} collective-permute-done((f32[4,2048]{1,0:T(4,128)S(1)}, f32[4,2048]{1,0:T(4,128)S(1)}, u32[]{:S(2)}, u32[]{:S(2)}) %collective-permute-start.21) | collective-permute-done | bytes 32800 | tf_op jit(solution)/shard_map/ppermute | solution.py:535
  106.8 1.3 collective-permute-done.22.spare3_ref
  108.1 0.4 shard_map.111
  108.5 17.0 %all_to_all.22.in_ref = f32[32,6,128]{2,1,0:T(8,128)S(1)} all-to-all(f32[32,6,128]{2,1,0:T(8,128)S(1)} %shard_map.111), channel_id=1, replica_groups=mesh['slot'=32,'limb'=4,'ct'=2] {'slot'}, dimensions={0} | all-to-all | bytes 196608 | tf_op jit(solution)/shard_map/all_to_all | solution.py:481
  125.6 0.8 shard_map.112
  126.3 14.1 %all_to_all.23.in_ref = f32[32,6,128]{2,1,0:T(8,128)S(1)} all-to-all(f32[32,6,128]{2,1,0:T(8,128)S(1)} %shard_map.112), channel_id=1, replica_groups=mesh['slot'=32,'limb'=4,'ct'=2] {'slot'}, dimensions={0} | all-to-all | bytes 196608 | tf_op jit(solution)/shard_map/all_to_all | solution.py:481
  140.4 1.1 shard_map.113
  (43 shorter events, 0.6 us)
Async XLA Ops:
  0.0 41.6 %copy-start.3 = (bf16[2,256,256]{2,1,0:T(8,128)(2,1)S(1)}, bf16[2,256,256]{2,1,0:T(8,128)(2,1)}, u32[]{:S(2)}) copy-start(bf16[2,256,256]{2,1,0:T(8,128)(2,1)} %constant.13.clone.table_ref) | copy-start | bytes 786436
  0.0 50.8 %copy-start.1 = (bf16[7,3,2,8,2048]{4,3,2,1,0:T(8,128)(2,1)S(1)}, bf16[7,3,2,8,2048]{4,3,2,1,0:T(8,128)(2,1)}, u32[]{:S(2)}) copy-start(bf16[7,3,2,8,2048]{4,3,2,1,0:T(8,128)(2,1)} %keys_ref.3) | copy-start | bytes 4128772
  0.0 1.0 copy-start.5
  24.5 1.0 copy-start.4
  25.5 21.8 %copy-start.7 = (f32[8,24]{1,0:T(8,128)S(1)}, f32[8,24]{1,0:T(8,128)}, u32[]{:S(2)}) copy-start(f32[8,24]{1,0:T(8,128)} %up_ref) | copy-start | bytes 2308
  42.2 5.4 %collective-permute-start = (f32[3,2,4096]{2,1,0:T(2,128)S(1)}, f32[3,2,4096]{2,1,0:T(2,128)S(1)}, u32[]{:S(2)}, u32[]{:S(2)}) collective-permute-start(f32[3,2,4096]{2,1,0:T(2,128)S(1)} %get-tuple-element.40), channel_id=1, source_target_pairs={{0,2},{2,4},{4,6},{6,0},{1,3},{3,5},{5,7},{7,1},{8,10},{10,12},{12... | collective-permute-start | bytes 294920 | tf_op jit(solution)/shard_map/ppermute | solution.py:535
  43.6 7.2 %collective-permute-start.1 = (f32[3,2,4096]{2,1,0:T(2,128)S(1)}, f32[3,2,4096]{2,1,0:T(2,128)S(1)}, u32[]{:S(2)}, u32[]{:S(2)}) collective-permute-start(f32[3,2,4096]{2,1,0:T(2,128)S(1)} %get-tuple-element.40), channel_id=1, source_target_pairs={{0,4},{2,6},{4,0},{6,2},{1,5},{3,7},{5,1},{7,3},{8,12},{10,14},{12... | collective-permute-start | bytes 294920 | tf_op jit(solution)/shard_map/ppermute | solution.py:535
  46.2 4.6 %collective-permute-start.2 = (f32[3,2,4096]{2,1,0:T(2,128)S(1)}, f32[3,2,4096]{2,1,0:T(2,128)S(1)}, u32[]{:S(2)}, u32[]{:S(2)}) collective-permute-start(f32[3,2,4096]{2,1,0:T(2,128)S(1)} %get-tuple-element.40), channel_id=1, source_target_pairs={{0,6},{2,0},{4,2},{6,4},{1,7},{3,1},{5,3},{7,5},{8,14},{10,8},{12,... | collective-permute-start | bytes 294920 | tf_op jit(solution)/shard_map/ppermute | solution.py:535
  47.3 11.4 %copy-start.8 = (bf16[8,8,6,2048]{3,1,2,0:T(8,128)(2,1)S(1)}, bf16[8,8,6,2048]{3,1,2,0:T(8,128)(2,1)}, u32[]{:S(2)}) copy-start(bf16[8,8,6,2048]{3,1,2,0:T(8,128)(2,1)} %param.11) | copy-start | bytes 4718596
  52.1 6.5 %collective-permute-start.3 = (f32[7,2,2048]{2,1,0:T(2,128)S(1)}, f32[7,2,2048]{2,1,0:T(2,128)S(1)}, u32[]{:S(2)}, u32[]{:S(2)}) collective-permute-start(f32[7,2,2048]{2,1,0:T(2,128)S(1)} %get-tuple-element.44.spare0_ref), channel_id=1, source_target_pairs={{0,2},{2,4},{4,6},{6,0},{1,3},{3,5},{5,7},{7,1},{8,10},{10,12},{12... | collective-permute-start | bytes 344072 | tf_op jit(solution)/shard_map/ppermute | solution.py:535
  52.6 7.0 %collective-permute-start.4 = (f32[7,2,2048]{2,1,0:T(2,128)S(1)}, f32[7,2,2048]{2,1,0:T(2,128)S(1)}, u32[]{:S(2)}, u32[]{:S(2)}) collective-permute-start(f32[7,2,2048]{2,1,0:T(2,128)S(1)} %get-tuple-element.44.spare0_ref), channel_id=1, source_target_pairs={{0,4},{2,6},{4,0},{6,2},{1,5},{3,7},{5,1},{7,3},{8,12},{10,14},{12... | collective-permute-start | bytes 344072 | tf_op jit(solution)/shard_map/ppermute | solution.py:535
  54.7 4.9 %collective-permute-start.5 = (f32[7,2,2048]{2,1,0:T(2,128)S(1)}, f32[7,2,2048]{2,1,0:T(2,128)S(1)}, u32[]{:S(2)}, u32[]{:S(2)}) collective-permute-start(f32[7,2,2048]{2,1,0:T(2,128)S(1)} %get-tuple-element.44.spare0_ref), channel_id=1, source_target_pairs={{0,6},{2,0},{4,2},{6,4},{1,7},{3,1},{5,3},{7,5},{8,14},{10,8},{12,... | collective-permute-start | bytes 344072 | tf_op jit(solution)/shard_map/ppermute | solution.py:535
  56.0 3.6 %copy-start.6 = (f32[6,8]{1,0:T(8,128)S(1)}, f32[6,8]{1,0:T(8,128)}, u32[]{:S(2)}) copy-start(f32[6,8]{1,0:T(8,128)} %down_ref.5) | copy-start | bytes 580
  56.0 12.9 %collective-permute-start.10 = (f32[7,2,2048]{2,1,0:T(2,128)S(1)}, f32[7,2,2048]{2,1,0:T(2,128)S(1)}, u32[]{:S(2)}, u32[]{:S(2)}) collective-permute-start(f32[7,2,2048]{2,1,0:T(2,128)S(1)} %get-tuple-element.48.spare0_ref), channel_id=1, source_target_pairs={{0,4},{2,6},{4,0},{6,2},{1,5},{3,7},{5,1},{7,3},{8,12},{10,14},{12... | collective-permute-start | bytes 344072 | tf_op jit(solution)/shard_map/ppermute | solution.py:535
  57.2 11.8 %collective-permute-start.11 = (f32[7,2,2048]{2,1,0:T(2,128)S(1)}, f32[7,2,2048]{2,1,0:T(2,128)S(1)}, u32[]{:S(2)}, u32[]{:S(2)}) collective-permute-start(f32[7,2,2048]{2,1,0:T(2,128)S(1)} %get-tuple-element.48.spare0_ref), channel_id=1, source_target_pairs={{0,6},{2,0},{4,2},{6,4},{1,7},{3,1},{5,3},{7,5},{8,14},{10,8},{12,... | collective-permute-start | bytes 344072 | tf_op jit(solution)/shard_map/ppermute | solution.py:535
  58.6 10.4 %collective-permute-start.9 = (f32[7,2,2048]{2,1,0:T(2,128)S(1)}, f32[7,2,2048]{2,1,0:T(2,128)S(1)}, u32[]{:S(2)}, u32[]{:S(2)}) collective-permute-start(f32[7,2,2048]{2,1,0:T(2,128)S(1)} %get-tuple-element.48.spare0_ref), channel_id=1, source_target_pairs={{0,2},{2,4},{4,6},{6,0},{1,3},{3,5},{5,7},{7,1},{8,10},{10,12},{12... | collective-permute-start | bytes 344072 | tf_op jit(solution)/shard_map/ppermute | solution.py:535
  61.1 9.5 %collective-permute-start.6 = (f32[6,2,2048]{2,1,0:T(2,128)S(1)}, f32[6,2,2048]{2,1,0:T(2,128)S(1)}, u32[]{:S(2)}, u32[]{:S(2)}) collective-permute-start(f32[6,2,2048]{2,1,0:T(2,128)S(1)} %get-tuple-element.45), channel_id=1, source_target_pairs={{0,8},{8,16},{16,24},{24,32},{32,40},{40,48},{48,56},{56,64},{64,7... | collective-permute-start | bytes 294920 | tf_op jit(solution)/shard_map/ppermute | solution.py:486
  66.7 7.8 %collective-permute-start.7 = (f32[6,2,2048]{2,1,0:T(2,128)S(1)}, f32[6,2,2048]{2,1,0:T(2,128)S(1)}, u32[]{:S(2)}, u32[]{:S(2)}) collective-permute-start(f32[6,2,2048]{2,1,0:T(2,128)S(1)} %get-tuple-element.46), channel_id=1, source_target_pairs={{0,16},{8,24},{16,32},{24,40},{32,48},{40,56},{48,64},{56,72},{64,... | collective-permute-start | bytes 294920 | tf_op jit(solution)/shard_map/ppermute | solution.py:486
  69.0 7.7 %collective-permute-start.8 = (f32[6,2,2048]{2,1,0:T(2,128)S(1)}, f32[6,2,2048]{2,1,0:T(2,128)S(1)}, u32[]{:S(2)}, u32[]{:S(2)}) collective-permute-start(f32[6,2,2048]{2,1,0:T(2,128)S(1)} %get-tuple-element.47), channel_id=1, source_target_pairs={{0,24},{8,32},{16,40},{24,48},{32,56},{40,64},{48,72},{56,80},{64,... | collective-permute-start | bytes 294920 | tf_op jit(solution)/shard_map/ppermute | solution.py:486
  69.0 21.9 %copy-start = (bf16[7,3,2,8,2048]{4,3,2,1,0:T(8,128)(2,1)S(1)}, bf16[7,3,2,8,2048]{4,3,2,1,0:T(8,128)(2,1)}, u32[]{:S(2)}) copy-start(bf16[7,3,2,8,2048]{4,3,2,1,0:T(8,128)(2,1)} %keys_ref.5) | copy-start | bytes 4128772
  76.7 10.5 %collective-permute-start.15 = (f32[24,2048]{1,0:T(8,128)S(1)}, f32[24,2048]{1,0:T(8,128)S(1)}, u32[]{:S(2)}, u32[]{:S(2)}) collective-permute-start(f32[24,2048]{1,0:T(8,128)S(1)} %get-tuple-element.56), channel_id=1, source_target_pairs={{0,32},{8,40},{16,48},{24,56},{32,64},{40,72},{48,80},{56,88},{64,... | collective-permute-start | bytes 589832 | tf_op jit(solution)/shard_map/ppermute | solution.py:486
  76.8 6.2 %collective-permute-start.12 = (f32[9,2,2048]{2,1,0:T(2,128)S(1)}, f32[9,2,2048]{2,1,0:T(2,128)S(1)}, u32[]{:S(2)}, u32[]{:S(2)}) collective-permute-start(f32[9,2,2048]{2,1,0:T(2,128)S(1)} %get-tuple-element.55.part0_ref), channel_id=1, source_target_pairs={{0,2},{2,4},{4,6},{6,0},{1,3},{3,5},{5,7},{7,1},{8,10},{10,12},{12... | collective-permute-start | bytes 442376 | tf_op jit(solution)/shard_map/ppermute | solution.py:535
  78.5 8.7 %collective-permute-start.13 = (f32[9,2,2048]{2,1,0:T(2,128)S(1)}, f32[9,2,2048]{2,1,0:T(2,128)S(1)}, u32[]{:S(2)}, u32[]{:S(2)}) collective-permute-start(f32[9,2,2048]{2,1,0:T(2,128)S(1)} %get-tuple-element.55.part0_ref), channel_id=1, source_target_pairs={{0,4},{2,6},{4,0},{6,2},{1,5},{3,7},{5,1},{7,3},{8,12},{10,14},{12... | collective-permute-start | bytes 442376 | tf_op jit(solution)/shard_map/ppermute | solution.py:535
  81.3 5.9 %collective-permute-start.14 = (f32[9,2,2048]{2,1,0:T(2,128)S(1)}, f32[9,2,2048]{2,1,0:T(2,128)S(1)}, u32[]{:S(2)}, u32[]{:S(2)}) collective-permute-start(f32[9,2,2048]{2,1,0:T(2,128)S(1)} %get-tuple-element.55.part0_ref), channel_id=1, source_target_pairs={{0,6},{2,0},{4,2},{6,4},{1,7},{3,1},{5,3},{7,5},{8,14},{10,8},{12,... | collective-permute-start | bytes 442376 | tf_op jit(solution)/shard_map/ppermute | solution.py:535
  81.3 11.0 %collective-permute-start.19 = (f32[24,2048]{1,0:T(8,128)S(1)}, f32[24,2048]{1,0:T(8,128)S(1)}, u32[]{:S(2)}, u32[]{:S(2)}) collective-permute-start(f32[24,2048]{1,0:T(8,128)S(1)} %get-tuple-element.59), channel_id=1, source_target_pairs={{0,32},{8,40},{16,48},{24,56},{32,64},{40,72},{48,80},{56,88},{64,... | collective-permute-start | bytes 589832 | tf_op jit(solution)/shard_map/ppermute | solution.py:486
  87.2 9.1 %collective-permute-start.16 = (f32[24,2048]{1,0:T(8,128)S(1)}, f32[24,2048]{1,0:T(8,128)S(1)}, u32[]{:S(2)}, u32[]{:S(2)}) collective-permute-start(f32[24,2048]{1,0:T(8,128)S(1)} %collective-permute-done.15.part0_ref), channel_id=1, source_target_pairs={{0,2},{2,4},{4,6},{6,0},{1,3},{3,5},{5,7},{7,1},{8,10},{10,12},{12... | collective-permute-start | bytes 589832 | tf_op jit(solution)/shard_map/ppermute | solution.py:535
  88.2 11.3 %collective-permute-start.17 = (f32[24,2048]{1,0:T(8,128)S(1)}, f32[24,2048]{1,0:T(8,128)S(1)}, u32[]{:S(2)}, u32[]{:S(2)}) collective-permute-start(f32[24,2048]{1,0:T(8,128)S(1)} %collective-permute-done.15.part0_ref), channel_id=1, source_target_pairs={{0,4},{2,6},{4,0},{6,2},{1,5},{3,7},{5,1},{7,3},{8,12},{10,14},{12... | collective-permute-start | bytes 589832 | tf_op jit(solution)/shard_map/ppermute | solution.py:535
  90.6 9.3 %collective-permute-start.18 = (f32[24,2048]{1,0:T(8,128)S(1)}, f32[24,2048]{1,0:T(8,128)S(1)}, u32[]{:S(2)}, u32[]{:S(2)}) collective-permute-start(f32[24,2048]{1,0:T(8,128)S(1)} %collective-permute-done.15.part0_ref), channel_id=1, source_target_pairs={{0,6},{2,0},{4,2},{6,4},{1,7},{3,1},{5,3},{7,5},{8,14},{10,8},{12,... | collective-permute-start | bytes 589832 | tf_op jit(solution)/shard_map/ppermute | solution.py:535
  92.4 12.6 %collective-permute-start.23 = (f32[6,2048]{1,0:T(8,128)S(1)}, f32[6,2048]{1,0:T(8,128)S(1)}, u32[]{:S(2)}, u32[]{:S(2)}) collective-permute-start(f32[6,2048]{1,0:T(8,128)S(1)} %get-tuple-element.70), channel_id=1, source_target_pairs={{0,8},{8,16},{16,24},{24,32},{32,40},{40,48},{48,56},{56,64},{64,7... | collective-permute-start | bytes 147464 | tf_op jit(solution)/shard_map/ppermute | solution.py:486
  93.6 11.4 %collective-permute-start.24 = (f32[6,2048]{1,0:T(8,128)S(1)}, f32[6,2048]{1,0:T(8,128)S(1)}, u32[]{:S(2)}, u32[]{:S(2)}) collective-permute-start(f32[6,2048]{1,0:T(8,128)S(1)} %get-tuple-element.71), channel_id=1, source_target_pairs={{0,16},{8,24},{16,32},{24,40},{32,48},{40,56},{48,64},{56,72},{64,... | collective-permute-start | bytes 147464 | tf_op jit(solution)/shard_map/ppermute | solution.py:486
  96.3 29.3 %copy-start.2 = (bf16[2,256,256]{2,1,0:T(8,128)(2,1)S(1)}, bf16[2,256,256]{2,1,0:T(8,128)(2,1)}, u32[]{:S(2)}) copy-start(bf16[2,256,256]{2,1,0:T(8,128)(2,1)} %constant.14.clone.table_ref) | copy-start | bytes 786436
  96.3 8.7 %collective-permute-start.25 = (f32[6,2048]{1,0:T(8,128)S(1)}, f32[6,2048]{1,0:T(8,128)S(1)}, u32[]{:S(2)}, u32[]{:S(2)}) collective-permute-start(f32[6,2048]{1,0:T(8,128)S(1)} %get-tuple-element.72), channel_id=1, source_target_pairs={{0,24},{8,32},{16,40},{24,48},{32,56},{40,64},{48,72},{56,80},{64,... | collective-permute-start | bytes 147464 | tf_op jit(solution)/shard_map/ppermute | solution.py:486
  101.2 4.1 %collective-permute-start.20 = (f32[4,2048]{1,0:T(4,128)S(1)}, f32[4,2048]{1,0:T(4,128)S(1)}, u32[]{:S(2)}, u32[]{:S(2)}) collective-permute-start(f32[4,2048]{1,0:T(4,128)S(1)} %get-tuple-element.65.spare0_ref), channel_id=1, source_target_pairs={{0,2},{2,4},{4,6},{6,0},{1,3},{3,5},{5,7},{7,1},{8,10},{10,12},{12... | collective-permute-start | bytes 98312 | tf_op jit(solution)/shard_map/ppermute | solution.py:535
  102.5 4.3 %collective-permute-start.21 = (f32[4,2048]{1,0:T(4,128)S(1)}, f32[4,2048]{1,0:T(4,128)S(1)}, u32[]{:S(2)}, u32[]{:S(2)}) collective-permute-start(f32[4,2048]{1,0:T(4,128)S(1)} %get-tuple-element.65.spare0_ref), channel_id=1, source_target_pairs={{0,4},{2,6},{4,0},{6,2},{1,5},{3,7},{5,1},{7,3},{8,12},{10,14},{12... | collective-permute-start | bytes 98312 | tf_op jit(solution)/shard_map/ppermute | solution.py:535
  105.0 3.1 %collective-permute-start.22 = (f32[4,2048]{1,0:T(4,128)S(1)}, f32[4,2048]{1,0:T(4,128)S(1)}, u32[]{:S(2)}, u32[]{:S(2)}) collective-permute-start(f32[4,2048]{1,0:T(4,128)S(1)} %get-tuple-element.65.spare0_ref), channel_id=1, source_target_pairs={{0,6},{2,0},{4,2},{6,4},{1,7},{3,1},{5,3},{7,5},{8,14},{10,8},{12,... | collective-permute-start | bytes 98312 | tf_op jit(solution)/shard_map/ppermute | solution.py:535

commit v5 on v4

--- a/solution.py
+++ b/solution.py
@@ -19,8 +19,8 @@
 HALO = 2 * POINTS_DEV
 SLOTS = 32
 GROUPS = 4
-CHUNK = 1024
-VMEM_BYTES = 14 * 1024 * 1024
+CHUNK = 2048
+VMEM_BYTES = 28 * 1024 * 1024
 F32 = jnp.float32
 BF16 = jnp.bfloat16
 

time: 142 us -> 141 us (level)
  Pallas kernels: 11.4 us -> 9.62 us
  transfers between devices with their start and end apart: 26 -> 26, of which waited for: 11 -> 11; matrix products, arithmetic and copies ran while one was open for 1% -> 1% of each run, Pallas kernels for 4% -> 3%
where the time goes in v5:
time: 141 us
  blocking collectives  69.4 us (49%)
  starting transfers between devices  35.4 us (25%)
  waiting for transfers between devices  22.7 us (16%)
  Pallas kernels  9.62 us (7%)
  local copies, waits for them, and re-layouts  3.17 us (2%)
    all_to_all x4, blocking collectives, swap(): return lax.all_to_all(values, axis, split_axis=0, concat_axis=0, tiled=True)  69.4 us
    ppermute x18, starting transfers between devices, gathered(): lax.ppermute(block, 'limb', routes[m])  23.7 us
    ppermute x18, waiting for transfers between devices, gathered(): lax.ppermute(block, 'limb', routes[m])  16.2 us
    ppermute x8, starting transfers between devices, shifted(): return lax.ppermute(block, 'slot', route)  11.8 us
    ppermute x8, waiting for transfers between devices, shifted(): return lax.ppermute(block, 'slot', route)  6.56 us
    pallas_call x7, Pallas kernels, call(): pl.pallas_call(kernel, out_shape=shapes if len(shapes) > 1 else shapes[0]...  3.81 us
    unnamed x19, local copies, waits for them, and re-layouts  3.04 us
  transfers between devices with their start and end apart: 26, of which 11 were waited for; matrix products, arithmetic and copies ran while one was open for 1% of the time, Pallas kernels for 3%

profile of v5, /device:TPU:1, one launch (start us, length us, event | category | flops | bytes accessed | tf_op | source)
XLA Modules:
  0.0 140.6 jit_solution(8710993823951746704)
XLA Ops:
  0.0 1.0 copy-done.5
  1.0 0.4 shard_map.100
  1.4 23.1 %all_to_all.20.in_ref = f32[32,6,128]{2,1,0:T(8,128)S(1)} all-to-all(f32[32,6,128]{2,1,0:T(8,128)S(1)} %shard_map.100), channel_id=1, replica_groups=mesh['slot'=32,'limb'=4,'ct'=2] {'slot'}, dimensions={0} | all-to-all | bytes 196608 | tf_op jit(solution)/shard_map/all_to_all | solution.py:481
  24.5 0.9 copy-done.4
  25.5 0.8 shard_map.101
  26.4 15.1 %all_to_all.21 = f32[32,2,6,128]{3,1,2,0:T(2,128)S(1)} all-to-all(f32[32,2,6,128]{3,1,2,0:T(2,128)S(1)} %copy.13), channel_id=1, replica_groups=mesh['slot'=32,'limb'=4,'ct'=2] {'slot'}, dimensions={0} | all-to-all | bytes 393216 | tf_op jit(solution)/shard_map/all_to_all | solution.py:481
  41.6 0.6 shard_map.102
  42.2 1.4 collective-permute-start
  43.6 2.6 %collective-permute-start.1 = (f32[3,2,4096]{2,1,0:T(2,128)S(1)}, f32[3,2,4096]{2,1,0:T(2,128)S(1)}, u32[]{:S(2)}, u32[]{:S(2)}) collective-permute-start(f32[3,2,4096]{2,1,0:T(2,128)S(1)} %get-tuple-element.40), channel_id=1, source_target_pairs={{0,4},{2,6},{4,0},{6,2},{1,5},{3,7},{5,1},{7,3},{8,12},{10,14},{12... | collective-permute-start | bytes 294920 | tf_op jit(solution)/shard_map/ppermute | solution.py:535
  46.2 1.1 collective-permute-start.2
  47.3 0.2 shard_map.103
  47.6 3.2 %collective-permute-done.1.e1c_ref = f32[3,2,4096]{2,1,0:T(2,128)S(1)} collective-permute-done((f32[3,2,4096]{2,1,0:T(2,128)S(1)}, f32[3,2,4096]{2,1,0:T(2,128)S(1)}, u32[]{:S(2)}, u32[]{:S(2)}) %collective-permute-start.1) | collective-permute-done | bytes 98336 | tf_op jit(solution)/shard_map/ppermute | solution.py:535
  50.8 1.0 shard_map.104
  51.9 0.5 collective-permute-start.3
  52.4 2.1 %collective-permute-start.4 = (f32[7,2,2048]{2,1,0:T(2,128)S(1)}, f32[7,2,2048]{2,1,0:T(2,128)S(1)}, u32[]{:S(2)}, u32[]{:S(2)}) collective-permute-start(f32[7,2,2048]{2,1,0:T(2,128)S(1)} %get-tuple-element.44.spare0_ref), channel_id=1, source_target_pairs={{0,4},{2,6},{4,0},{6,2},{1,5},{3,7},{5,1},{7,3},{8,12},{10,14},{12... | collective-permute-start | bytes 344072 | tf_op jit(solution)/shard_map/ppermute | solution.py:535
  54.5 1.3 collective-permute-start.5
  55.8 1.2 collective-permute-start.10
  57.0 1.4 collective-permute-start.11
  58.5 1.0 copy.15.diag_ref
  59.5 1.1 shard_map.105
  60.6 5.5 %collective-permute-start.6 = (f32[6,2,2048]{2,1,0:T(2,128)S(1)}, f32[6,2,2048]{2,1,0:T(2,128)S(1)}, u32[]{:S(2)}, u32[]{:S(2)}) collective-permute-start(f32[6,2,2048]{2,1,0:T(2,128)S(1)} %get-tuple-element.45), channel_id=1, source_target_pairs={{0,8},{8,16},{16,24},{24,32},{32,40},{40,48},{48,56},{56,64},{64,7... | collective-permute-start | bytes 294920 | tf_op jit(solution)/shard_map/ppermute | solution.py:486
  66.1 2.2 %collective-permute-start.7 = (f32[6,2,2048]{2,1,0:T(2,128)S(1)}, f32[6,2,2048]{2,1,0:T(2,128)S(1)}, u32[]{:S(2)}, u32[]{:S(2)}) collective-permute-start(f32[6,2,2048]{2,1,0:T(2,128)S(1)} %get-tuple-element.46), channel_id=1, source_target_pairs={{0,16},{8,24},{16,32},{24,40},{32,48},{40,56},{48,64},{56,72},{64,... | collective-permute-start | bytes 294920 | tf_op jit(solution)/shard_map/ppermute | solution.py:486
  68.4 1.1 shard_map.106
  69.6 4.4 %collective-permute-done.7.got2_ref = f32[6,2,2048]{2,1,0:T(2,128)S(1)} collective-permute-done((f32[6,2,2048]{2,1,0:T(2,128)S(1)}, f32[6,2,2048]{2,1,0:T(2,128)S(1)}, u32[]{:S(2)}, u32[]{:S(2)}) %collective-permute-start.7) | collective-permute-done | bytes 98336 | tf_op jit(solution)/shard_map/ppermute | solution.py:486
  74.0 2.1 %collective-permute-done.8.got3_ref = f32[6,2,2048]{2,1,0:T(2,128)S(1)} collective-permute-done((f32[6,2,2048]{2,1,0:T(2,128)S(1)}, f32[6,2,2048]{2,1,0:T(2,128)S(1)}, u32[]{:S(2)}, u32[]{:S(2)}) %collective-permute-start.8) | collective-permute-done | bytes 98336 | tf_op jit(solution)/shard_map/ppermute | solution.py:486
  76.3 1.7 %collective-permute-start.12 = (f32[9,2,2048]{2,1,0:T(2,128)S(1)}, f32[9,2,2048]{2,1,0:T(2,128)S(1)}, u32[]{:S(2)}, u32[]{:S(2)}) collective-permute-start(f32[9,2,2048]{2,1,0:T(2,128)S(1)} %get-tuple-element.55.part0_ref), channel_id=1, source_target_pairs={{0,2},{2,4},{4,6},{6,0},{1,3},{3,5},{5,7},{7,1},{8,10},{10,12},{12... | collective-permute-start | bytes 442376 | tf_op jit(solution)/shard_map/ppermute | solution.py:535
  77.9 2.8 %collective-permute-start.13 = (f32[9,2,2048]{2,1,0:T(2,128)S(1)}, f32[9,2,2048]{2,1,0:T(2,128)S(1)}, u32[]{:S(2)}, u32[]{:S(2)}) collective-permute-start(f32[9,2,2048]{2,1,0:T(2,128)S(1)} %get-tuple-element.55.part0_ref), channel_id=1, source_target_pairs={{0,4},{2,6},{4,0},{6,2},{1,5},{3,7},{5,1},{7,3},{8,12},{10,14},{12... | collective-permute-start | bytes 442376 | tf_op jit(solution)/shard_map/ppermute | solution.py:535
  80.8 1.7 %collective-permute-done.12.part1_ref = f32[9,2,2048]{2,1,0:T(2,128)S(1)} collective-permute-done((f32[9,2,2048]{2,1,0:T(2,128)S(1)}, f32[9,2,2048]{2,1,0:T(2,128)S(1)}, u32[]{:S(2)}, u32[]{:S(2)}) %collective-permute-start.12) | collective-permute-done | bytes 147488 | tf_op jit(solution)/shard_map/ppermute | solution.py:535
  82.5 4.2 %collective-permute-done.13.part2_ref = f32[9,2,2048]{2,1,0:T(2,128)S(1)} collective-permute-done((f32[9,2,2048]{2,1,0:T(2,128)S(1)}, f32[9,2,2048]{2,1,0:T(2,128)S(1)}, u32[]{:S(2)}, u32[]{:S(2)}) %collective-permute-start.13) | collective-permute-done | bytes 147488 | tf_op jit(solution)/shard_map/ppermute | solution.py:535
  86.6 1.0 collective-permute-start.16
  87.6 2.4 %collective-permute-start.17 = (f32[24,2048]{1,0:T(8,128)S(1)}, f32[24,2048]{1,0:T(8,128)S(1)}, u32[]{:S(2)}, u32[]{:S(2)}) collective-permute-start(f32[24,2048]{1,0:T(8,128)S(1)} %collective-permute-done.15.part0_ref), channel_id=1, source_target_pairs={{0,4},{2,6},{4,0},{6,2},{1,5},{3,7},{5,1},{7,3},{8,12},{10,14},{12... | collective-permute-start | bytes 589832 | tf_op jit(solution)/shard_map/ppermute | solution.py:535
  90.0 0.3 collective-permute-start.18
  90.3 1.1 shard_map.108.refs_0_
  91.5 1.3 collective-permute-start.23
  92.7 2.6 %collective-permute-start.24 = (f32[6,2048]{1,0:T(8,128)S(1)}, f32[6,2048]{1,0:T(8,128)S(1)}, u32[]{:S(2)}, u32[]{:S(2)}) collective-permute-start(f32[6,2048]{1,0:T(8,128)S(1)} %get-tuple-element.71), channel_id=1, source_target_pairs={{0,16},{8,24},{16,32},{24,40},{32,48},{40,56},{48,64},{56,72},{64,... | collective-permute-start | bytes 147464 | tf_op jit(solution)/shard_map/ppermute | solution.py:486
  95.4 3.6 %collective-permute-done.17.part2_ref = f32[24,2048]{1,0:T(8,128)S(1)} collective-permute-done((f32[24,2048]{1,0:T(8,128)S(1)}, f32[24,2048]{1,0:T(8,128)S(1)}, u32[]{:S(2)}, u32[]{:S(2)}) %collective-permute-start.17) | collective-permute-done | bytes 196640 | tf_op jit(solution)/shard_map/ppermute | solution.py:535
  99.0 0.3 collective-permute-done.18.part3_ref
  99.3 0.9 shard_map.109
  100.2 1.3 collective-permute-start.20
  101.5 2.6 %collective-permute-start.21 = (f32[4,2048]{1,0:T(4,128)S(1)}, f32[4,2048]{1,0:T(4,128)S(1)}, u32[]{:S(2)}, u32[]{:S(2)}) collective-permute-start(f32[4,2048]{1,0:T(4,128)S(1)} %get-tuple-element.65.spare0_ref), channel_id=1, source_target_pairs={{0,4},{2,6},{4,0},{6,2},{1,5},{3,7},{5,1},{7,3},{8,12},{10,14},{12... | collective-permute-start | bytes 98312 | tf_op jit(solution)/shard_map/ppermute | solution.py:535
  104.1 0.2 collective-permute-done.20.spare1_ref
  104.3 1.6 %collective-permute-done.21.spare2_ref = f32[4,2048]{1,0:T(4,128)S(1)} collective-permute-done((f32[4,2048]{1,0:T(4,128)S(1)}, f32[4,2048]{1,0:T(4,128)S(1)}, u32[]{:S(2)}, u32[]{:S(2)}) %collective-permute-start.21) | collective-permute-done | bytes 32800 | tf_op jit(solution)/shard_map/ppermute | solution.py:535
  105.8 1.3 collective-permute-done.22.spare3_ref
  107.1 0.4 shard_map.111
  107.6 17.0 %all_to_all.22.in_ref = f32[32,6,128]{2,1,0:T(8,128)S(1)} all-to-all(f32[32,6,128]{2,1,0:T(8,128)S(1)} %shard_map.111), channel_id=1, replica_groups=mesh['slot'=32,'limb'=4,'ct'=2] {'slot'}, dimensions={0} | all-to-all | bytes 196608 | tf_op jit(solution)/shard_map/all_to_all | solution.py:481
  124.6 0.8 shard_map.112
  125.4 14.1 %all_to_all.23.in_ref = f32[32,6,128]{2,1,0:T(8,128)S(1)} all-to-all(f32[32,6,128]{2,1,0:T(8,128)S(1)} %shard_map.112), channel_id=1, replica_groups=mesh['slot'=32,'limb'=4,'ct'=2] {'slot'}, dimensions={0} | all-to-all | bytes 196608 | tf_op jit(solution)/shard_map/all_to_all | solution.py:481
  139.4 1.1 shard_map.113
  (43 shorter events, 0.6 us)
Async XLA Ops:
  0.0 41.6 %copy-start.3 = (bf16[2,256,256]{2,1,0:T(8,128)(2,1)S(1)}, bf16[2,256,256]{2,1,0:T(8,128)(2,1)}, u32[]{:S(2)}) copy-start(bf16[2,256,256]{2,1,0:T(8,128)(2,1)} %constant.13.clone.table_ref) | copy-start | bytes 786436
  0.0 50.8 %copy-start.1 = (bf16[7,3,2,8,2048]{4,3,2,1,0:T(8,128)(2,1)S(1)}, bf16[7,3,2,8,2048]{4,3,2,1,0:T(8,128)(2,1)}, u32[]{:S(2)}) copy-start(bf16[7,3,2,8,2048]{4,3,2,1,0:T(8,128)(2,1)} %keys_ref.3) | copy-start | bytes 4128772
  0.0 1.0 copy-start.5
  24.5 1.0 copy-start.4
  25.5 21.8 %copy-start.7 = (f32[8,24]{1,0:T(8,128)S(1)}, f32[8,24]{1,0:T(8,128)}, u32[]{:S(2)}) copy-start(f32[8,24]{1,0:T(8,128)} %up_ref) | copy-start | bytes 2308
  42.2 5.4 %collective-permute-start = (f32[3,2,4096]{2,1,0:T(2,128)S(1)}, f32[3,2,4096]{2,1,0:T(2,128)S(1)}, u32[]{:S(2)}, u32[]{:S(2)}) collective-permute-start(f32[3,2,4096]{2,1,0:T(2,128)S(1)} %get-tuple-element.40), channel_id=1, source_target_pairs={{0,2},{2,4},{4,6},{6,0},{1,3},{3,5},{5,7},{7,1},{8,10},{10,12},{12... | collective-permute-start | bytes 294920 | tf_op jit(solution)/shard_map/ppermute | solution.py:535
  43.6 7.2 %collective-permute-start.1 = (f32[3,2,4096]{2,1,0:T(2,128)S(1)}, f32[3,2,4096]{2,1,0:T(2,128)S(1)}, u32[]{:S(2)}, u32[]{:S(2)}) collective-permute-start(f32[3,2,4096]{2,1,0:T(2,128)S(1)} %get-tuple-element.40), channel_id=1, source_target_pairs={{0,4},{2,6},{4,0},{6,2},{1,5},{3,7},{5,1},{7,3},{8,12},{10,14},{12... | collective-permute-start | bytes 294920 | tf_op jit(solution)/shard_map/ppermute | solution.py:535
  46.2 4.6 %collective-permute-start.2 = (f32[3,2,4096]{2,1,0:T(2,128)S(1)}, f32[3,2,4096]{2,1,0:T(2,128)S(1)}, u32[]{:S(2)}, u32[]{:S(2)}) collective-permute-start(f32[3,2,4096]{2,1,0:T(2,128)S(1)} %get-tuple-element.40), channel_id=1, source_target_pairs={{0,6},{2,0},{4,2},{6,4},{1,7},{3,1},{5,3},{7,5},{8,14},{10,8},{12,... | collective-permute-start | bytes 294920 | tf_op jit(solution)/shard_map/ppermute | solution.py:535
  47.3 11.2 %copy-start.8 = (bf16[8,8,6,2048]{3,1,2,0:T(8,128)(2,1)S(1)}, bf16[8,8,6,2048]{3,1,2,0:T(8,128)(2,1)}, u32[]{:S(2)}) copy-start(bf16[8,8,6,2048]{3,1,2,0:T(8,128)(2,1)} %param.11) | copy-start | bytes 4718596
  51.9 6.5 %collective-permute-start.3 = (f32[7,2,2048]{2,1,0:T(2,128)S(1)}, f32[7,2,2048]{2,1,0:T(2,128)S(1)}, u32[]{:S(2)}, u32[]{:S(2)}) collective-permute-start(f32[7,2,2048]{2,1,0:T(2,128)S(1)} %get-tuple-element.44.spare0_ref), channel_id=1, source_target_pairs={{0,2},{2,4},{4,6},{6,0},{1,3},{3,5},{5,7},{7,1},{8,10},{10,12},{12... | collective-permute-start | bytes 344072 | tf_op jit(solution)/shard_map/ppermute | solution.py:535
  52.4 7.1 %collective-permute-start.4 = (f32[7,2,2048]{2,1,0:T(2,128)S(1)}, f32[7,2,2048]{2,1,0:T(2,128)S(1)}, u32[]{:S(2)}, u32[]{:S(2)}) collective-permute-start(f32[7,2,2048]{2,1,0:T(2,128)S(1)} %get-tuple-element.44.spare0_ref), channel_id=1, source_target_pairs={{0,4},{2,6},{4,0},{6,2},{1,5},{3,7},{5,1},{7,3},{8,12},{10,14},{12... | collective-permute-start | bytes 344072 | tf_op jit(solution)/shard_map/ppermute | solution.py:535
  54.5 5.0 %collective-permute-start.5 = (f32[7,2,2048]{2,1,0:T(2,128)S(1)}, f32[7,2,2048]{2,1,0:T(2,128)S(1)}, u32[]{:S(2)}, u32[]{:S(2)}) collective-permute-start(f32[7,2,2048]{2,1,0:T(2,128)S(1)} %get-tuple-element.44.spare0_ref), channel_id=1, source_target_pairs={{0,6},{2,0},{4,2},{6,4},{1,7},{3,1},{5,3},{7,5},{8,14},{10,8},{12,... | collective-permute-start | bytes 344072 | tf_op jit(solution)/shard_map/ppermute | solution.py:535
  55.8 3.7 %copy-start.6 = (f32[6,8]{1,0:T(8,128)S(1)}, f32[6,8]{1,0:T(8,128)}, u32[]{:S(2)}) copy-start(f32[6,8]{1,0:T(8,128)} %down_ref.5) | copy-start | bytes 580
  55.8 12.6 %collective-permute-start.10 = (f32[7,2,2048]{2,1,0:T(2,128)S(1)}, f32[7,2,2048]{2,1,0:T(2,128)S(1)}, u32[]{:S(2)}, u32[]{:S(2)}) collective-permute-start(f32[7,2,2048]{2,1,0:T(2,128)S(1)} %get-tuple-element.48.spare0_ref), channel_id=1, source_target_pairs={{0,4},{2,6},{4,0},{6,2},{1,5},{3,7},{5,1},{7,3},{8,12},{10,14},{12... | collective-permute-start | bytes 344072 | tf_op jit(solution)/shard_map/ppermute | solution.py:535
  57.0 11.4 %collective-permute-start.11 = (f32[7,2,2048]{2,1,0:T(2,128)S(1)}, f32[7,2,2048]{2,1,0:T(2,128)S(1)}, u32[]{:S(2)}, u32[]{:S(2)}) collective-permute-start(f32[7,2,2048]{2,1,0:T(2,128)S(1)} %get-tuple-element.48.spare0_ref), channel_id=1, source_target_pairs={{0,6},{2,0},{4,2},{6,4},{1,7},{3,1},{5,3},{7,5},{8,14},{10,8},{12,... | collective-permute-start | bytes 344072 | tf_op jit(solution)/shard_map/ppermute | solution.py:535
  58.4 10.0 %collective-permute-start.9 = (f32[7,2,2048]{2,1,0:T(2,128)S(1)}, f32[7,2,2048]{2,1,0:T(2,128)S(1)}, u32[]{:S(2)}, u32[]{:S(2)}) collective-permute-start(f32[7,2,2048]{2,1,0:T(2,128)S(1)} %get-tuple-element.48.spare0_ref), channel_id=1, source_target_pairs={{0,2},{2,4},{4,6},{6,0},{1,3},{3,5},{5,7},{7,1},{8,10},{10,12},{12... | collective-permute-start | bytes 344072 | tf_op jit(solution)/shard_map/ppermute | solution.py:535
  60.6 8.9 %collective-permute-start.6 = (f32[6,2,2048]{2,1,0:T(2,128)S(1)}, f32[6,2,2048]{2,1,0:T(2,128)S(1)}, u32[]{:S(2)}, u32[]{:S(2)}) collective-permute-start(f32[6,2,2048]{2,1,0:T(2,128)S(1)} %get-tuple-element.45), channel_id=1, source_target_pairs={{0,8},{8,16},{16,24},{24,32},{32,40},{40,48},{48,56},{56,64},{64,7... | collective-permute-start | bytes 294920 | tf_op jit(solution)/shard_map/ppermute | solution.py:486
  66.1 7.8 %collective-permute-start.7 = (f32[6,2,2048]{2,1,0:T(2,128)S(1)}, f32[6,2,2048]{2,1,0:T(2,128)S(1)}, u32[]{:S(2)}, u32[]{:S(2)}) collective-permute-start(f32[6,2,2048]{2,1,0:T(2,128)S(1)} %get-tuple-element.46), channel_id=1, source_target_pairs={{0,16},{8,24},{16,32},{24,40},{32,48},{40,56},{48,64},{56,72},{64,... | collective-permute-start | bytes 294920 | tf_op jit(solution)/shard_map/ppermute | solution.py:486
  68.4 7.7 %collective-permute-start.8 = (f32[6,2,2048]{2,1,0:T(2,128)S(1)}, f32[6,2,2048]{2,1,0:T(2,128)S(1)}, u32[]{:S(2)}, u32[]{:S(2)}) collective-permute-start(f32[6,2,2048]{2,1,0:T(2,128)S(1)} %get-tuple-element.47), channel_id=1, source_target_pairs={{0,24},{8,32},{16,40},{24,48},{32,56},{40,64},{48,72},{56,80},{64,... | collective-permute-start | bytes 294920 | tf_op jit(solution)/shard_map/ppermute | solution.py:486
  68.4 21.9 %copy-start = (bf16[7,3,2,8,2048]{4,3,2,1,0:T(8,128)(2,1)S(1)}, bf16[7,3,2,8,2048]{4,3,2,1,0:T(8,128)(2,1)}, u32[]{:S(2)}) copy-start(bf16[7,3,2,8,2048]{4,3,2,1,0:T(8,128)(2,1)} %keys_ref.5) | copy-start | bytes 4128772
  76.2 10.5 %collective-permute-start.15 = (f32[24,2048]{1,0:T(8,128)S(1)}, f32[24,2048]{1,0:T(8,128)S(1)}, u32[]{:S(2)}, u32[]{:S(2)}) collective-permute-start(f32[24,2048]{1,0:T(8,128)S(1)} %get-tuple-element.56), channel_id=1, source_target_pairs={{0,32},{8,40},{16,48},{24,56},{32,64},{40,72},{48,80},{56,88},{64,... | collective-permute-start | bytes 589832 | tf_op jit(solution)/shard_map/ppermute | solution.py:486
  76.3 6.2 %collective-permute-start.12 = (f32[9,2,2048]{2,1,0:T(2,128)S(1)}, f32[9,2,2048]{2,1,0:T(2,128)S(1)}, u32[]{:S(2)}, u32[]{:S(2)}) collective-permute-start(f32[9,2,2048]{2,1,0:T(2,128)S(1)} %get-tuple-element.55.part0_ref), channel_id=1, source_target_pairs={{0,2},{2,4},{4,6},{6,0},{1,3},{3,5},{5,7},{7,1},{8,10},{10,12},{12... | collective-permute-start | bytes 442376 | tf_op jit(solution)/shard_map/ppermute | solution.py:535
  77.9 8.7 %collective-permute-start.13 = (f32[9,2,2048]{2,1,0:T(2,128)S(1)}, f32[9,2,2048]{2,1,0:T(2,128)S(1)}, u32[]{:S(2)}, u32[]{:S(2)}) collective-permute-start(f32[9,2,2048]{2,1,0:T(2,128)S(1)} %get-tuple-element.55.part0_ref), channel_id=1, source_target_pairs={{0,4},{2,6},{4,0},{6,2},{1,5},{3,7},{5,1},{7,3},{8,12},{10,14},{12... | collective-permute-start | bytes 442376 | tf_op jit(solution)/shard_map/ppermute | solution.py:535
  80.8 5.9 %collective-permute-start.14 = (f32[9,2,2048]{2,1,0:T(2,128)S(1)}, f32[9,2,2048]{2,1,0:T(2,128)S(1)}, u32[]{:S(2)}, u32[]{:S(2)}) collective-permute-start(f32[9,2,2048]{2,1,0:T(2,128)S(1)} %get-tuple-element.55.part0_ref), channel_id=1, source_target_pairs={{0,6},{2,0},{4,2},{6,4},{1,7},{3,1},{5,3},{7,5},{8,14},{10,8},{12,... | collective-permute-start | bytes 442376 | tf_op jit(solution)/shard_map/ppermute | solution.py:535
  80.8 10.6 %collective-permute-start.19 = (f32[24,2048]{1,0:T(8,128)S(1)}, f32[24,2048]{1,0:T(8,128)S(1)}, u32[]{:S(2)}, u32[]{:S(2)}) collective-permute-start(f32[24,2048]{1,0:T(8,128)S(1)} %get-tuple-element.59), channel_id=1, source_target_pairs={{0,32},{8,40},{16,48},{24,56},{32,64},{40,72},{48,80},{56,88},{64,... | collective-permute-start | bytes 589832 | tf_op jit(solution)/shard_map/ppermute | solution.py:486
  86.6 8.7 %collective-permute-start.16 = (f32[24,2048]{1,0:T(8,128)S(1)}, f32[24,2048]{1,0:T(8,128)S(1)}, u32[]{:S(2)}, u32[]{:S(2)}) collective-permute-start(f32[24,2048]{1,0:T(8,128)S(1)} %collective-permute-done.15.part0_ref), channel_id=1, source_target_pairs={{0,2},{2,4},{4,6},{6,0},{1,3},{3,5},{5,7},{7,1},{8,10},{10,12},{12... | collective-permute-start | bytes 589832 | tf_op jit(solution)/shard_map/ppermute | solution.py:535
  87.6 11.3 %collective-permute-start.17 = (f32[24,2048]{1,0:T(8,128)S(1)}, f32[24,2048]{1,0:T(8,128)S(1)}, u32[]{:S(2)}, u32[]{:S(2)}) collective-permute-start(f32[24,2048]{1,0:T(8,128)S(1)} %collective-permute-done.15.part0_ref), channel_id=1, source_target_pairs={{0,4},{2,6},{4,0},{6,2},{1,5},{3,7},{5,1},{7,3},{8,12},{10,14},{12... | collective-permute-start | bytes 589832 | tf_op jit(solution)/shard_map/ppermute | solution.py:535
  90.0 9.3 %collective-permute-start.18 = (f32[24,2048]{1,0:T(8,128)S(1)}, f32[24,2048]{1,0:T(8,128)S(1)}, u32[]{:S(2)}, u32[]{:S(2)}) collective-permute-start(f32[24,2048]{1,0:T(8,128)S(1)} %collective-permute-done.15.part0_ref), channel_id=1, source_target_pairs={{0,6},{2,0},{4,2},{6,4},{1,7},{3,1},{5,3},{7,5},{8,14},{10,8},{12,... | collective-permute-start | bytes 589832 | tf_op jit(solution)/shard_map/ppermute | solution.py:535
  91.5 12.6 %collective-permute-start.23 = (f32[6,2048]{1,0:T(8,128)S(1)}, f32[6,2048]{1,0:T(8,128)S(1)}, u32[]{:S(2)}, u32[]{:S(2)}) collective-permute-start(f32[6,2048]{1,0:T(8,128)S(1)} %get-tuple-element.70), channel_id=1, source_target_pairs={{0,8},{8,16},{16,24},{24,32},{32,40},{40,48},{48,56},{56,64},{64,7... | collective-permute-start | bytes 147464 | tf_op jit(solution)/shard_map/ppermute | solution.py:486
  92.7 11.3 %collective-permute-start.24 = (f32[6,2048]{1,0:T(8,128)S(1)}, f32[6,2048]{1,0:T(8,128)S(1)}, u32[]{:S(2)}, u32[]{:S(2)}) collective-permute-start(f32[6,2048]{1,0:T(8,128)S(1)} %get-tuple-element.71), channel_id=1, source_target_pairs={{0,16},{8,24},{16,32},{24,40},{32,48},{40,56},{48,64},{56,72},{64,... | collective-permute-start | bytes 147464 | tf_op jit(solution)/shard_map/ppermute | solution.py:486
  95.4 29.2 %copy-start.2 = (bf16[2,256,256]{2,1,0:T(8,128)(2,1)S(1)}, bf16[2,256,256]{2,1,0:T(8,128)(2,1)}, u32[]{:S(2)}) copy-start(bf16[2,256,256]{2,1,0:T(8,128)(2,1)} %constant.14.clone.table_ref) | copy-start | bytes 786436
  95.4 8.7 %collective-permute-start.25 = (f32[6,2048]{1,0:T(8,128)S(1)}, f32[6,2048]{1,0:T(8,128)S(1)}, u32[]{:S(2)}, u32[]{:S(2)}) collective-permute-start(f32[6,2048]{1,0:T(8,128)S(1)} %get-tuple-element.72), channel_id=1, source_target_pairs={{0,24},{8,32},{16,40},{24,48},{32,56},{40,64},{48,72},{56,80},{64,... | collective-permute-start | bytes 147464 | tf_op jit(solution)/shard_map/ppermute | solution.py:486
  100.2 4.1 %collective-permute-start.20 = (f32[4,2048]{1,0:T(4,128)S(1)}, f32[4,2048]{1,0:T(4,128)S(1)}, u32[]{:S(2)}, u32[]{:S(2)}) collective-permute-start(f32[4,2048]{1,0:T(4,128)S(1)} %get-tuple-element.65.spare0_ref), channel_id=1, source_target_pairs={{0,2},{2,4},{4,6},{6,0},{1,3},{3,5},{5,7},{7,1},{8,10},{10,12},{12... | collective-permute-start | bytes 98312 | tf_op jit(solution)/shard_map/ppermute | solution.py:535
  101.5 4.3 %collective-permute-start.21 = (f32[4,2048]{1,0:T(4,128)S(1)}, f32[4,2048]{1,0:T(4,128)S(1)}, u32[]{:S(2)}, u32[]{:S(2)}) collective-permute-start(f32[4,2048]{1,0:T(4,128)S(1)} %get-tuple-element.65.spare0_ref), channel_id=1, source_target_pairs={{0,4},{2,6},{4,0},{6,2},{1,5},{3,7},{5,1},{7,3},{8,12},{10,14},{12... | collective-permute-start | bytes 98312 | tf_op jit(solution)/shard_map/ppermute | solution.py:535
  104.1 3.1 %collective-permute-start.22 = (f32[4,2048]{1,0:T(4,128)S(1)}, f32[4,2048]{1,0:T(4,128)S(1)}, u32[]{:S(2)}, u32[]{:S(2)}) collective-permute-start(f32[4,2048]{1,0:T(4,128)S(1)} %get-tuple-element.65.spare0_ref), channel_id=1, source_target_pairs={{0,6},{2,0},{4,2},{6,4},{1,7},{3,1},{5,3},{7,5},{8,14},{10,8},{12,... | collective-permute-start | bytes 98312 | tf_op jit(solution)/shard_map/ppermute | solution.py:535

commit v6 on v5

--- a/solution.py
+++ b/solution.py
@@ -174,20 +174,20 @@
             out_ref[2 * i, p] = both[:Q_DEV]
 
 
-def evals_kernel(in_ref, table_ref, e0_ref, e1_ref, sent_ref, hold_ref):
+def evals_kernel(poly, in_ref, table_ref, *refs):
+    *out_refs, hold_ref = refs
     hold_ref[...] = jnp.zeros_like(hold_ref)
-    for p in range(2):
-        for h in range(2):
-            parts = exchange([in_ref[h * 16 + c, p] for c in range(16)], (3, 2, 1, 0))
-            for row, part in enumerate(parts):
-                hold_ref[p * 16 + row, 0:Q_DEV, h * LANES : (h + 1) * LANES] = part
-    result = transform(hold_ref[...].reshape(256, SIDE), table_ref).reshape(32, 8, SIDE)
+    for h in range(2):
+        parts = exchange([in_ref[h * 16 + c, poly] for c in range(16)], (3, 2, 1, 0))
+        for row, part in enumerate(parts):
+            hold_ref[row, 0:Q_DEV, h * LANES : (h + 1) * LANES] = part
+    result = transform(hold_ref[...].reshape(128, SIDE), table_ref).reshape(16, 8, SIDE)
     for row in range(16):
         at = slice(row * SIDE, (row + 1) * SIDE)
-        e0_ref[:, at] = result[row][:Q_DEV]
-        e1_ref[:, at] = result[16 + row][:Q_DEV]
-        for i in range(3):
-            sent_ref[i, :, at] = result[16 + row][2 * i : 2 * i + 2]
+        out_refs[0][:, at] = result[row][:Q_DEV]
+        if poly == 1:
+            for i in range(3):
+                out_refs[1][i, :, at] = result[row][2 * i : 2 * i + 2]
 
 
 def factors_kernel(place_ref, up_ref, baby_ref, giant_ref):
@@ -496,14 +496,19 @@
         columns_kernel, [(SLOTS, 2, Q_DEV, LANES)], held, col_fwd, scratch=hold, flops=50000000
     )
     held = swap(sent, "slot")
-    return call(
-        evals_kernel,
-        [(Q_DEV, HALO), (Q_DEV, HALO), (3, 2, HALO)],
-        held,
-        row_fwd,
-        scratch=[pltpu.VMEM((32, 8, SIDE), F32)],
-        flops=100000000,
-    )
+    shapes = [[(Q_DEV, HALO)], [(Q_DEV, HALO), (3, 2, HALO)]]
+    e0, second = [
+        call(
+            functools.partial(evals_kernel, poly),
+            shapes[poly],
+            held,
+            row_fwd,
+            scratch=hold,
+            flops=50000000,
+        )
+        for poly in range(2)
+    ]
+    return e0, *second
 
 
 def inverse(sent):

time: 141 us -> 141 us (level)
    pallas_call x7 -> x8, Pallas kernels: 3.81 us -> 4.15 us  [call(): pl.pallas_call(kernel, out_shape=shapes if len(shapes) > 1 else shapes[0]...]
where the time goes in v6:
time: 141 us; the launch traced here: 140 us
  blocking collectives  69.4 us (49%)
  starting transfers between devices  35.4 us (25%)
  waiting for transfers between devices  22.2 us (16%)
  Pallas kernels  9.96 us (7%)
  local copies, waits for them, and re-layouts  3.17 us (2%)
    all_to_all x4, blocking collectives, swap(): return lax.all_to_all(values, axis, split_axis=0, concat_axis=0, tiled=True)  69.4 us
    ppermute x18, starting transfers between devices, gathered(): lax.ppermute(block, 'limb', routes[m])  23.7 us
    ppermute x18, waiting for transfers between devices, gathered(): lax.ppermute(block, 'limb', routes[m])  16.2 us
    ppermute x8, starting transfers between devices, shifted(): return lax.ppermute(block, 'slot', route)  11.8 us
    ppermute x8, waiting for transfers between devices, shifted(): return lax.ppermute(block, 'slot', route)  6.07 us
    pallas_call x8, Pallas kernels, call(): pl.pallas_call(kernel, out_shape=shapes if len(shapes) > 1 else shapes[0]...  4.15 us
    unnamed x19, local copies, waits for them, and re-layouts  3.04 us
  transfers between devices with their start and end apart: 26, of which 11 were waited for; matrix products, arithmetic and copies ran while one was open for 1% of the time, Pallas kernels for 3%

profile of v6, /device:TPU:1, one launch (start us, length us, event | category | flops | bytes accessed | tf_op | source)
XLA Modules:
  0.0 140.4 jit_solution(177000125637878435)
XLA Ops:
  0.0 1.0 copy-done.5
  1.0 0.4 shard_map.100
  1.4 23.1 %all_to_all.20.in_ref = f32[32,6,128]{2,1,0:T(8,128)S(1)} all-to-all(f32[32,6,128]{2,1,0:T(8,128)S(1)} %shard_map.100), channel_id=1, replica_groups=mesh['slot'=32,'limb'=4,'ct'=2] {'slot'}, dimensions={0} | all-to-all | bytes 196608 | tf_op jit(solution)/shard_map/all_to_all | solution.py:481
  24.5 0.9 copy-done.4
  25.5 0.8 shard_map.101
  26.4 15.1 %all_to_all.21 = f32[32,2,6,128]{3,1,2,0:T(2,128)S(1)} all-to-all(f32[32,2,6,128]{3,1,2,0:T(2,128)S(1)} %copy.13), channel_id=1, replica_groups=mesh['slot'=32,'limb'=4,'ct'=2] {'slot'}, dimensions={0} | all-to-all | bytes 393216 | tf_op jit(solution)/shard_map/all_to_all | solution.py:481
  41.6 0.5 shard_map.102
  42.1 1.4 collective-permute-start
  43.5 2.6 %collective-permute-start.1 = (f32[3,2,4096]{2,1,0:T(2,128)S(1)}, f32[3,2,4096]{2,1,0:T(2,128)S(1)}, u32[]{:S(2)}, u32[]{:S(2)}) collective-permute-start(f32[3,2,4096]{2,1,0:T(2,128)S(1)} %get-tuple-element.39), channel_id=1, source_target_pairs={{0,4},{2,6},{4,0},{6,2},{1,5},{3,7},{5,1},{7,3},{8,12},{10,14},{12... | collective-permute-start | bytes 294920 | tf_op jit(solution)/shard_map/ppermute | solution.py:540
  46.1 1.1 collective-permute-start.2
  47.2 0.2 shard_map.103
  47.5 3.2 %collective-permute-done.1.e1c_ref = f32[3,2,4096]{2,1,0:T(2,128)S(1)} collective-permute-done((f32[3,2,4096]{2,1,0:T(2,128)S(1)}, f32[3,2,4096]{2,1,0:T(2,128)S(1)}, u32[]{:S(2)}, u32[]{:S(2)}) %collective-permute-start.1) | collective-permute-done | bytes 98336 | tf_op jit(solution)/shard_map/ppermute | solution.py:540
  50.7 1.0 shard_map.104
  51.7 0.5 collective-permute-start.3
  52.2 2.1 %collective-permute-start.4 = (f32[7,2,2048]{2,1,0:T(2,128)S(1)}, f32[7,2,2048]{2,1,0:T(2,128)S(1)}, u32[]{:S(2)}, u32[]{:S(2)}) collective-permute-start(f32[7,2,2048]{2,1,0:T(2,128)S(1)} %get-tuple-element.43.spare0_ref), channel_id=1, source_target_pairs={{0,4},{2,6},{4,0},{6,2},{1,5},{3,7},{5,1},{7,3},{8,12},{10,14},{12... | collective-permute-start | bytes 344072 | tf_op jit(solution)/shard_map/ppermute | solution.py:540
  54.4 1.3 collective-permute-start.5
  55.7 1.2 collective-permute-start.10
  56.8 1.4 collective-permute-start.11
  58.3 1.0 copy.15.diag_ref
  59.4 1.1 shard_map.105
  60.5 5.5 %collective-permute-start.6 = (f32[6,2,2048]{2,1,0:T(2,128)S(1)}, f32[6,2,2048]{2,1,0:T(2,128)S(1)}, u32[]{:S(2)}, u32[]{:S(2)}) collective-permute-start(f32[6,2,2048]{2,1,0:T(2,128)S(1)} %get-tuple-element.44), channel_id=1, source_target_pairs={{0,8},{8,16},{16,24},{24,32},{32,40},{40,48},{48,56},{56,64},{64,7... | collective-permute-start | bytes 294920 | tf_op jit(solution)/shard_map/ppermute | solution.py:486
  66.0 2.2 %collective-permute-start.7 = (f32[6,2,2048]{2,1,0:T(2,128)S(1)}, f32[6,2,2048]{2,1,0:T(2,128)S(1)}, u32[]{:S(2)}, u32[]{:S(2)}) collective-permute-start(f32[6,2,2048]{2,1,0:T(2,128)S(1)} %get-tuple-element.45), channel_id=1, source_target_pairs={{0,16},{8,24},{16,32},{24,40},{32,48},{40,56},{48,64},{56,72},{64,... | collective-permute-start | bytes 294920 | tf_op jit(solution)/shard_map/ppermute | solution.py:486
  68.3 0.5 shard_map.106.evals_ref
  68.8 1.1 shard_map.107
  69.9 4.0 %collective-permute-done.7.got2_ref = f32[6,2,2048]{2,1,0:T(2,128)S(1)} collective-permute-done((f32[6,2,2048]{2,1,0:T(2,128)S(1)}, f32[6,2,2048]{2,1,0:T(2,128)S(1)}, u32[]{:S(2)}, u32[]{:S(2)}) %collective-permute-start.7) | collective-permute-done | bytes 98336 | tf_op jit(solution)/shard_map/ppermute | solution.py:486
  73.9 2.1 %collective-permute-done.8.got3_ref = f32[6,2,2048]{2,1,0:T(2,128)S(1)} collective-permute-done((f32[6,2,2048]{2,1,0:T(2,128)S(1)}, f32[6,2,2048]{2,1,0:T(2,128)S(1)}, u32[]{:S(2)}, u32[]{:S(2)}) %collective-permute-start.8) | collective-permute-done | bytes 98336 | tf_op jit(solution)/shard_map/ppermute | solution.py:486
  76.1 1.7 %collective-permute-start.12 = (f32[9,2,2048]{2,1,0:T(2,128)S(1)}, f32[9,2,2048]{2,1,0:T(2,128)S(1)}, u32[]{:S(2)}, u32[]{:S(2)}) collective-permute-start(f32[9,2,2048]{2,1,0:T(2,128)S(1)} %get-tuple-element.53.part0_ref), channel_id=1, source_target_pairs={{0,2},{2,4},{4,6},{6,0},{1,3},{3,5},{5,7},{7,1},{8,10},{10,12},{12... | collective-permute-start | bytes 442376 | tf_op jit(solution)/shard_map/ppermute | solution.py:540
  77.8 2.8 %collective-permute-start.13 = (f32[9,2,2048]{2,1,0:T(2,128)S(1)}, f32[9,2,2048]{2,1,0:T(2,128)S(1)}, u32[]{:S(2)}, u32[]{:S(2)}) collective-permute-start(f32[9,2,2048]{2,1,0:T(2,128)S(1)} %get-tuple-element.53.part0_ref), channel_id=1, source_target_pairs={{0,4},{2,6},{4,0},{6,2},{1,5},{3,7},{5,1},{7,3},{8,12},{10,14},{12... | collective-permute-start | bytes 442376 | tf_op jit(solution)/shard_map/ppermute | solution.py:540
  80.6 1.7 %collective-permute-done.12.part1_ref = f32[9,2,2048]{2,1,0:T(2,128)S(1)} collective-permute-done((f32[9,2,2048]{2,1,0:T(2,128)S(1)}, f32[9,2,2048]{2,1,0:T(2,128)S(1)}, u32[]{:S(2)}, u32[]{:S(2)}) %collective-permute-start.12) | collective-permute-done | bytes 147488 | tf_op jit(solution)/shard_map/ppermute | solution.py:540
  82.3 4.2 %collective-permute-done.13.part2_ref = f32[9,2,2048]{2,1,0:T(2,128)S(1)} collective-permute-done((f32[9,2,2048]{2,1,0:T(2,128)S(1)}, f32[9,2,2048]{2,1,0:T(2,128)S(1)}, u32[]{:S(2)}, u32[]{:S(2)}) %collective-permute-start.13) | collective-permute-done | bytes 147488 | tf_op jit(solution)/shard_map/ppermute | solution.py:540
  86.5 1.0 collective-permute-start.16
  87.5 2.4 %collective-permute-start.17 = (f32[24,2048]{1,0:T(8,128)S(1)}, f32[24,2048]{1,0:T(8,128)S(1)}, u32[]{:S(2)}, u32[]{:S(2)}) collective-permute-start(f32[24,2048]{1,0:T(8,128)S(1)} %collective-permute-done.15.part0_ref), channel_id=1, source_target_pairs={{0,4},{2,6},{4,0},{6,2},{1,5},{3,7},{5,1},{7,3},{8,12},{10,14},{12... | collective-permute-start | bytes 589832 | tf_op jit(solution)/shard_map/ppermute | solution.py:540
  89.9 0.3 collective-permute-start.18
  90.2 1.1 shard_map.109.refs_0_
  91.3 1.3 collective-permute-start.23
  92.6 2.6 %collective-permute-start.24 = (f32[6,2048]{1,0:T(8,128)S(1)}, f32[6,2048]{1,0:T(8,128)S(1)}, u32[]{:S(2)}, u32[]{:S(2)}) collective-permute-start(f32[6,2048]{1,0:T(8,128)S(1)} %get-tuple-element.69), channel_id=1, source_target_pairs={{0,16},{8,24},{16,32},{24,40},{32,48},{40,56},{48,64},{56,72},{64,... | collective-permute-start | bytes 147464 | tf_op jit(solution)/shard_map/ppermute | solution.py:486
  95.2 3.6 %collective-permute-done.17.part2_ref = f32[24,2048]{1,0:T(8,128)S(1)} collective-permute-done((f32[24,2048]{1,0:T(8,128)S(1)}, f32[24,2048]{1,0:T(8,128)S(1)}, u32[]{:S(2)}, u32[]{:S(2)}) %collective-permute-start.17) | collective-permute-done | bytes 196640 | tf_op jit(solution)/shard_map/ppermute | solution.py:540
  98.8 0.3 collective-permute-done.18.part3_ref
  99.2 0.9 shard_map.110
  100.1 1.3 collective-permute-start.20
  101.4 2.6 %collective-permute-start.21 = (f32[4,2048]{1,0:T(4,128)S(1)}, f32[4,2048]{1,0:T(4,128)S(1)}, u32[]{:S(2)}, u32[]{:S(2)}) collective-permute-start(f32[4,2048]{1,0:T(4,128)S(1)} %get-tuple-element.63.spare0_ref), channel_id=1, source_target_pairs={{0,4},{2,6},{4,0},{6,2},{1,5},{3,7},{5,1},{7,3},{8,12},{10,14},{12... | collective-permute-start | bytes 98312 | tf_op jit(solution)/shard_map/ppermute | solution.py:540
  104.1 1.6 %collective-permute-done.21.spare2_ref = f32[4,2048]{1,0:T(4,128)S(1)} collective-permute-done((f32[4,2048]{1,0:T(4,128)S(1)}, f32[4,2048]{1,0:T(4,128)S(1)}, u32[]{:S(2)}, u32[]{:S(2)}) %collective-permute-start.21) | collective-permute-done | bytes 32800 | tf_op jit(solution)/shard_map/ppermute | solution.py:540
  105.7 1.3 collective-permute-done.22.spare3_ref
  107.0 0.4 shard_map.112
  107.4 17.0 %all_to_all.22.in_ref = f32[32,6,128]{2,1,0:T(8,128)S(1)} all-to-all(f32[32,6,128]{2,1,0:T(8,128)S(1)} %shard_map.112), channel_id=1, replica_groups=mesh['slot'=32,'limb'=4,'ct'=2] {'slot'}, dimensions={0} | all-to-all | bytes 196608 | tf_op jit(solution)/shard_map/all_to_all | solution.py:481
  124.5 0.8 shard_map.113
  125.2 14.1 %all_to_all.23.in_ref = f32[32,6,128]{2,1,0:T(8,128)S(1)} all-to-all(f32[32,6,128]{2,1,0:T(8,128)S(1)} %shard_map.113), channel_id=1, replica_groups=mesh['slot'=32,'limb'=4,'ct'=2] {'slot'}, dimensions={0} | all-to-all | bytes 196608 | tf_op jit(solution)/shard_map/all_to_all | solution.py:481
  139.3 1.1 shard_map.114
  (44 shorter events, 0.8 us)
Async XLA Ops:
  0.0 41.6 %copy-start.2 = (bf16[2,256,256]{2,1,0:T(8,128)(2,1)S(1)}, bf16[2,256,256]{2,1,0:T(8,128)(2,1)}, u32[]{:S(2)}) copy-start(bf16[2,256,256]{2,1,0:T(8,128)(2,1)} %constant.13.clone.table_ref) | copy-start | bytes 786436
  0.0 50.7 %copy-start.1 = (bf16[7,3,2,8,2048]{4,3,2,1,0:T(8,128)(2,1)S(1)}, bf16[7,3,2,8,2048]{4,3,2,1,0:T(8,128)(2,1)}, u32[]{:S(2)}) copy-start(bf16[7,3,2,8,2048]{4,3,2,1,0:T(8,128)(2,1)} %keys_ref.3) | copy-start | bytes 4128772
  0.0 1.0 copy-start.5
  24.5 1.0 copy-start.4
  25.5 21.7 %copy-start.7 = (f32[8,24]{1,0:T(8,128)S(1)}, f32[8,24]{1,0:T(8,128)}, u32[]{:S(2)}) copy-start(f32[8,24]{1,0:T(8,128)} %up_ref) | copy-start | bytes 2308
  42.1 5.4 %collective-permute-start = (f32[3,2,4096]{2,1,0:T(2,128)S(1)}, f32[3,2,4096]{2,1,0:T(2,128)S(1)}, u32[]{:S(2)}, u32[]{:S(2)}) collective-permute-start(f32[3,2,4096]{2,1,0:T(2,128)S(1)} %get-tuple-element.39), channel_id=1, source_target_pairs={{0,2},{2,4},{4,6},{6,0},{1,3},{3,5},{5,7},{7,1},{8,10},{10,12},{12... | collective-permute-start | bytes 294920 | tf_op jit(solution)/shard_map/ppermute | solution.py:540
  43.5 7.2 %collective-permute-start.1 = (f32[3,2,4096]{2,1,0:T(2,128)S(1)}, f32[3,2,4096]{2,1,0:T(2,128)S(1)}, u32[]{:S(2)}, u32[]{:S(2)}) collective-permute-start(f32[3,2,4096]{2,1,0:T(2,128)S(1)} %get-tuple-element.39), channel_id=1, source_target_pairs={{0,4},{2,6},{4,0},{6,2},{1,5},{3,7},{5,1},{7,3},{8,12},{10,14},{12... | collective-permute-start | bytes 294920 | tf_op jit(solution)/shard_map/ppermute | solution.py:540
  46.1 4.6 %collective-permute-start.2 = (f32[3,2,4096]{2,1,0:T(2,128)S(1)}, f32[3,2,4096]{2,1,0:T(2,128)S(1)}, u32[]{:S(2)}, u32[]{:S(2)}) collective-permute-start(f32[3,2,4096]{2,1,0:T(2,128)S(1)} %get-tuple-element.39), channel_id=1, source_target_pairs={{0,6},{2,0},{4,2},{6,4},{1,7},{3,1},{5,3},{7,5},{8,14},{10,8},{12,... | collective-permute-start | bytes 294920 | tf_op jit(solution)/shard_map/ppermute | solution.py:540
  47.1 11.2 %copy-start.8 = (bf16[8,8,6,2048]{3,1,2,0:T(8,128)(2,1)S(1)}, bf16[8,8,6,2048]{3,1,2,0:T(8,128)(2,1)}, u32[]{:S(2)}) copy-start(bf16[8,8,6,2048]{3,1,2,0:T(8,128)(2,1)} %param.11) | copy-start | bytes 4718596
  51.7 6.5 %collective-permute-start.3 = (f32[7,2,2048]{2,1,0:T(2,128)S(1)}, f32[7,2,2048]{2,1,0:T(2,128)S(1)}, u32[]{:S(2)}, u32[]{:S(2)}) collective-permute-start(f32[7,2,2048]{2,1,0:T(2,128)S(1)} %get-tuple-element.43.spare0_ref), channel_id=1, source_target_pairs={{0,2},{2,4},{4,6},{6,0},{1,3},{3,5},{5,7},{7,1},{8,10},{10,12},{12... | collective-permute-start | bytes 344072 | tf_op jit(solution)/shard_map/ppermute | solution.py:540
  52.2 7.1 %collective-permute-start.4 = (f32[7,2,2048]{2,1,0:T(2,128)S(1)}, f32[7,2,2048]{2,1,0:T(2,128)S(1)}, u32[]{:S(2)}, u32[]{:S(2)}) collective-permute-start(f32[7,2,2048]{2,1,0:T(2,128)S(1)} %get-tuple-element.43.spare0_ref), channel_id=1, source_target_pairs={{0,4},{2,6},{4,0},{6,2},{1,5},{3,7},{5,1},{7,3},{8,12},{10,14},{12... | collective-permute-start | bytes 344072 | tf_op jit(solution)/shard_map/ppermute | solution.py:540
  54.4 5.0 %collective-permute-start.5 = (f32[7,2,2048]{2,1,0:T(2,128)S(1)}, f32[7,2,2048]{2,1,0:T(2,128)S(1)}, u32[]{:S(2)}, u32[]{:S(2)}) collective-permute-start(f32[7,2,2048]{2,1,0:T(2,128)S(1)} %get-tuple-element.43.spare0_ref), channel_id=1, source_target_pairs={{0,6},{2,0},{4,2},{6,4},{1,7},{3,1},{5,3},{7,5},{8,14},{10,8},{12,... | collective-permute-start | bytes 344072 | tf_op jit(solution)/shard_map/ppermute | solution.py:540
  55.7 3.7 %copy-start.6 = (f32[6,8]{1,0:T(8,128)S(1)}, f32[6,8]{1,0:T(8,128)}, u32[]{:S(2)}) copy-start(f32[6,8]{1,0:T(8,128)} %down_ref.5) | copy-start | bytes 580
  55.7 12.6 %collective-permute-start.10 = (f32[7,2,2048]{2,1,0:T(2,128)S(1)}, f32[7,2,2048]{2,1,0:T(2,128)S(1)}, u32[]{:S(2)}, u32[]{:S(2)}) collective-permute-start(f32[7,2,2048]{2,1,0:T(2,128)S(1)} %get-tuple-element.47.spare0_ref), channel_id=1, source_target_pairs={{0,4},{2,6},{4,0},{6,2},{1,5},{3,7},{5,1},{7,3},{8,12},{10,14},{12... | collective-permute-start | bytes 344072 | tf_op jit(solution)/shard_map/ppermute | solution.py:540
  56.8 11.9 %collective-permute-start.11 = (f32[7,2,2048]{2,1,0:T(2,128)S(1)}, f32[7,2,2048]{2,1,0:T(2,128)S(1)}, u32[]{:S(2)}, u32[]{:S(2)}) collective-permute-start(f32[7,2,2048]{2,1,0:T(2,128)S(1)} %get-tuple-element.47.spare0_ref), channel_id=1, source_target_pairs={{0,6},{2,0},{4,2},{6,4},{1,7},{3,1},{5,3},{7,5},{8,14},{10,8},{12,... | collective-permute-start | bytes 344072 | tf_op jit(solution)/shard_map/ppermute | solution.py:540
  58.2 10.5 %collective-permute-start.9 = (f32[7,2,2048]{2,1,0:T(2,128)S(1)}, f32[7,2,2048]{2,1,0:T(2,128)S(1)}, u32[]{:S(2)}, u32[]{:S(2)}) collective-permute-start(f32[7,2,2048]{2,1,0:T(2,128)S(1)} %get-tuple-element.47.spare0_ref), channel_id=1, source_target_pairs={{0,2},{2,4},{4,6},{6,0},{1,3},{3,5},{5,7},{7,1},{8,10},{10,12},{12... | collective-permute-start | bytes 344072 | tf_op jit(solution)/shard_map/ppermute | solution.py:540
  60.5 9.4 %collective-permute-start.6 = (f32[6,2,2048]{2,1,0:T(2,128)S(1)}, f32[6,2,2048]{2,1,0:T(2,128)S(1)}, u32[]{:S(2)}, u32[]{:S(2)}) collective-permute-start(f32[6,2,2048]{2,1,0:T(2,128)S(1)} %get-tuple-element.44), channel_id=1, source_target_pairs={{0,8},{8,16},{16,24},{24,32},{32,40},{40,48},{48,56},{56,64},{64,7... | collective-permute-start | bytes 294920 | tf_op jit(solution)/shard_map/ppermute | solution.py:486
  66.0 7.8 %collective-permute-start.7 = (f32[6,2,2048]{2,1,0:T(2,128)S(1)}, f32[6,2,2048]{2,1,0:T(2,128)S(1)}, u32[]{:S(2)}, u32[]{:S(2)}) collective-permute-start(f32[6,2,2048]{2,1,0:T(2,128)S(1)} %get-tuple-element.45), channel_id=1, source_target_pairs={{0,16},{8,24},{16,32},{24,40},{32,48},{40,56},{48,64},{56,72},{64,... | collective-permute-start | bytes 294920 | tf_op jit(solution)/shard_map/ppermute | solution.py:486
  68.2 7.7 %collective-permute-start.8 = (f32[6,2,2048]{2,1,0:T(2,128)S(1)}, f32[6,2,2048]{2,1,0:T(2,128)S(1)}, u32[]{:S(2)}, u32[]{:S(2)}) collective-permute-start(f32[6,2,2048]{2,1,0:T(2,128)S(1)} %get-tuple-element.46), channel_id=1, source_target_pairs={{0,24},{8,32},{16,40},{24,48},{32,56},{40,64},{48,72},{56,80},{64,... | collective-permute-start | bytes 294920 | tf_op jit(solution)/shard_map/ppermute | solution.py:486
  68.7 21.5 %copy-start = (bf16[7,3,2,8,2048]{4,3,2,1,0:T(8,128)(2,1)S(1)}, bf16[7,3,2,8,2048]{4,3,2,1,0:T(8,128)(2,1)}, u32[]{:S(2)}) copy-start(bf16[7,3,2,8,2048]{4,3,2,1,0:T(8,128)(2,1)} %keys_ref.5) | copy-start | bytes 4128772
  76.0 10.5 %collective-permute-start.15 = (f32[24,2048]{1,0:T(8,128)S(1)}, f32[24,2048]{1,0:T(8,128)S(1)}, u32[]{:S(2)}, u32[]{:S(2)}) collective-permute-start(f32[24,2048]{1,0:T(8,128)S(1)} %get-tuple-element.54), channel_id=1, source_target_pairs={{0,32},{8,40},{16,48},{24,56},{32,64},{40,72},{48,80},{56,88},{64,... | collective-permute-start | bytes 589832 | tf_op jit(solution)/shard_map/ppermute | solution.py:486
  76.1 6.2 %collective-permute-start.12 = (f32[9,2,2048]{2,1,0:T(2,128)S(1)}, f32[9,2,2048]{2,1,0:T(2,128)S(1)}, u32[]{:S(2)}, u32[]{:S(2)}) collective-permute-start(f32[9,2,2048]{2,1,0:T(2,128)S(1)} %get-tuple-element.53.part0_ref), channel_id=1, source_target_pairs={{0,2},{2,4},{4,6},{6,0},{1,3},{3,5},{5,7},{7,1},{8,10},{10,12},{12... | collective-permute-start | bytes 442376 | tf_op jit(solution)/shard_map/ppermute | solution.py:540
  77.8 8.7 %collective-permute-start.13 = (f32[9,2,2048]{2,1,0:T(2,128)S(1)}, f32[9,2,2048]{2,1,0:T(2,128)S(1)}, u32[]{:S(2)}, u32[]{:S(2)}) collective-permute-start(f32[9,2,2048]{2,1,0:T(2,128)S(1)} %get-tuple-element.53.part0_ref), channel_id=1, source_target_pairs={{0,4},{2,6},{4,0},{6,2},{1,5},{3,7},{5,1},{7,3},{8,12},{10,14},{12... | collective-permute-start | bytes 442376 | tf_op jit(solution)/shard_map/ppermute | solution.py:540
  80.6 5.9 %collective-permute-start.14 = (f32[9,2,2048]{2,1,0:T(2,128)S(1)}, f32[9,2,2048]{2,1,0:T(2,128)S(1)}, u32[]{:S(2)}, u32[]{:S(2)}) collective-permute-start(f32[9,2,2048]{2,1,0:T(2,128)S(1)} %get-tuple-element.53.part0_ref), channel_id=1, source_target_pairs={{0,6},{2,0},{4,2},{6,4},{1,7},{3,1},{5,3},{7,5},{8,14},{10,8},{12,... | collective-permute-start | bytes 442376 | tf_op jit(solution)/shard_map/ppermute | solution.py:540
  80.6 10.6 %collective-permute-start.19 = (f32[24,2048]{1,0:T(8,128)S(1)}, f32[24,2048]{1,0:T(8,128)S(1)}, u32[]{:S(2)}, u32[]{:S(2)}) collective-permute-start(f32[24,2048]{1,0:T(8,128)S(1)} %get-tuple-element.57), channel_id=1, source_target_pairs={{0,32},{8,40},{16,48},{24,56},{32,64},{40,72},{48,80},{56,88},{64,... | collective-permute-start | bytes 589832 | tf_op jit(solution)/shard_map/ppermute | solution.py:486
  86.5 8.7 %collective-permute-start.16 = (f32[24,2048]{1,0:T(8,128)S(1)}, f32[24,2048]{1,0:T(8,128)S(1)}, u32[]{:S(2)}, u32[]{:S(2)}) collective-permute-start(f32[24,2048]{1,0:T(8,128)S(1)} %collective-permute-done.15.part0_ref), channel_id=1, source_target_pairs={{0,2},{2,4},{4,6},{6,0},{1,3},{3,5},{5,7},{7,1},{8,10},{10,12},{12... | collective-permute-start | bytes 589832 | tf_op jit(solution)/shard_map/ppermute | solution.py:540
  87.5 11.3 %collective-permute-start.17 = (f32[24,2048]{1,0:T(8,128)S(1)}, f32[24,2048]{1,0:T(8,128)S(1)}, u32[]{:S(2)}, u32[]{:S(2)}) collective-permute-start(f32[24,2048]{1,0:T(8,128)S(1)} %collective-permute-done.15.part0_ref), channel_id=1, source_target_pairs={{0,4},{2,6},{4,0},{6,2},{1,5},{3,7},{5,1},{7,3},{8,12},{10,14},{12... | collective-permute-start | bytes 589832 | tf_op jit(solution)/shard_map/ppermute | solution.py:540
  89.9 9.3 %collective-permute-start.18 = (f32[24,2048]{1,0:T(8,128)S(1)}, f32[24,2048]{1,0:T(8,128)S(1)}, u32[]{:S(2)}, u32[]{:S(2)}) collective-permute-start(f32[24,2048]{1,0:T(8,128)S(1)} %collective-permute-done.15.part0_ref), channel_id=1, source_target_pairs={{0,6},{2,0},{4,2},{6,4},{1,7},{3,1},{5,3},{7,5},{8,14},{10,8},{12,... | collective-permute-start | bytes 589832 | tf_op jit(solution)/shard_map/ppermute | solution.py:540
  91.3 12.6 %collective-permute-start.23 = (f32[6,2048]{1,0:T(8,128)S(1)}, f32[6,2048]{1,0:T(8,128)S(1)}, u32[]{:S(2)}, u32[]{:S(2)}) collective-permute-start(f32[6,2048]{1,0:T(8,128)S(1)} %get-tuple-element.68), channel_id=1, source_target_pairs={{0,8},{8,16},{16,24},{24,32},{32,40},{40,48},{48,56},{56,64},{64,7... | collective-permute-start | bytes 147464 | tf_op jit(solution)/shard_map/ppermute | solution.py:486
  92.6 11.3 %collective-permute-start.24 = (f32[6,2048]{1,0:T(8,128)S(1)}, f32[6,2048]{1,0:T(8,128)S(1)}, u32[]{:S(2)}, u32[]{:S(2)}) collective-permute-start(f32[6,2048]{1,0:T(8,128)S(1)} %get-tuple-element.69), channel_id=1, source_target_pairs={{0,16},{8,24},{16,32},{24,40},{32,48},{40,56},{48,64},{56,72},{64,... | collective-permute-start | bytes 147464 | tf_op jit(solution)/shard_map/ppermute | solution.py:486
  95.2 29.2 %copy-start.3 = (bf16[2,256,256]{2,1,0:T(8,128)(2,1)S(1)}, bf16[2,256,256]{2,1,0:T(8,128)(2,1)}, u32[]{:S(2)}) copy-start(bf16[2,256,256]{2,1,0:T(8,128)(2,1)} %constant.14.clone.table_ref) | copy-start | bytes 786436
  95.2 8.7 %collective-permute-start.25 = (f32[6,2048]{1,0:T(8,128)S(1)}, f32[6,2048]{1,0:T(8,128)S(1)}, u32[]{:S(2)}, u32[]{:S(2)}) collective-permute-start(f32[6,2048]{1,0:T(8,128)S(1)} %get-tuple-element.70), channel_id=1, source_target_pairs={{0,24},{8,32},{16,40},{24,48},{32,56},{40,64},{48,72},{56,80},{64,... | collective-permute-start | bytes 147464 | tf_op jit(solution)/shard_map/ppermute | solution.py:486
  100.1 4.1 %collective-permute-start.20 = (f32[4,2048]{1,0:T(4,128)S(1)}, f32[4,2048]{1,0:T(4,128)S(1)}, u32[]{:S(2)}, u32[]{:S(2)}) collective-permute-start(f32[4,2048]{1,0:T(4,128)S(1)} %get-tuple-element.63.spare0_ref), channel_id=1, source_target_pairs={{0,2},{2,4},{4,6},{6,0},{1,3},{3,5},{5,7},{7,1},{8,10},{10,12},{12... | collective-permute-start | bytes 98312 | tf_op jit(solution)/shard_map/ppermute | solution.py:540
  101.4 4.3 %collective-permute-start.21 = (f32[4,2048]{1,0:T(4,128)S(1)}, f32[4,2048]{1,0:T(4,128)S(1)}, u32[]{:S(2)}, u32[]{:S(2)}) collective-permute-start(f32[4,2048]{1,0:T(4,128)S(1)} %get-tuple-element.63.spare0_ref), channel_id=1, source_target_pairs={{0,4},{2,6},{4,0},{6,2},{1,5},{3,7},{5,1},{7,3},{8,12},{10,14},{12... | collective-permute-start | bytes 98312 | tf_op jit(solution)/shard_map/ppermute | solution.py:540
  103.9 3.1 %collective-permute-start.22 = (f32[4,2048]{1,0:T(4,128)S(1)}, f32[4,2048]{1,0:T(4,128)S(1)}, u32[]{:S(2)}, u32[]{:S(2)}) collective-permute-start(f32[4,2048]{1,0:T(4,128)S(1)} %get-tuple-element.63.spare0_ref), channel_id=1, source_target_pairs={{0,6},{2,0},{4,2},{6,4},{1,7},{3,1},{5,3},{7,5},{8,14},{10,8},{12,... | collective-permute-start | bytes 98312 | tf_op jit(solution)/shard_map/ppermute | solution.py:540

commit v7 on v6

--- a/solution.py
+++ b/solution.py
@@ -359,8 +359,9 @@
 
 def pair_sum_kernel(low_ref, high_ref, *out_refs):
     for r, out_ref in enumerate(out_refs):
-        at = slice(6 * r, 6 * r + 6)
-        out_ref[...] = low_ref[at, :] + high_ref[at, :]
+        for i in range(3):
+            at = slice(6 * r + 2 * i, 6 * r + 2 * i + 2)
+            out_ref[i] = low_ref[at, :] + high_ref[at, :]
 
 
 def giants_kernel(
@@ -437,7 +438,7 @@
         value = total_ref[p, :, here]
         if p == 0:
             for rest in (rest0_ref, rest1_ref, rest2_ref, rest3_ref):
-                value = value + rest[:, here]
+                value = value + jnp.concatenate([rest[i, :, here] for i in range(3)], axis=0)
         else:
             value = value + zero_ref[:, here]
         return lowered(value, rows, columns)
@@ -570,7 +571,7 @@
     nears[1:], (far,) = together(nears[1:], [far])
     (before,) = giants_call(1, nears, giant_factors, giant_keys)
     (high,), (before,) = together([high], [before])
-    rests = call(pair_sum_kernel, [(Q_DEV, POINTS_DEV)] * 4, low, high, flops=10000)
+    rests = call(pair_sum_kernel, [(3, 2, POINTS_DEV)] * 4, low, high, flops=10000)
     rests = [rests[0]] + [shifted(rests[r], r) for r in range(1, 4)]
     total, spare = giants_call(4, gathered(far), giant_factors, giant_keys, before)
     return inverse(lower_call(place, total, gathered(spare), down, zero, rests))

time: 141 us -> 141 us (level)
  transfers between devices with their start and end apart: 26 -> 26, of which waited for: 11 -> 11; matrix products, arithmetic and copies ran while one was open for 1% -> 1% of each run, Pallas kernels for 3% -> 4%
where the time goes in v7:
time: 141 us; the launch traced here: 140 us
  blocking collectives  69.4 us (49%)
  starting transfers between devices  35.4 us (25%)
  waiting for transfers between devices  22.2 us (16%)
  Pallas kernels  10 us (7%)
  local copies, waits for them, and re-layouts  3.17 us (2%)
    all_to_all x4, blocking collectives, swap(): return lax.all_to_all(values, axis, split_axis=0, concat_axis=0, tiled=True)  69.4 us
    ppermute x18, starting transfers between devices, gathered(): lax.ppermute(block, 'limb', routes[m])  23.7 us
    ppermute x18, waiting for transfers between devices, gathered(): lax.ppermute(block, 'limb', routes[m])  16.1 us
    ppermute x8, starting transfers between devices, shifted(): return lax.ppermute(block, 'slot', route)  11.8 us
    ppermute x8, waiting for transfers between devices, shifted(): return lax.ppermute(block, 'slot', route)  6.07 us
    pallas_call x8, Pallas kernels, call(): pl.pallas_call(kernel, out_shape=shapes if len(shapes) > 1 else shapes[0]...  4.2 us
    unnamed x19, local copies, waits for them, and re-layouts  3.04 us
  transfers between devices with their start and end apart: 26, of which 11 were waited for; matrix products, arithmetic and copies ran while one was open for 1% of the time, Pallas kernels for 4%

profile of v7, /device:TPU:1, one launch (start us, length us, event | category | flops | bytes accessed | tf_op | source)
XLA Modules:
  0.0 140.5 jit_solution(13554470845759293138)
XLA Ops:
  0.0 1.0 copy-done.5
  1.0 0.4 shard_map.100
  1.4 23.1 %all_to_all.20.in_ref = f32[32,6,128]{2,1,0:T(8,128)S(1)} all-to-all(f32[32,6,128]{2,1,0:T(8,128)S(1)} %shard_map.100), channel_id=1, replica_groups=mesh['slot'=32,'limb'=4,'ct'=2] {'slot'}, dimensions={0} | all-to-all | bytes 196608 | tf_op jit(solution)/shard_map/all_to_all | solution.py:482
  24.5 0.9 copy-done.4
  25.5 0.8 shard_map.101
  26.4 15.1 %all_to_all.21 = f32[32,2,6,128]{3,1,2,0:T(2,128)S(1)} all-to-all(f32[32,2,6,128]{3,1,2,0:T(2,128)S(1)} %copy.13), channel_id=1, replica_groups=mesh['slot'=32,'limb'=4,'ct'=2] {'slot'}, dimensions={0} | all-to-all | bytes 393216 | tf_op jit(solution)/shard_map/all_to_all | solution.py:482
  41.6 0.5 shard_map.102
  42.1 1.4 collective-permute-start
  43.5 2.6 %collective-permute-start.1 = (f32[3,2,4096]{2,1,0:T(2,128)S(1)}, f32[3,2,4096]{2,1,0:T(2,128)S(1)}, u32[]{:S(2)}, u32[]{:S(2)}) collective-permute-start(f32[3,2,4096]{2,1,0:T(2,128)S(1)} %get-tuple-element.39), channel_id=1, source_target_pairs={{0,4},{2,6},{4,0},{6,2},{1,5},{3,7},{5,1},{7,3},{8,12},{10,14},{12... | collective-permute-start | bytes 294920 | tf_op jit(solution)/shard_map/ppermute | solution.py:541
  46.1 1.1 collective-permute-start.2
  47.2 0.2 shard_map.103
  47.5 3.2 %collective-permute-done.1.e1c_ref = f32[3,2,4096]{2,1,0:T(2,128)S(1)} collective-permute-done((f32[3,2,4096]{2,1,0:T(2,128)S(1)}, f32[3,2,4096]{2,1,0:T(2,128)S(1)}, u32[]{:S(2)}, u32[]{:S(2)}) %collective-permute-start.1) | collective-permute-done | bytes 98336 | tf_op jit(solution)/shard_map/ppermute | solution.py:541
  50.7 1.0 shard_map.104
  51.7 0.5 collective-permute-start.3
  52.2 2.1 %collective-permute-start.4 = (f32[7,2,2048]{2,1,0:T(2,128)S(1)}, f32[7,2,2048]{2,1,0:T(2,128)S(1)}, u32[]{:S(2)}, u32[]{:S(2)}) collective-permute-start(f32[7,2,2048]{2,1,0:T(2,128)S(1)} %get-tuple-element.43.spare0_ref), channel_id=1, source_target_pairs={{0,4},{2,6},{4,0},{6,2},{1,5},{3,7},{5,1},{7,3},{8,12},{10,14},{12... | collective-permute-start | bytes 344072 | tf_op jit(solution)/shard_map/ppermute | solution.py:541
  54.4 1.3 collective-permute-start.5
  55.7 1.2 collective-permute-start.10
  56.8 1.4 collective-permute-start.11
  58.3 1.0 copy.15.diag_ref
  59.4 1.1 shard_map.105
  60.5 5.5 %collective-permute-start.6 = (f32[6,2,2048]{2,1,0:T(2,128)S(1)}, f32[6,2,2048]{2,1,0:T(2,128)S(1)}, u32[]{:S(2)}, u32[]{:S(2)}) collective-permute-start(f32[6,2,2048]{2,1,0:T(2,128)S(1)} %get-tuple-element.44), channel_id=1, source_target_pairs={{0,8},{8,16},{16,24},{24,32},{32,40},{40,48},{48,56},{56,64},{64,7... | collective-permute-start | bytes 294920 | tf_op jit(solution)/shard_map/ppermute | solution.py:487
  66.0 2.2 %collective-permute-start.7 = (f32[6,2,2048]{2,1,0:T(2,128)S(1)}, f32[6,2,2048]{2,1,0:T(2,128)S(1)}, u32[]{:S(2)}, u32[]{:S(2)}) collective-permute-start(f32[6,2,2048]{2,1,0:T(2,128)S(1)} %get-tuple-element.45), channel_id=1, source_target_pairs={{0,16},{8,24},{16,32},{24,40},{32,48},{40,56},{48,64},{56,72},{64,... | collective-permute-start | bytes 294920 | tf_op jit(solution)/shard_map/ppermute | solution.py:487
  68.3 0.5 shard_map.106.evals_ref
  68.8 1.1 shard_map.107
  69.9 4.0 %collective-permute-done.7.got2_ref = f32[6,2,2048]{2,1,0:T(2,128)S(1)} collective-permute-done((f32[6,2,2048]{2,1,0:T(2,128)S(1)}, f32[6,2,2048]{2,1,0:T(2,128)S(1)}, u32[]{:S(2)}, u32[]{:S(2)}) %collective-permute-start.7) | collective-permute-done | bytes 98336 | tf_op jit(solution)/shard_map/ppermute | solution.py:487
  73.9 2.1 %collective-permute-done.8.got3_ref = f32[6,2,2048]{2,1,0:T(2,128)S(1)} collective-permute-done((f32[6,2,2048]{2,1,0:T(2,128)S(1)}, f32[6,2,2048]{2,1,0:T(2,128)S(1)}, u32[]{:S(2)}, u32[]{:S(2)}) %collective-permute-start.8) | collective-permute-done | bytes 98336 | tf_op jit(solution)/shard_map/ppermute | solution.py:487
  76.1 1.7 %collective-permute-start.12 = (f32[9,2,2048]{2,1,0:T(2,128)S(1)}, f32[9,2,2048]{2,1,0:T(2,128)S(1)}, u32[]{:S(2)}, u32[]{:S(2)}) collective-permute-start(f32[9,2,2048]{2,1,0:T(2,128)S(1)} %get-tuple-element.53.part0_ref), channel_id=1, source_target_pairs={{0,2},{2,4},{4,6},{6,0},{1,3},{3,5},{5,7},{7,1},{8,10},{10,12},{12... | collective-permute-start | bytes 442376 | tf_op jit(solution)/shard_map/ppermute | solution.py:541
  77.8 2.8 %collective-permute-start.13 = (f32[9,2,2048]{2,1,0:T(2,128)S(1)}, f32[9,2,2048]{2,1,0:T(2,128)S(1)}, u32[]{:S(2)}, u32[]{:S(2)}) collective-permute-start(f32[9,2,2048]{2,1,0:T(2,128)S(1)} %get-tuple-element.53.part0_ref), channel_id=1, source_target_pairs={{0,4},{2,6},{4,0},{6,2},{1,5},{3,7},{5,1},{7,3},{8,12},{10,14},{12... | collective-permute-start | bytes 442376 | tf_op jit(solution)/shard_map/ppermute | solution.py:541
  80.6 1.7 %collective-permute-done.12.part1_ref = f32[9,2,2048]{2,1,0:T(2,128)S(1)} collective-permute-done((f32[9,2,2048]{2,1,0:T(2,128)S(1)}, f32[9,2,2048]{2,1,0:T(2,128)S(1)}, u32[]{:S(2)}, u32[]{:S(2)}) %collective-permute-start.12) | collective-permute-done | bytes 147488 | tf_op jit(solution)/shard_map/ppermute | solution.py:541
  82.3 4.2 %collective-permute-done.13.part2_ref = f32[9,2,2048]{2,1,0:T(2,128)S(1)} collective-permute-done((f32[9,2,2048]{2,1,0:T(2,128)S(1)}, f32[9,2,2048]{2,1,0:T(2,128)S(1)}, u32[]{:S(2)}, u32[]{:S(2)}) %collective-permute-start.13) | collective-permute-done | bytes 147488 | tf_op jit(solution)/shard_map/ppermute | solution.py:541
  86.5 1.0 collective-permute-start.16
  87.5 2.4 %collective-permute-start.17 = (f32[24,2048]{1,0:T(8,128)S(1)}, f32[24,2048]{1,0:T(8,128)S(1)}, u32[]{:S(2)}, u32[]{:S(2)}) collective-permute-start(f32[24,2048]{1,0:T(8,128)S(1)} %collective-permute-done.15.part0_ref), channel_id=1, source_target_pairs={{0,4},{2,6},{4,0},{6,2},{1,5},{3,7},{5,1},{7,3},{8,12},{10,14},{12... | collective-permute-start | bytes 589832 | tf_op jit(solution)/shard_map/ppermute | solution.py:541
  89.9 0.3 collective-permute-start.18
  90.2 1.1 shard_map.109.refs_0_
  91.4 1.3 collective-permute-start.23
  92.6 2.6 %collective-permute-start.24 = (f32[3,2,2048]{2,1,0:T(2,128)S(1)}, f32[3,2,2048]{2,1,0:T(2,128)S(1)}, u32[]{:S(2)}, u32[]{:S(2)}) collective-permute-start(f32[3,2,2048]{2,1,0:T(2,128)S(1)} %get-tuple-element.69), channel_id=1, source_target_pairs={{0,16},{8,24},{16,32},{24,40},{32,48},{40,56},{48,64},{56,72},{64,... | collective-permute-start | bytes 147464 | tf_op jit(solution)/shard_map/ppermute | solution.py:487
  95.3 3.5 %collective-permute-done.17.part2_ref = f32[24,2048]{1,0:T(8,128)S(1)} collective-permute-done((f32[24,2048]{1,0:T(8,128)S(1)}, f32[24,2048]{1,0:T(8,128)S(1)}, u32[]{:S(2)}, u32[]{:S(2)}) %collective-permute-start.17) | collective-permute-done | bytes 196640 | tf_op jit(solution)/shard_map/ppermute | solution.py:541
  98.8 0.3 collective-permute-done.18.part3_ref
  99.2 0.9 shard_map.110
  100.1 1.3 collective-permute-start.20
  101.4 2.6 %collective-permute-start.21 = (f32[4,2048]{1,0:T(4,128)S(1)}, f32[4,2048]{1,0:T(4,128)S(1)}, u32[]{:S(2)}, u32[]{:S(2)}) collective-permute-start(f32[4,2048]{1,0:T(4,128)S(1)} %get-tuple-element.63.spare0_ref), channel_id=1, source_target_pairs={{0,4},{2,6},{4,0},{6,2},{1,5},{3,7},{5,1},{7,3},{8,12},{10,14},{12... | collective-permute-start | bytes 98312 | tf_op jit(solution)/shard_map/ppermute | solution.py:541
  104.1 1.6 %collective-permute-done.21.spare2_ref = f32[4,2048]{1,0:T(4,128)S(1)} collective-permute-done((f32[4,2048]{1,0:T(4,128)S(1)}, f32[4,2048]{1,0:T(4,128)S(1)}, u32[]{:S(2)}, u32[]{:S(2)}) %collective-permute-start.21) | collective-permute-done | bytes 32800 | tf_op jit(solution)/shard_map/ppermute | solution.py:541
  105.7 1.3 collective-permute-done.22.spare3_ref
  107.0 0.5 shard_map.112
  107.4 17.0 %all_to_all.22.in_ref = f32[32,6,128]{2,1,0:T(8,128)S(1)} all-to-all(f32[32,6,128]{2,1,0:T(8,128)S(1)} %shard_map.112), channel_id=1, replica_groups=mesh['slot'=32,'limb'=4,'ct'=2] {'slot'}, dimensions={0} | all-to-all | bytes 196608 | tf_op jit(solution)/shard_map/all_to_all | solution.py:482
  124.5 0.8 shard_map.113
  125.3 14.1 %all_to_all.23.in_ref = f32[32,6,128]{2,1,0:T(8,128)S(1)} all-to-all(f32[32,6,128]{2,1,0:T(8,128)S(1)} %shard_map.113), channel_id=1, replica_groups=mesh['slot'=32,'limb'=4,'ct'=2] {'slot'}, dimensions={0} | all-to-all | bytes 196608 | tf_op jit(solution)/shard_map/all_to_all | solution.py:482
  139.3 1.1 shard_map.114
  (44 shorter events, 0.9 us)
Async XLA Ops:
  0.0 41.6 %copy-start.2 = (bf16[2,256,256]{2,1,0:T(8,128)(2,1)S(1)}, bf16[2,256,256]{2,1,0:T(8,128)(2,1)}, u32[]{:S(2)}) copy-start(bf16[2,256,256]{2,1,0:T(8,128)(2,1)} %constant.13.clone.table_ref) | copy-start | bytes 786436
  0.0 50.7 %copy-start.1 = (bf16[7,3,2,8,2048]{4,3,2,1,0:T(8,128)(2,1)S(1)}, bf16[7,3,2,8,2048]{4,3,2,1,0:T(8,128)(2,1)}, u32[]{:S(2)}) copy-start(bf16[7,3,2,8,2048]{4,3,2,1,0:T(8,128)(2,1)} %keys_ref.3) | copy-start | bytes 4128772
  0.0 1.0 copy-start.5
  24.5 1.0 copy-start.4
  25.5 21.7 %copy-start.7 = (f32[8,24]{1,0:T(8,128)S(1)}, f32[8,24]{1,0:T(8,128)}, u32[]{:S(2)}) copy-start(f32[8,24]{1,0:T(8,128)} %up_ref) | copy-start | bytes 2308
  42.1 5.4 %collective-permute-start = (f32[3,2,4096]{2,1,0:T(2,128)S(1)}, f32[3,2,4096]{2,1,0:T(2,128)S(1)}, u32[]{:S(2)}, u32[]{:S(2)}) collective-permute-start(f32[3,2,4096]{2,1,0:T(2,128)S(1)} %get-tuple-element.39), channel_id=1, source_target_pairs={{0,2},{2,4},{4,6},{6,0},{1,3},{3,5},{5,7},{7,1},{8,10},{10,12},{12... | collective-permute-start | bytes 294920 | tf_op jit(solution)/shard_map/ppermute | solution.py:541
  43.5 7.2 %collective-permute-start.1 = (f32[3,2,4096]{2,1,0:T(2,128)S(1)}, f32[3,2,4096]{2,1,0:T(2,128)S(1)}, u32[]{:S(2)}, u32[]{:S(2)}) collective-permute-start(f32[3,2,4096]{2,1,0:T(2,128)S(1)} %get-tuple-element.39), channel_id=1, source_target_pairs={{0,4},{2,6},{4,0},{6,2},{1,5},{3,7},{5,1},{7,3},{8,12},{10,14},{12... | collective-permute-start | bytes 294920 | tf_op jit(solution)/shard_map/ppermute | solution.py:541
  46.1 4.6 %collective-permute-start.2 = (f32[3,2,4096]{2,1,0:T(2,128)S(1)}, f32[3,2,4096]{2,1,0:T(2,128)S(1)}, u32[]{:S(2)}, u32[]{:S(2)}) collective-permute-start(f32[3,2,4096]{2,1,0:T(2,128)S(1)} %get-tuple-element.39), channel_id=1, source_target_pairs={{0,6},{2,0},{4,2},{6,4},{1,7},{3,1},{5,3},{7,5},{8,14},{10,8},{12,... | collective-permute-start | bytes 294920 | tf_op jit(solution)/shard_map/ppermute | solution.py:541
  47.1 11.2 %copy-start.8 = (bf16[8,8,6,2048]{3,1,2,0:T(8,128)(2,1)S(1)}, bf16[8,8,6,2048]{3,1,2,0:T(8,128)(2,1)}, u32[]{:S(2)}) copy-start(bf16[8,8,6,2048]{3,1,2,0:T(8,128)(2,1)} %param.11) | copy-start | bytes 4718596
  51.7 6.5 %collective-permute-start.3 = (f32[7,2,2048]{2,1,0:T(2,128)S(1)}, f32[7,2,2048]{2,1,0:T(2,128)S(1)}, u32[]{:S(2)}, u32[]{:S(2)}) collective-permute-start(f32[7,2,2048]{2,1,0:T(2,128)S(1)} %get-tuple-element.43.spare0_ref), channel_id=1, source_target_pairs={{0,2},{2,4},{4,6},{6,0},{1,3},{3,5},{5,7},{7,1},{8,10},{10,12},{12... | collective-permute-start | bytes 344072 | tf_op jit(solution)/shard_map/ppermute | solution.py:541
  52.2 7.1 %collective-permute-start.4 = (f32[7,2,2048]{2,1,0:T(2,128)S(1)}, f32[7,2,2048]{2,1,0:T(2,128)S(1)}, u32[]{:S(2)}, u32[]{:S(2)}) collective-permute-start(f32[7,2,2048]{2,1,0:T(2,128)S(1)} %get-tuple-element.43.spare0_ref), channel_id=1, source_target_pairs={{0,4},{2,6},{4,0},{6,2},{1,5},{3,7},{5,1},{7,3},{8,12},{10,14},{12... | collective-permute-start | bytes 344072 | tf_op jit(solution)/shard_map/ppermute | solution.py:541
  54.4 5.0 %collective-permute-start.5 = (f32[7,2,2048]{2,1,0:T(2,128)S(1)}, f32[7,2,2048]{2,1,0:T(2,128)S(1)}, u32[]{:S(2)}, u32[]{:S(2)}) collective-permute-start(f32[7,2,2048]{2,1,0:T(2,128)S(1)} %get-tuple-element.43.spare0_ref), channel_id=1, source_target_pairs={{0,6},{2,0},{4,2},{6,4},{1,7},{3,1},{5,3},{7,5},{8,14},{10,8},{12,... | collective-permute-start | bytes 344072 | tf_op jit(solution)/shard_map/ppermute | solution.py:541
  55.7 3.7 %copy-start.6 = (f32[6,8]{1,0:T(8,128)S(1)}, f32[6,8]{1,0:T(8,128)}, u32[]{:S(2)}) copy-start(f32[6,8]{1,0:T(8,128)} %down_ref.5) | copy-start | bytes 580
  55.7 12.6 %collective-permute-start.10 = (f32[7,2,2048]{2,1,0:T(2,128)S(1)}, f32[7,2,2048]{2,1,0:T(2,128)S(1)}, u32[]{:S(2)}, u32[]{:S(2)}) collective-permute-start(f32[7,2,2048]{2,1,0:T(2,128)S(1)} %get-tuple-element.47.spare0_ref), channel_id=1, source_target_pairs={{0,4},{2,6},{4,0},{6,2},{1,5},{3,7},{5,1},{7,3},{8,12},{10,14},{12... | collective-permute-start | bytes 344072 | tf_op jit(solution)/shard_map/ppermute | solution.py:541
  56.8 11.9 %collective-permute-start.11 = (f32[7,2,2048]{2,1,0:T(2,128)S(1)}, f32[7,2,2048]{2,1,0:T(2,128)S(1)}, u32[]{:S(2)}, u32[]{:S(2)}) collective-permute-start(f32[7,2,2048]{2,1,0:T(2,128)S(1)} %get-tuple-element.47.spare0_ref), channel_id=1, source_target_pairs={{0,6},{2,0},{4,2},{6,4},{1,7},{3,1},{5,3},{7,5},{8,14},{10,8},{12,... | collective-permute-start | bytes 344072 | tf_op jit(solution)/shard_map/ppermute | solution.py:541
  58.2 10.5 %collective-permute-start.9 = (f32[7,2,2048]{2,1,0:T(2,128)S(1)}, f32[7,2,2048]{2,1,0:T(2,128)S(1)}, u32[]{:S(2)}, u32[]{:S(2)}) collective-permute-start(f32[7,2,2048]{2,1,0:T(2,128)S(1)} %get-tuple-element.47.spare0_ref), channel_id=1, source_target_pairs={{0,2},{2,4},{4,6},{6,0},{1,3},{3,5},{5,7},{7,1},{8,10},{10,12},{12... | collective-permute-start | bytes 344072 | tf_op jit(solution)/shard_map/ppermute | solution.py:541
  60.5 9.4 %collective-permute-start.6 = (f32[6,2,2048]{2,1,0:T(2,128)S(1)}, f32[6,2,2048]{2,1,0:T(2,128)S(1)}, u32[]{:S(2)}, u32[]{:S(2)}) collective-permute-start(f32[6,2,2048]{2,1,0:T(2,128)S(1)} %get-tuple-element.44), channel_id=1, source_target_pairs={{0,8},{8,16},{16,24},{24,32},{32,40},{40,48},{48,56},{56,64},{64,7... | collective-permute-start | bytes 294920 | tf_op jit(solution)/shard_map/ppermute | solution.py:487
  66.0 7.8 %collective-permute-start.7 = (f32[6,2,2048]{2,1,0:T(2,128)S(1)}, f32[6,2,2048]{2,1,0:T(2,128)S(1)}, u32[]{:S(2)}, u32[]{:S(2)}) collective-permute-start(f32[6,2,2048]{2,1,0:T(2,128)S(1)} %get-tuple-element.45), channel_id=1, source_target_pairs={{0,16},{8,24},{16,32},{24,40},{32,48},{40,56},{48,64},{56,72},{64,... | collective-permute-start | bytes 294920 | tf_op jit(solution)/shard_map/ppermute | solution.py:487
  68.2 7.7 %collective-permute-start.8 = (f32[6,2,2048]{2,1,0:T(2,128)S(1)}, f32[6,2,2048]{2,1,0:T(2,128)S(1)}, u32[]{:S(2)}, u32[]{:S(2)}) collective-permute-start(f32[6,2,2048]{2,1,0:T(2,128)S(1)} %get-tuple-element.46), channel_id=1, source_target_pairs={{0,24},{8,32},{16,40},{24,48},{32,56},{40,64},{48,72},{56,80},{64,... | collective-permute-start | bytes 294920 | tf_op jit(solution)/shard_map/ppermute | solution.py:487
  68.7 21.5 %copy-start = (bf16[7,3,2,8,2048]{4,3,2,1,0:T(8,128)(2,1)S(1)}, bf16[7,3,2,8,2048]{4,3,2,1,0:T(8,128)(2,1)}, u32[]{:S(2)}) copy-start(bf16[7,3,2,8,2048]{4,3,2,1,0:T(8,128)(2,1)} %keys_ref.5) | copy-start | bytes 4128772
  76.0 10.5 %collective-permute-start.15 = (f32[24,2048]{1,0:T(8,128)S(1)}, f32[24,2048]{1,0:T(8,128)S(1)}, u32[]{:S(2)}, u32[]{:S(2)}) collective-permute-start(f32[24,2048]{1,0:T(8,128)S(1)} %get-tuple-element.54), channel_id=1, source_target_pairs={{0,32},{8,40},{16,48},{24,56},{32,64},{40,72},{48,80},{56,88},{64,... | collective-permute-start | bytes 589832 | tf_op jit(solution)/shard_map/ppermute | solution.py:487
  76.1 6.2 %collective-permute-start.12 = (f32[9,2,2048]{2,1,0:T(2,128)S(1)}, f32[9,2,2048]{2,1,0:T(2,128)S(1)}, u32[]{:S(2)}, u32[]{:S(2)}) collective-permute-start(f32[9,2,2048]{2,1,0:T(2,128)S(1)} %get-tuple-element.53.part0_ref), channel_id=1, source_target_pairs={{0,2},{2,4},{4,6},{6,0},{1,3},{3,5},{5,7},{7,1},{8,10},{10,12},{12... | collective-permute-start | bytes 442376 | tf_op jit(solution)/shard_map/ppermute | solution.py:541
  77.8 8.7 %collective-permute-start.13 = (f32[9,2,2048]{2,1,0:T(2,128)S(1)}, f32[9,2,2048]{2,1,0:T(2,128)S(1)}, u32[]{:S(2)}, u32[]{:S(2)}) collective-permute-start(f32[9,2,2048]{2,1,0:T(2,128)S(1)} %get-tuple-element.53.part0_ref), channel_id=1, source_target_pairs={{0,4},{2,6},{4,0},{6,2},{1,5},{3,7},{5,1},{7,3},{8,12},{10,14},{12... | collective-permute-start | bytes 442376 | tf_op jit(solution)/shard_map/ppermute | solution.py:541
  80.6 5.9 %collective-permute-start.14 = (f32[9,2,2048]{2,1,0:T(2,128)S(1)}, f32[9,2,2048]{2,1,0:T(2,128)S(1)}, u32[]{:S(2)}, u32[]{:S(2)}) collective-permute-start(f32[9,2,2048]{2,1,0:T(2,128)S(1)} %get-tuple-element.53.part0_ref), channel_id=1, source_target_pairs={{0,6},{2,0},{4,2},{6,4},{1,7},{3,1},{5,3},{7,5},{8,14},{10,8},{12,... | collective-permute-start | bytes 442376 | tf_op jit(solution)/shard_map/ppermute | solution.py:541
  80.6 10.6 %collective-permute-start.19 = (f32[24,2048]{1,0:T(8,128)S(1)}, f32[24,2048]{1,0:T(8,128)S(1)}, u32[]{:S(2)}, u32[]{:S(2)}) collective-permute-start(f32[24,2048]{1,0:T(8,128)S(1)} %get-tuple-element.57), channel_id=1, source_target_pairs={{0,32},{8,40},{16,48},{24,56},{32,64},{40,72},{48,80},{56,88},{64,... | collective-permute-start | bytes 589832 | tf_op jit(solution)/shard_map/ppermute | solution.py:487
  86.5 8.8 %collective-permute-start.16 = (f32[24,2048]{1,0:T(8,128)S(1)}, f32[24,2048]{1,0:T(8,128)S(1)}, u32[]{:S(2)}, u32[]{:S(2)}) collective-permute-start(f32[24,2048]{1,0:T(8,128)S(1)} %collective-permute-done.15.part0_ref), channel_id=1, source_target_pairs={{0,2},{2,4},{4,6},{6,0},{1,3},{3,5},{5,7},{7,1},{8,10},{10,12},{12... | collective-permute-start | bytes 589832 | tf_op jit(solution)/shard_map/ppermute | solution.py:541
  87.5 11.3 %collective-permute-start.17 = (f32[24,2048]{1,0:T(8,128)S(1)}, f32[24,2048]{1,0:T(8,128)S(1)}, u32[]{:S(2)}, u32[]{:S(2)}) collective-permute-start(f32[24,2048]{1,0:T(8,128)S(1)} %collective-permute-done.15.part0_ref), channel_id=1, source_target_pairs={{0,4},{2,6},{4,0},{6,2},{1,5},{3,7},{5,1},{7,3},{8,12},{10,14},{12... | collective-permute-start | bytes 589832 | tf_op jit(solution)/shard_map/ppermute | solution.py:541
  89.9 9.3 %collective-permute-start.18 = (f32[24,2048]{1,0:T(8,128)S(1)}, f32[24,2048]{1,0:T(8,128)S(1)}, u32[]{:S(2)}, u32[]{:S(2)}) collective-permute-start(f32[24,2048]{1,0:T(8,128)S(1)} %collective-permute-done.15.part0_ref), channel_id=1, source_target_pairs={{0,6},{2,0},{4,2},{6,4},{1,7},{3,1},{5,3},{7,5},{8,14},{10,8},{12,... | collective-permute-start | bytes 589832 | tf_op jit(solution)/shard_map/ppermute | solution.py:541
  91.4 12.6 %collective-permute-start.23 = (f32[3,2,2048]{2,1,0:T(2,128)S(1)}, f32[3,2,2048]{2,1,0:T(2,128)S(1)}, u32[]{:S(2)}, u32[]{:S(2)}) collective-permute-start(f32[3,2,2048]{2,1,0:T(2,128)S(1)} %get-tuple-element.68), channel_id=1, source_target_pairs={{0,8},{8,16},{16,24},{24,32},{32,40},{40,48},{48,56},{56,64},{64,7... | collective-permute-start | bytes 147464 | tf_op jit(solution)/shard_map/ppermute | solution.py:487
  92.6 11.3 %collective-permute-start.24 = (f32[3,2,2048]{2,1,0:T(2,128)S(1)}, f32[3,2,2048]{2,1,0:T(2,128)S(1)}, u32[]{:S(2)}, u32[]{:S(2)}) collective-permute-start(f32[3,2,2048]{2,1,0:T(2,128)S(1)} %get-tuple-element.69), channel_id=1, source_target_pairs={{0,16},{8,24},{16,32},{24,40},{32,48},{40,56},{48,64},{56,72},{64,... | collective-permute-start | bytes 147464 | tf_op jit(solution)/shard_map/ppermute | solution.py:487
  95.3 29.2 %copy-start.3 = (bf16[2,256,256]{2,1,0:T(8,128)(2,1)S(1)}, bf16[2,256,256]{2,1,0:T(8,128)(2,1)}, u32[]{:S(2)}) copy-start(bf16[2,256,256]{2,1,0:T(8,128)(2,1)} %constant.14.clone.table_ref) | copy-start | bytes 786436
  95.3 8.7 %collective-permute-start.25 = (f32[3,2,2048]{2,1,0:T(2,128)S(1)}, f32[3,2,2048]{2,1,0:T(2,128)S(1)}, u32[]{:S(2)}, u32[]{:S(2)}) collective-permute-start(f32[3,2,2048]{2,1,0:T(2,128)S(1)} %get-tuple-element.70), channel_id=1, source_target_pairs={{0,24},{8,32},{16,40},{24,48},{32,56},{40,64},{48,72},{56,80},{64,... | collective-permute-start | bytes 147464 | tf_op jit(solution)/shard_map/ppermute | solution.py:487
  100.1 4.1 %collective-permute-start.20 = (f32[4,2048]{1,0:T(4,128)S(1)}, f32[4,2048]{1,0:T(4,128)S(1)}, u32[]{:S(2)}, u32[]{:S(2)}) collective-permute-start(f32[4,2048]{1,0:T(4,128)S(1)} %get-tuple-element.63.spare0_ref), channel_id=1, source_target_pairs={{0,2},{2,4},{4,6},{6,0},{1,3},{3,5},{5,7},{7,1},{8,10},{10,12},{12... | collective-permute-start | bytes 98312 | tf_op jit(solution)/shard_map/ppermute | solution.py:541
  101.4 4.3 %collective-permute-start.21 = (f32[4,2048]{1,0:T(4,128)S(1)}, f32[4,2048]{1,0:T(4,128)S(1)}, u32[]{:S(2)}, u32[]{:S(2)}) collective-permute-start(f32[4,2048]{1,0:T(4,128)S(1)} %get-tuple-element.63.spare0_ref), channel_id=1, source_target_pairs={{0,4},{2,6},{4,0},{6,2},{1,5},{3,7},{5,1},{7,3},{8,12},{10,14},{12... | collective-permute-start | bytes 98312 | tf_op jit(solution)/shard_map/ppermute | solution.py:541
  103.9 3.1 %collective-permute-start.22 = (f32[4,2048]{1,0:T(4,128)S(1)}, f32[4,2048]{1,0:T(4,128)S(1)}, u32[]{:S(2)}, u32[]{:S(2)}) collective-permute-start(f32[4,2048]{1,0:T(4,128)S(1)} %get-tuple-element.63.spare0_ref), channel_id=1, source_target_pairs={{0,6},{2,0},{4,2},{6,4},{1,7},{3,1},{5,3},{7,5},{8,14},{10,8},{12,... | collective-permute-start | bytes 98312 | tf_op jit(solution)/shard_map/ppermute | solution.py:541
